TPU v7x, 512 devices: a whole 4x4x16 slice. The times are simulated.
512 devices in a mesh: seq: 64 (over z_lo, y, core), head: 8 (over x, z_hi).
Axes of the slice: x: 4, y: 4, z: 16 (z_hi: 2, z_lo: 8; z = z_hi * 8 + z_lo), core: 2. Of those that a mesh axis runs over, the one named last changes fastest.
Arguments:
- query: bfloat16 [16384, 8192], P('seq', 'head'), may hold values from -6 to 6
- key_in: bfloat16 [16384, 1024], P('seq', 'head'), may hold values from -6 to 6
- value_input: bfloat16 [16384, 1024], P('seq', 'head'), may hold values from -6 to 6
- output_gradient: bfloat16 [16384, 8192], P('seq', 'head'), may hold values from -6 to 6
- block_order: int32 [64], replicated, may hold values from 0 to 63, each once
Outputs:
- attn_out: bfloat16 [16384, 8192], P('seq', 'head')
- d_query: bfloat16 [16384, 8192], P('seq', 'head')
- d_keyvalue: bfloat16 [2, 16384, 1024], P(None, 'seq', 'head')
- gram: float32 [8, 1024, 1024], P('head', 'seq')
Inputs may be any that keep to these rules, and one draw needn't show every extreme that they name: `block_order`: each sequence block number appears once.
All inputs are finite; a program needn't handle non-finite values.
Results may differ from a plain program's by a relative error of at most 0.025.
Values may be sent and summed in bfloat16 or wider, within the bound.
No kernel may reach another device: no remote copies, remote signals or barrier semaphores. Data moves between devices by JAX's collectives and lax.ppermute only.
A program may use at most 64 MiB of HBM per device.

v0:
```python
import jax
import jax.numpy as jnp
from jax import lax
from jax.sharding import PartitionSpec as P


def passed_along(block, axis, distance):
    devices = range(lax.axis_size(axis))
    route = [((i - distance) % len(devices), i) for i in devices]
    return lax.ppermute(block, axis, route)


def local(query, key_in, value_input, output_gradient, block_order):
    tok_rows = query.shape[0]
    head_dim = key_in.shape[1]
    groups = query.shape[1] // head_dim
    width = query.shape[1]
    n_blocks = lax.axis_size("seq")
    my_index = lax.axis_index("seq")
    scale = 1.0 / head_dim**0.5
    offsets = jnp.arange(tok_rows, dtype=jnp.int32)
    key_value = jnp.stack([key_in, value_input])
    blocks = [key_value]
    current = key_value
    for step in range(2):
        current = passed_along(current, "seq", 1)
        blocks.append(current)
    all_keys = jnp.concatenate([block[0] for block in blocks], 0)
    all_values = jnp.concatenate([block[1] for block in blocks], 0)
    pos_list = []
    for step in range(3):
        source = (my_index - step) % n_blocks
        pos_list.append(block_order[source] * tok_rows + offsets)
    k_pos = jnp.concatenate(pos_list, 0)
    q_pos = block_order[my_index] * tok_rows + offsets
    q_heads = query.reshape(tok_rows, groups, head_dim)
    go_heads = output_gradient.reshape(tok_rows, groups, head_dim)
    scores = (
        jnp.einsum("tgd,sd->gts", q_heads, all_keys, preferred_element_type=jnp.float32) * scale
    )
    visible = k_pos[None, None, :] <= q_pos[None, :, None]
    scores = jnp.where(visible, scores, -1e30)
    top = jnp.max(scores, axis=-1, keepdims=True)
    expo = jnp.exp(scores - top)
    weights = expo / jnp.sum(expo, axis=-1, keepdims=True)
    weights_bf = weights.astype(jnp.bfloat16)
    output = jnp.einsum("gts,sd->tgd", weights_bf, all_values, preferred_element_type=jnp.float32)
    out_bf = output.astype(jnp.bfloat16)
    row_dot = jnp.sum(go_heads.astype(jnp.float32) * out_bf.astype(jnp.float32), axis=-1)
    dprob = jnp.einsum("tgd,sd->gts", go_heads, all_values, preferred_element_type=jnp.float32)
    dscore = (weights * (dprob - jnp.transpose(row_dot)[:, :, None]) * scale).astype(jnp.bfloat16)
    d_query = jnp.einsum(
        "gts,sd->tgd", dscore, all_keys, preferred_element_type=jnp.float32
    ).astype(jnp.bfloat16)
    d_keys = jnp.einsum("gts,tgd->sd", dscore, q_heads, preferred_element_type=jnp.float32)
    d_values = jnp.einsum("gts,tgd->sd", weights_bf, go_heads, preferred_element_type=jnp.float32)
    partials = jnp.stack([d_keys, d_values]).reshape(2, 3, tok_rows, head_dim)
    carried = partials[:, 2]
    for step in (1, 0):
        carried = passed_along(carried, "seq", -1) + partials[:, step]
    out_rows = out_bf.reshape(tok_rows, width)
    owned = lax.psum_scatter(
        lax.dot_general(
            out_rows, out_rows, (((0,), (0,)), ((), ())), preferred_element_type=jnp.float32
        ),
        "seq",
        scatter_dimension=0,
        tiled=True,
    )
    gram = (owned / (tok_rows * n_blocks) ** 0.5)[None]
    return (out_rows, d_query.reshape(tok_rows, width), carried.astype(jnp.bfloat16), gram)


def solution(mesh):
    in_specs = (P("seq", "head"), P("seq", "head"), P("seq", "head"), P("seq", "head"), P())
    out_specs = (P("seq", "head"), P("seq", "head"), P(None, "seq", "head"), P("head", "seq", None))
    return jax.shard_map(local, mesh=mesh, in_specs=in_specs, out_specs=out_specs, check_vma=False)
```

profile of v0, /device:TPU:6, one launch (start us, length us, event | category | flops | bytes accessed | tf_op | source)
XLA Modules:
  0.0 499.7 jit_solution(163145210650516551)
XLA Ops:
  7.2 0.0 reduce-scatter.2.cloned.1.call-start
  7.2 0.9 pad_maximum_fusion.1
  8.1 1.9 collective-permute-start
  10.1 1.4 fusion.47
  14.1 1.2 copy.12
  15.4 0.2 broadcast_compare_fusion.1
  15.6 10.2 %collective-permute-done = bf16[2,256,128]{2,1,0:T(8,128)(2,1)S(1)} collective-permute-done((bf16[2,256,128]{2,1,0:T(8,128)(2,1)S(1)}, bf16[2,256,128]{2,1,0:T(8,128)(2,1)S(1)}, u32[]{:S(2)}, u32[]{:S(2)}) %collective-permute-start) | collective-permute-done | bytes 131104 | tf_op jit(solution)/shard_map/ppermute | solution.py:10
  25.8 1.9 collective-permute-start.1
  27.7 13.1 %collective-permute-done.1 = bf16[2,256,128]{2,1,0:T(8,128)(2,1)S(1)} collective-permute-done((bf16[2,256,128]{2,1,0:T(8,128)(2,1)S(1)}, bf16[2,256,128]{2,1,0:T(8,128)(2,1)S(1)}, u32[]{:S(2)}, u32[]{:S(2)}) %collective-permute-start.1) | collective-permute-done | bytes 131104 | tf_op jit(solution)/shard_map/ppermute | solution.py:10
  40.8 0.0 copy-start.2
  40.8 2.2 fusion.8
  43.0 0.0 copy-start
  43.0 1.3 fusion.10
  44.4 0.0 copy-done.2
  44.4 1.9 multiply_reduce_fusion
  46.3 0.0 copy-done
  46.3 0.0 copy-start.1
  46.3 2.8 fusion.48
  49.1 0.0 reduce-scatter.2.cloned.1.call-update
  49.1 0.0 copy-done.1
  49.1 0.1 copy.42
  49.2 0.2 broadcast_compare_fusion
  49.4 0.0 slice-start
  49.4 0.0 slice-start.1
  49.4 5.8 %fusion.23 = (bf16[768,8,256]{2,0,1:T(8,128)(2,1)S(1)}, bf16[768,8,256]{2,0,1:T(8,128)(2,1)S(1)}, f32[768,256,8]{1,0,2:T(8,128)S(1)}) fusion(f32[8,256]{1,0:T(8,128)S(1)} %fusion.10, f32[8,256]{1,0:T(8,128)S(1)} %get-tuple-element.18, f32[768,256,8]{1,0,2:T(8,128)} %copy-done, pred[768,256]{1,0:T(8,128)(4,1)S(1)} %broadcast_compare_fusion, ...), kind=kOutput, calls=%fused_computation.26 | convolution fusion | flops 417398784 | bytes 19816448 | tf_op jit(solution)/shard_map/tgd,sd->gts/dot_general | solution.py:50
  55.3 0.0 copy-start.3
  55.3 1.0 convolution_bitcast_fusion
  56.3 1.0 convolution_bitcast_fusion.1
  57.3 1.9 collective-permute-start.2
  59.2 3.9 collective-permute-done.2
  63.1 12.5 %collective-permute-start.3 = (f32[2,256,128]{2,1,0:T(8,128)S(1)}, f32[2,256,128]{2,1,0:T(8,128)S(1)}, u32[]{:S(2)}, u32[]{:S(2)}) collective-permute-start(f32[2,256,128]{2,1,0:T(8,128)S(1)} %fusion.32), channel_id=1, source_target_pairs={{8,0},{16,8},{24,16},{32,24},{40,32},{48,40},{56,48},{64,56},{72,6... | collective-permute-start | bytes 786440 | tf_op jit(solution)/shard_map/ppermute | solution.py:10
  75.6 0.0 slice-done
  75.6 0.0 slice-done.1
  75.6 0.0 copy-done.3
  75.7 2.6 fusion.20
  78.2 1.0 copy.22
  79.2 1.0 copy.23
  80.2 0.0 collective-permute-done.3
  80.2 0.7 fusion.37
  80.9 410.5 %reduce-scatter.2.cloned.1.call-done = f32[16,1024]{1,0:T(8,128)} async-done(((f32[1024,1024]{1,0:T(8,128)}), f32[16,1024]{1,0:T(8,128)}) %reduce-scatter.2.cloned.1.call-update) | async-done | bytes 65552 | tf_op jit(solution)/shard_map/reduce_scatter | solution.py:62
  491.4 1.5 multiply_bitcast_fusion
  (9 shorter events, 0.1 us)
Async XLA Ops:
  7.2 484.2 %reduce-scatter.2.cloned.1.call-start = ((), (), s32[]{:S(2)}) async-start(), calls=%async_computation.1 | async-start | bytes 4259840 | tf_op jit(solution)/shard_map/reduce_scatter | solution.py:62
  8.1 17.7 %collective-permute-start = (bf16[2,256,128]{2,1,0:T(8,128)(2,1)S(1)}, bf16[2,256,128]{2,1,0:T(8,128)(2,1)S(1)}, u32[]{:S(2)}, u32[]{:S(2)}) collective-permute-start(bf16[2,256,128]{2,1,0:T(8,128)(2,1)S(1)} %pad_maximum_fusion.1), channel_id=1, source_target_pairs={{504,0},{0,8},{8,16},{16,24},{24,32},{32,40},{40,48},{48,56},{56,6... | collective-permute-start | bytes 393224 | tf_op jit(solution)/shard_map/ppermute | solution.py:10
  25.8 15.0 %collective-permute-start.1 = (bf16[2,256,128]{2,1,0:T(8,128)(2,1)S(1)}, bf16[2,256,128]{2,1,0:T(8,128)(2,1)S(1)}, u32[]{:S(2)}, u32[]{:S(2)}) collective-permute-start(bf16[2,256,128]{2,1,0:T(8,128)(2,1)S(1)} %collective-permute-done), channel_id=1, source_target_pairs={{504,0},{0,8},{8,16},{16,24},{24,32},{32,40},{40,48},{48,56},{56,6... | collective-permute-start | bytes 393224 | tf_op jit(solution)/shard_map/ppermute | solution.py:10
  40.8 3.6 copy-start.2
  43.0 3.3 copy-start
  46.3 2.8 copy-start.1
  49.4 26.2 %slice-start = ((s8[6291456]{0:T(1024)(128)(4,1)}), s8[4194304]{0:T(1024)(128)(4,1)S(1)}, s32[]{:S(2)}) async-start(s8[6291456]{0:T(1024)(128)(4,1)} %bitcast.136), calls=%async_computation.2 | async-start | bytes 8388608
  49.4 26.2 %slice-start.1 = ((s8[6291456]{0:T(1024)(128)(4,1)}), s8[2097152]{0:T(1024)(128)(4,1)S(1)}, s32[]{:S(2)}) async-start(s8[6291456]{0:T(1024)(128)(4,1)} %bitcast.136), calls=%async_computation.3 | async-start | bytes 4194304
  55.3 20.4 %copy-start.3 = (bf16[256,128]{1,0:T(8,128)(2,1)S(1)}, bf16[256,128]{1,0:T(8,128)(2,1)}, u32[]{:S(2)}) copy-start(bf16[256,128]{1,0:T(8,128)(2,1)} %param.6) | copy-start | bytes 196612
  57.3 5.8 %collective-permute-start.2 = (f32[2,256,128]{2,1,0:T(8,128)S(1)}, f32[2,256,128]{2,1,0:T(8,128)S(1)}, u32[]{:S(2)}, u32[]{:S(2)}) collective-permute-start(f32[2,256,128]{2,1,0:T(8,128)S(1)} %fusion.34), channel_id=1, source_target_pairs={{8,0},{16,8},{24,16},{32,24},{40,32},{48,40},{56,48},{64,56},{72,6... | collective-permute-start | bytes 786440 | tf_op jit(solution)/shard_map/ppermute | solution.py:10
  63.1 17.1 %collective-permute-start.3 = (f32[2,256,128]{2,1,0:T(8,128)S(1)}, f32[2,256,128]{2,1,0:T(8,128)S(1)}, u32[]{:S(2)}, u32[]{:S(2)}) collective-permute-start(f32[2,256,128]{2,1,0:T(8,128)S(1)} %fusion.32), channel_id=1, source_target_pairs={{8,0},{16,8},{24,16},{32,24},{40,32},{48,40},{56,48},{64,56},{72,6... | collective-permute-start | bytes 786440 | tf_op jit(solution)/shard_map/ppermute | solution.py:10
Sparse Core Ops, SparseCore 0:
  49.2 442.1 reduce-scatter.1
where the time goes:
time: 500 us
  waiting for transfers between devices  438 us (88%)
  starting transfers between devices  18.3 us (4%)
  matrix products  17.2 us (3%)
  between operations  16.9 us (3%)
    reduce_scatter x1, waiting for transfers between devices, local(): lax.psum_scatter(lax.dot_general(out_rows, out_rows, (((0,), (0,)), ((),...  410 us
    ppermute x4, waiting for transfers between devices, passed_along(): return lax.ppermute(block, axis, route)  27.1 us
    ppermute x4, starting transfers between devices, passed_along(): return lax.ppermute(block, axis, route)  18.3 us
  transfers between devices with their start and end apart: 5, of which 4 were waited for; matrix products, arithmetic and copies ran while one was open for 3% of the time, Pallas kernels for 0%

commit v1 on v0

v1 whole, which is shorter than its diff:
```python
import math

import jax
import jax.numpy as jnp
from jax import lax
from jax.experimental import pallas as pl
from jax.experimental.pallas import tpu as pltpu
from jax.sharding import PartitionSpec as P

NT = (((1,), (1,)), ((), ()))
NN = (((1,), (0,)), ((), ()))
LOWEST = -1e30
VMEM_LIMIT = 48 * 1024 * 1024


def dot(a, b, dims):
    return lax.dot_general(a, b, dims, preferred_element_type=jnp.float32)


def visibility(place_ref, order_ref):
    me = place_ref[0]
    count = order_ref.shape[0]
    mine = order_ref[me]
    out = []
    for step in (1, 2):
        theirs = order_ref[lax.rem(me + count - step, count)]
        out.append(jnp.where(theirs <= mine, 0.0, -LOWEST).astype(jnp.float32))
    return out


def forward_kernel(place_ref, order_ref, q_ref, k0_ref, v0_ref, kv1_ref, kv2_ref, out_ref, out_t_ref, lse_ref):
    tok, dim = k0_ref.shape
    heads = q_ref.shape[1] // dim
    unit = math.log2(math.e) / dim**0.5
    hide = [None] + visibility(place_ref, order_ref)
    keys = [k0_ref[...], kv1_ref[:tok, :], kv2_ref[:tok, :]]
    values_t = [v0_ref[...].T, kv1_ref[tok:, :].T, kv2_ref[tok:, :].T]
    causal = lax.broadcasted_iota(jnp.int32, (tok, tok), 0) <= lax.broadcasted_iota(jnp.int32, (tok, tok), 1)
    for h in range(heads):
        cols = slice(h * dim, (h + 1) * dim)
        qh = q_ref[:, cols]
        scores = [dot(key, qh, NT) for key in keys]
        scores[0] = jnp.where(causal, scores[0], LOWEST)
        top = jnp.max(scores[0], axis=0, keepdims=True) * unit
        for j in (1, 2):
            top = jnp.maximum(top, jnp.max(scores[j], axis=0, keepdims=True) * unit - hide[j])
        total = None
        mixed = None
        for j in range(3):
            base = top if j == 0 else top + hide[j]
            expo = jnp.exp2(scores[j] * unit - base)
            part = jnp.sum(expo, axis=0, keepdims=True)
            total = part if total is None else total + part
            piece = dot(values_t[j], expo.astype(jnp.bfloat16), NN)
            mixed = piece if mixed is None else mixed + piece
        mixed = mixed * (1.0 / total)
        out_t_ref[cols, :] = mixed.astype(jnp.bfloat16)
        out_ref[:, cols] = mixed.T.astype(jnp.bfloat16)
        lse_ref[h:h + 1, :] = top + jnp.log2(total)


def backward_kernel(place_ref, order_ref, q_ref, go_ref, out_ref, lse_ref, k0_ref, v0_ref, kv1_ref, kv2_ref,
                    dq_ref, dkv0_ref, dkv1_ref, dkv2_ref, acc_ref):
    tok, dim = k0_ref.shape
    heads = q_ref.shape[1] // dim
    scale = 1.0 / dim**0.5
    unit = math.log2(math.e) * scale
    hide = [None] + visibility(place_ref, order_ref)
    keys = [k0_ref[...], kv1_ref[:tok, :], kv2_ref[:tok, :]]
    values = [v0_ref[...], kv1_ref[tok:, :], kv2_ref[tok:, :]]
    keys_t = [key.T for key in keys]
    causal = lax.broadcasted_iota(jnp.int32, (tok, tok), 0) <= lax.broadcasted_iota(jnp.int32, (tok, tok), 1)
    for h in range(heads):
        cols = slice(h * dim, (h + 1) * dim)
        qh = q_ref[:, cols]
        gh = go_ref[:, cols]
        lse = lse_ref[h:h + 1, :]
        row_dot = jnp.sum((gh.astype(jnp.float32) * out_ref[:, cols].astype(jnp.float32)).T, axis=0, keepdims=True)
        dq_t = None
        for j in range(3):
            scores = dot(keys[j], qh, NT)
            if j == 0:
                scores = jnp.where(causal, scores, LOWEST)
            base = lse if j == 0 else lse + hide[j]
            weights = jnp.exp2(scores * unit - base)
            dprob = dot(values[j], gh, NT)
            dscore = (weights * (dprob - row_dot)).astype(jnp.bfloat16)
            piece = dot(keys_t[j], dscore, NN)
            dq_t = piece if dq_t is None else dq_t + piece
            dk = dot(dscore, qh, NN)
            dv = dot(weights.astype(jnp.bfloat16), gh, NN)
            if h == 0:
                acc_ref[j, 0] = dk
                acc_ref[j, 1] = dv
            else:
                acc_ref[j, 0] += dk
                acc_ref[j, 1] += dv
        dq_ref[:, cols] = (dq_t * scale).T.astype(jnp.bfloat16)
    for j, ref in enumerate((dkv0_ref, dkv1_ref, dkv2_ref)):
        ref[0] = (acc_ref[j, 0] * scale).astype(ref.dtype)
        ref[1] = acc_ref[j, 1].astype(ref.dtype)


def gram_kernel(place_ref, mine_ref, other_ref, part_ref):
    core = place_ref[1]
    planes, rows, _, unit, tok = mine_ref.shape
    feats = planes * rows * 2 * unit
    left = jnp.concatenate(
        [ref[:, :, core].reshape(planes * rows * unit, tok) for ref in (mine_ref, other_ref)], axis=1
    )
    wide = 2 * rows * unit * 2
    for first in range(0, feats, wide):
        at = first // (2 * rows * unit)
        right = jnp.concatenate([ref[at:at + 2].reshape(wide, tok) for ref in (mine_ref, other_ref)], axis=1)
        got = dot(left, right, NT).astype(jnp.bfloat16)
        for plane in range(planes):
            block = got[plane * rows * unit:(plane + 1) * rows * unit]
            part_ref[:, plane, :, first:first + wide] = block.reshape(rows, unit, wide)


SMEM = pl.BlockSpec(memory_space=pltpu.SMEM)
VMEM = pl.BlockSpec(memory_space=pltpu.VMEM)
PARAMS = pltpu.CompilerParams(vmem_limit_bytes=VMEM_LIMIT)


def forward(place, order, q, k0, v0, kv1, kv2):
    tok, width = q.shape
    heads = width // k0.shape[1]
    return pl.pallas_call(
        forward_kernel,
        out_shape=(jax.ShapeDtypeStruct((tok, width), jnp.bfloat16), jax.ShapeDtypeStruct((width, tok), jnp.bfloat16),
                   jax.ShapeDtypeStruct((heads, tok), jnp.float32)),
        in_specs=[SMEM] * 2 + [VMEM] * 5,
        out_specs=(VMEM,) * 3,
        compiler_params=PARAMS,
        cost_estimate=pl.CostEstimate(flops=4 * tok * width * 3 * tok, bytes_accessed=2000000, transcendentals=0),
        name="attention_forward",
    )(place, order, q, k0, v0, kv1, kv2)


def backward(place, order, q, go, out, lse, k0, v0, kv1, kv2):
    tok, width = q.shape
    dim = k0.shape[1]
    pair = jax.ShapeDtypeStruct((2, tok, dim), jnp.bfloat16)
    return pl.pallas_call(
        backward_kernel,
        out_shape=(jax.ShapeDtypeStruct((tok, width), jnp.bfloat16), jax.ShapeDtypeStruct((2, tok, dim), jnp.float32), pair, pair),
        in_specs=[SMEM] * 2 + [VMEM] * 8,
        out_specs=(VMEM,) * 4,
        scratch_shapes=[pltpu.VMEM((3, 2, tok, dim), jnp.float32)],
        compiler_params=PARAMS,
        cost_estimate=pl.CostEstimate(flops=10 * tok * width * 3 * tok, bytes_accessed=3000000, transcendentals=0),
        name="attention_backward",
    )(place, order, q, go, out, lse, k0, v0, kv1, kv2)


def gram_part(place, mine, other):
    planes, rows, cores, unit, tok = mine.shape
    feats = planes * rows * cores * unit
    return pl.pallas_call(
        gram_kernel,
        out_shape=jax.ShapeDtypeStruct((rows, planes, unit, feats), jnp.bfloat16),
        in_specs=[SMEM] + [VMEM] * 2,
        out_specs=VMEM,
        compiler_params=PARAMS,
        cost_estimate=pl.CostEstimate(flops=2 * feats * feats * tok, bytes_accessed=2000000, transcendentals=0),
        name="gram_part",
    )(place, mine, other)


CORES = 2
ROWS = 4


def shifted(block, distance):
    count = lax.axis_size("seq")
    return lax.ppermute(block, "seq", [(i, (i + distance) % count) for i in range(count)])


def local(query, key_in, value_input, output_gradient, block_order):
    tok, width = query.shape
    count = lax.axis_size("seq")
    planes = count // (CORES * ROWS)
    unit = width // count
    me = lax.axis_index("seq").astype(jnp.int32)
    place = jnp.stack([me, me % CORES])
    held = jnp.concatenate([key_in, value_input])
    kv2 = shifted(held, 2)
    kv1 = shifted(held, 1)
    out, out_t, lse = forward(place, block_order, query, key_in, value_input, kv1, kv2)
    other_t = lax.ppermute(out_t, "seq", [(i, i ^ 1) for i in range(count)])
    split = (planes, ROWS, CORES, unit, tok)
    part = gram_part(place, out_t.reshape(split), other_t.reshape(split))
    row_groups = [[(z * ROWS + y) * CORES + c for y in range(ROWS)] for z in range(planes) for c in range(CORES)]
    plane_groups = [[(z * ROWS + y) * CORES + c for z in range(planes)] for y in range(ROWS) for c in range(CORES)]
    part = lax.all_to_all(part, "seq", 0, 0, axis_index_groups=row_groups, tiled=True)
    d_query, kept, away1, away2 = backward(
        place, block_order, query, output_gradient, out, lse, key_in, value_input, kv1, kv2
    )
    part = jnp.sum(part.astype(jnp.float32), axis=0).astype(jnp.bfloat16)
    back2 = shifted(away2, -2)
    back1 = shifted(away1, -1)
    part = lax.all_to_all(part, "seq", 0, 0, axis_index_groups=plane_groups, tiled=True)
    gram = jnp.sum(part.astype(jnp.float32), axis=0) / (tok * count) ** 0.5
    total = kept + back1.astype(jnp.float32) + back2.astype(jnp.float32)
    return out, d_query, total.astype(jnp.bfloat16), gram[None]


def solution(mesh):
    in_specs = (P("seq", "head"), P("seq", "head"), P("seq", "head"), P("seq", "head"), P())
    out_specs = (P("seq", "head"), P("seq", "head"), P(None, "seq", "head"), P("head", "seq", None))
    return jax.shard_map(local, mesh=mesh, in_specs=in_specs, out_specs=out_specs, check_vma=False)
```

time: 500 us -> 85.3 us (0.17)
  the two profiles are of different devices: /device:TPU:6 before, /device:TPU:510 now
where the time goes in v1:
time: 85.3 us; the launch traced here: 84.8 us
  starting transfers between devices  27.5 us (32%)
  waiting for transfers between devices  20.1 us (24%)
  blocking collectives  17.6 us (21%)
  Pallas kernels  14.5 us (17%)
  other arithmetic  2.4 us (3%)
  local copies, waits for them, and re-layouts  1.96 us (2%)
    ppermute x4, waiting for transfers between devices, shifted(): lax.ppermute(block, 'seq', [(i, (i + distance) % count) for i in range(co...  18.2 us
    all_to_all x1, blocking collectives, local(): lax.all_to_all(part, 'seq', 0, 0, axis_index_groups=row_groups, tiled=True)  17.6 us
    ppermute x4, starting transfers between devices, shifted(): lax.ppermute(block, 'seq', [(i, (i + distance) % count) for i in range(co...  12.8 us
    all_to_all x1, starting transfers between devices, local(): lax.all_to_all(part, 'seq', 0, 0, axis_index_groups=plane_groups, tiled=T...  12.7 us
    pallas_call x1, Pallas kernels, backward(): pl.pallas_call(backward_kernel, out_shape=(jax.ShapeDtypeStruct((tok, wid...  8.08 us
    pallas_call x1, Pallas kernels, forward(): pl.pallas_call(forward_kernel, out_shape=(jax.ShapeDtypeStruct((tok, widt...  5.1 us
    unnamed x15, local copies, waits for them, and re-layouts  1.95 us
    ppermute x1, starting transfers between devices, local(): other_t = lax.ppermute(out_t, 'seq', [(i, i ^ 1) for i in range(count)])  1.91 us
  transfers between devices with their start and end apart: 6, of which 4 were waited for; matrix products, arithmetic and copies ran while one was open for 1% of the time, Pallas kernels for 10%

profile of v1, /device:TPU:510, one launch (start us, length us, event | category | flops | bytes accessed | tf_op | source)
XLA Modules:
  0.0 84.8 jit_solution(3853706190664370043)
XLA Ops:
  0.6 0.0 copy-start.1
  0.6 0.9 %constant_dynamic-update-slice_fusion.1 = bf16[512,128]{1,0:T(8,128)(2,1)S(1)} fusion(bf16[256,128]{1,0:T(8,128)(2,1)} %k0_ref.3), kind=kLoop, calls=%fused_computation.4 | loop fusion | bytes 131072
  1.5 0.0 copy-done.1
  1.5 0.0 copy-start
  1.5 6.5 %collective-permute-start.1 = (bf16[512,128]{1,0:T(8,128)(2,1)S(1)}, bf16[512,128]{1,0:T(8,128)(2,1)S(1)}, u32[]{:S(2)}, u32[]{:S(2)}) collective-permute-start(bf16[512,128]{1,0:T(8,128)(2,1)S(1)} %constant_dynamic-update-slice_fusion), channel_id=1, source_target_pairs={{0,16},{8,24},{16,32},{24,40},{32,48},{40,56},{48,64},{56,72},{64,... | collective-permute-start | bytes 393224 | tf_op jit(solution)/shard_map/ppermute | solution.py:177
  8.0 1.9 %collective-permute-start = (bf16[512,128]{1,0:T(8,128)(2,1)S(1)}, bf16[512,128]{1,0:T(8,128)(2,1)S(1)}, u32[]{:S(2)}, u32[]{:S(2)}) collective-permute-start(bf16[512,128]{1,0:T(8,128)(2,1)S(1)} %constant_dynamic-update-slice_fusion), channel_id=1, source_target_pairs={{0,8},{8,16},{16,24},{24,32},{32,40},{40,48},{48,56},{56,64},{64,7... | collective-permute-start | bytes 393224 | tf_op jit(solution)/shard_map/ppermute | solution.py:177
  9.9 0.0 copy-start.5
  10.0 0.1 pad_add_fusion.place_ref
  10.0 0.7 collective-permute-done.1.kv2_ref
  10.7 3.6 %collective-permute-done.kv1_ref = bf16[512,128]{1,0:T(8,128)(2,1)S(1)} collective-permute-done((bf16[512,128]{1,0:T(8,128)(2,1)S(1)}, bf16[512,128]{1,0:T(8,128)(2,1)S(1)}, u32[]{:S(2)}, u32[]{:S(2)}) %collective-permute-start) | collective-permute-done | bytes 131104 | tf_op jit(solution)/shard_map/ppermute | solution.py:177
  14.3 0.0 copy-done
  14.3 0.0 copy-done.5
  14.3 0.0 copy-start.2
  14.3 1.0 %copy-done.2 = bf16[256,1024]{1,0:T(8,128)(2,1)S(1)} copy-done((bf16[256,1024]{1,0:T(8,128)(2,1)S(1)}, bf16[256,1024]{1,0:T(8,128)(2,1)}, u32[]{:S(2)}) %copy-start.2) | copy-done | bytes 524312
  15.3 5.1 %attention_forward.1 = (bf16[256,1024]{1,0:T(8,128)(2,1)}, bf16[1024,256]{1,0:T(8,128)(2,1)S(1)}, f32[8,256]{1,0:T(8,128)S(1)}) custom-call(s32[2]{0:T(128)S(1)} %pad_add_fusion.place_ref, s32[64]{0:T(128)S(1)} %copy-done.5, bf16[256,1024]{1,0:T(8,128)(2,1)S(1)} %copy-done.2, bf16[256,128]{1,0:T(8,128)(2,1)S(1)} %copy-done, bf16[256,128]{1,0:T(8,128)(2,1)S(1)} %copy-done.1, ...), custom_call_target="tpu_custom_call" | custom-call | flops 805306368 | bytes 2000000 | tf_op jit(solution)/shard_map/attention_forward/pallas_call | solution.py:129
  20.4 1.9 %collective-permute-start.4 = (bf16[1024,256]{1,0:T(8,128)(2,1)S(1)}, bf16[1024,256]{1,0:T(8,128)(2,1)S(1)}, u32[]{:S(2)}, u32[]{:S(2)}) collective-permute-start(bf16[1024,256]{1,0:T(8,128)(2,1)S(1)} %get-tuple-element.17), channel_id=1, source_target_pairs={{0,8},{8,0},{16,24},{24,16},{32,40},{40,32},{48,56},{56,48},{64,72... | collective-permute-start | bytes 1572872 | tf_op jit(solution)/shard_map/ppermute | solution.py:191
  22.4 1.9 %collective-permute-done.4 = bf16[1024,256]{1,0:T(8,128)(2,1)S(1)} collective-permute-done((bf16[1024,256]{1,0:T(8,128)(2,1)S(1)}, bf16[1024,256]{1,0:T(8,128)(2,1)S(1)}, u32[]{:S(2)}, u32[]{:S(2)}) %collective-permute-start.4) | collective-permute-done | bytes 524320 | tf_op jit(solution)/shard_map/ppermute | solution.py:191
  24.2 1.3 %gram_part.1 = bf16[4,8,16,1024]{3,2,1,0:T(8,128)(2,1)S(1)} custom-call(s32[2]{0:T(128)S(1)} %pad_add_fusion.place_ref, bf16[8,4,2,16,256]{4,3,2,1,0:T(8,128)(2,1)S(1)} %bitcast.6, bf16[8,4,2,16,256]{4,3,2,1,0:T(8,128)(2,1)S(1)} %bitcast.7), custom_call_target="tpu_custom_call" | custom-call | flops 536870912 | bytes 2000000 | tf_op jit(solution)/shard_map/gram_part/pallas_call | solution.py:160
  25.5 17.6 %all_to_all.10 = bf16[4,8,16,1024]{3,2,1,0:T(8,128)(2,1)S(1)} all-to-all(bf16[4,8,16,1024]{3,2,1,0:T(8,128)(2,1)S(1)} %gram_part.1), channel_id=1, replica_groups={{0,16,32,48},{8,24,40,56},{64,80,96,112},{72,88,104,120},{128,144,160,1..., dimensions={0} | all-to-all | bytes 2097152 | tf_op jit(solution)/shard_map/all_to_all | solution.py:196
  43.2 0.0 copy-start.4
  43.2 0.0 copy-start.6
  43.2 1.0 %reduce_sum.21 = bf16[8,16,1024]{2,1,0:T(8,128)(2,1)} reduce(bf16[4,8,16,1024]{3,2,1,0:T(8,128)(2,1)S(1)} %all_to_all.10, bf16[]{:T(256)} %constant.23.clone.1), dimensions={0}, to_apply=%region_0.1 | reduce | flops 393216 | bytes 1310722 | tf_op jit(solution)/shard_map/reduce_sum | solution.py:200
  44.1 0.0 copy-start.3
  44.1 12.7 %all-to-all-start.1 = ((bf16[8,16,1024]{2,1,0:T(8,128)(2,1)}), bf16[8,16,1024]{2,1,0:T(8,128)(2,1)S(1)}, u32[]{:S(2)}, u32[]{:S(2)}) async-start(bf16[8,16,1024]{2,1,0:T(8,128)(2,1)} %reduce_sum.21), calls=%async_computation.1 | async-start | bytes 524288 | tf_op jit(solution)/shard_map/all_to_all | solution.py:203
  56.9 0.0 copy-done.4
  56.9 0.0 copy-done.6
  56.9 0.0 copy-done.3
  56.9 8.1 %attention_backward.1 = (bf16[256,1024]{1,0:T(8,128)(2,1)}, f32[2,256,128]{2,1,0:T(8,128)S(1)}, bf16[2,256,128]{2,1,0:T(8,128)(2,1)S(1)}, bf16[2,256,128]{2,1,0:T(8,128)(2,1)S(1)}) custom-call(s32[2]{0:T(128)S(1)} %pad_add_fusion.place_ref, s32[64]{0:T(128)S(1)} %copy-done.5, bf16[256,1024]{1,0:T(8,128)(2,1)S(1)} %copy-done.3, ...), custom_call_target="tpu_custom_call" | custom-call | flops 2013265920 | bytes 3000000 | tf_op jit(solution)/shard_map/attention_backward/pallas_call | solution.py:145
  64.9 1.9 %collective-permute-start.2 = (bf16[2,256,128]{2,1,0:T(8,128)(2,1)S(1)}, bf16[2,256,128]{2,1,0:T(8,128)(2,1)S(1)}, u32[]{:S(2)}, u32[]{:S(2)}) collective-permute-start(bf16[2,256,128]{2,1,0:T(8,128)(2,1)S(1)} %get-tuple-element.15), channel_id=1, source_target_pairs={{0,504},{8,0},{16,8},{24,16},{32,24},{40,32},{48,40},{56,48},{64,5... | collective-permute-start | bytes 393224 | tf_op jit(solution)/shard_map/ppermute | solution.py:177
  66.9 2.6 %collective-permute-start.3 = (bf16[2,256,128]{2,1,0:T(8,128)(2,1)S(1)}, bf16[2,256,128]{2,1,0:T(8,128)(2,1)S(1)}, u32[]{:S(2)}, u32[]{:S(2)}) collective-permute-start(bf16[2,256,128]{2,1,0:T(8,128)(2,1)S(1)} %get-tuple-element.16), channel_id=1, source_target_pairs={{0,496},{8,504},{16,0},{24,8},{32,16},{40,24},{48,32},{56,40},{64,... | collective-permute-start | bytes 393224 | tf_op jit(solution)/shard_map/ppermute | solution.py:177
  69.4 0.0 collective-permute-done.2
  69.4 13.9 %collective-permute-done.3 = bf16[2,256,128]{2,1,0:T(8,128)(2,1)S(1)} collective-permute-done((bf16[2,256,128]{2,1,0:T(8,128)(2,1)S(1)}, bf16[2,256,128]{2,1,0:T(8,128)(2,1)S(1)}, u32[]{:S(2)}, u32[]{:S(2)}) %collective-permute-start.3) | collective-permute-done | bytes 131104 | tf_op jit(solution)/shard_map/ppermute | solution.py:177
  83.4 0.7 add_convert_fusion
  84.1 0.0 all-to-all-done.1
  84.1 0.6 multiply_bitcast_fusion
  (2 shorter events, 0.1 us)
Async XLA Ops:
  0.6 0.9 %copy-start.1 = (bf16[256,128]{1,0:T(8,128)(2,1)S(1)}, bf16[256,128]{1,0:T(8,128)(2,1)}, u32[]{:S(2)}) copy-start(bf16[256,128]{1,0:T(8,128)(2,1)} %v0_ref.3) | copy-start | bytes 196612
  1.5 12.8 %copy-start = (bf16[256,128]{1,0:T(8,128)(2,1)S(1)}, bf16[256,128]{1,0:T(8,128)(2,1)}, u32[]{:S(2)}) copy-start(bf16[256,128]{1,0:T(8,128)(2,1)} %k0_ref.3) | copy-start | bytes 196612
  1.5 9.2 %collective-permute-start.1 = (bf16[512,128]{1,0:T(8,128)(2,1)S(1)}, bf16[512,128]{1,0:T(8,128)(2,1)S(1)}, u32[]{:S(2)}, u32[]{:S(2)}) collective-permute-start(bf16[512,128]{1,0:T(8,128)(2,1)S(1)} %constant_dynamic-update-slice_fusion), channel_id=1, source_target_pairs={{0,16},{8,24},{16,32},{24,40},{32,48},{40,56},{48,64},{56,72},{64,... | collective-permute-start | bytes 393224 | tf_op jit(solution)/shard_map/ppermute | solution.py:177
  8.0 6.3 %collective-permute-start = (bf16[512,128]{1,0:T(8,128)(2,1)S(1)}, bf16[512,128]{1,0:T(8,128)(2,1)S(1)}, u32[]{:S(2)}, u32[]{:S(2)}) collective-permute-start(bf16[512,128]{1,0:T(8,128)(2,1)S(1)} %constant_dynamic-update-slice_fusion), channel_id=1, source_target_pairs={{0,8},{8,16},{16,24},{24,32},{32,40},{40,48},{48,56},{56,64},{64,7... | collective-permute-start | bytes 393224 | tf_op jit(solution)/shard_map/ppermute | solution.py:177
  9.9 4.4 %copy-start.5 = (s32[64]{0:T(128)S(1)}, s32[64]{0:T(128)}, u32[]{:S(2)}) copy-start(s32[64]{0:T(128)} %order_ref.3) | copy-start | bytes 772
  14.3 1.0 %copy-start.2 = (bf16[256,1024]{1,0:T(8,128)(2,1)S(1)}, bf16[256,1024]{1,0:T(8,128)(2,1)}, u32[]{:S(2)}) copy-start(bf16[256,1024]{1,0:T(8,128)(2,1)} %q_ref.3) | copy-start | bytes 1572868
  20.4 3.8 %collective-permute-start.4 = (bf16[1024,256]{1,0:T(8,128)(2,1)S(1)}, bf16[1024,256]{1,0:T(8,128)(2,1)S(1)}, u32[]{:S(2)}, u32[]{:S(2)}) collective-permute-start(bf16[1024,256]{1,0:T(8,128)(2,1)S(1)} %get-tuple-element.17), channel_id=1, source_target_pairs={{0,8},{8,0},{16,24},{24,16},{32,40},{40,32},{48,56},{56,48},{64,72... | collective-permute-start | bytes 1572872 | tf_op jit(solution)/shard_map/ppermute | solution.py:191
  43.2 13.7 %copy-start.4 = (bf16[256,1024]{1,0:T(8,128)(2,1)S(1)}, bf16[256,1024]{1,0:T(8,128)(2,1)}, u32[]{:S(2)}) copy-start(bf16[256,1024]{1,0:T(8,128)(2,1)} %go_ref.1) | copy-start | bytes 1572868
  43.2 13.7 %copy-start.6 = (bf16[256,1024]{1,0:T(8,128)(2,1)S(1)}, bf16[256,1024]{1,0:T(8,128)(2,1)}, u32[]{:S(2)}) copy-start(bf16[256,1024]{1,0:T(8,128)(2,1)} %get-tuple-element.7.out_ref) | copy-start | bytes 1572868
  44.1 12.7 %copy-start.3 = (bf16[256,1024]{1,0:T(8,128)(2,1)S(1)}, bf16[256,1024]{1,0:T(8,128)(2,1)}, u32[]{:S(2)}) copy-start(bf16[256,1024]{1,0:T(8,128)(2,1)} %q_ref.3) | copy-start | bytes 1572868
  44.1 40.0 %all-to-all-start.1 = ((bf16[8,16,1024]{2,1,0:T(8,128)(2,1)}), bf16[8,16,1024]{2,1,0:T(8,128)(2,1)S(1)}, u32[]{:S(2)}, u32[]{:S(2)}) async-start(bf16[8,16,1024]{2,1,0:T(8,128)(2,1)} %reduce_sum.21), calls=%async_computation.1 | async-start | bytes 524288 | tf_op jit(solution)/shard_map/all_to_all | solution.py:203
  64.9 4.5 %collective-permute-start.2 = (bf16[2,256,128]{2,1,0:T(8,128)(2,1)S(1)}, bf16[2,256,128]{2,1,0:T(8,128)(2,1)S(1)}, u32[]{:S(2)}, u32[]{:S(2)}) collective-permute-start(bf16[2,256,128]{2,1,0:T(8,128)(2,1)S(1)} %get-tuple-element.15), channel_id=1, source_target_pairs={{0,504},{8,0},{16,8},{24,16},{32,24},{40,32},{48,40},{56,48},{64,5... | collective-permute-start | bytes 393224 | tf_op jit(solution)/shard_map/ppermute | solution.py:177
  66.9 16.5 %collective-permute-start.3 = (bf16[2,256,128]{2,1,0:T(8,128)(2,1)S(1)}, bf16[2,256,128]{2,1,0:T(8,128)(2,1)S(1)}, u32[]{:S(2)}, u32[]{:S(2)}) collective-permute-start(bf16[2,256,128]{2,1,0:T(8,128)(2,1)S(1)} %get-tuple-element.16), channel_id=1, source_target_pairs={{0,496},{8,504},{16,0},{24,8},{32,16},{40,24},{48,32},{56,40},{64,... | collective-permute-start | bytes 393224 | tf_op jit(solution)/shard_map/ppermute | solution.py:177

commit v2 on v1

v2 whole, which is shorter than its diff:
```python
import math

import jax
import jax.numpy as jnp
from jax import lax
from jax.experimental import pallas as pl
from jax.experimental.pallas import tpu as pltpu
from jax.sharding import PartitionSpec as P

NT = (((1,), (1,)), ((), ()))
NN = (((1,), (0,)), ((), ()))
LOWEST = -1e30
VMEM_LIMIT = 16 * 1024 * 1024


def dot(a, b, dims):
    return lax.dot_general(a, b, dims, preferred_element_type=jnp.float32)


def widened(block):
    return jnp.concatenate([block, jnp.ones(block.shape, block.dtype)], 1)


def twice(block):
    return jnp.concatenate([block, block], 1)


def own_kernel(place_ref, order_ref, q_ref, kv0_ref, q_out_ref, mixed_ref, top_ref, facts_ref):
    tok, dim = kv0_ref.shape[0] // 2, kv0_ref.shape[1]
    me = place_ref[0]
    count = order_ref.shape[0]
    mine = order_ref[me]
    for step in (1, 2):
        theirs = order_ref[lax.rem(me + count - step, count)]
        hide = jnp.where(theirs <= mine, 0.0, -LOWEST).astype(jnp.float32)
        facts_ref[step - 1:step, :] = jnp.full((1, dim), hide, jnp.float32)
    facts_ref[2:3, :] = jnp.full((1, dim), place_ref[1].astype(jnp.float32), jnp.float32)
    unit = math.log2(math.e) / dim**0.5
    key = kv0_ref[:tok, :]
    value = widened(kv0_ref[tok:, :])
    causal = lax.broadcasted_iota(jnp.int32, (tok, tok), 1) <= lax.broadcasted_iota(jnp.int32, (tok, tok), 0)
    q_out_ref[...] = q_ref[...]
    for h in range(q_ref.shape[1] // dim):
        scores = jnp.where(causal, dot(q_ref[:, h * dim:(h + 1) * dim], key, NT), LOWEST)
        top = jnp.max(scores, axis=1, keepdims=True) * unit
        expo = jnp.exp2(scores * unit - top)
        mixed_ref[h] = dot(expo.astype(jnp.bfloat16), value, NN)
        top_ref[h] = jnp.broadcast_to(top, (tok, dim))


def forward_kernel(facts_ref, q_ref, mixed_ref, top_ref, kv1_ref, kv2_ref, out_t_ref, lse_ref):
    heads, tok, dim = top_ref.shape
    unit = math.log2(math.e) / dim**0.5
    hide = [facts_ref[j:j + 1, :] for j in range(2)]
    keys = [kv_ref[:tok, :] for kv_ref in (kv1_ref, kv2_ref)]
    values = [widened(kv_ref[tok:, :]) for kv_ref in (kv1_ref, kv2_ref)]
    for h in range(heads):
        cols = slice(h * dim, (h + 1) * dim)
        qh = q_ref[:, cols]
        scores = [dot(qh, key, NT) for key in keys]
        own = top_ref[h]
        top = own
        for j in range(2):
            top = jnp.maximum(top, jnp.max(scores[j], axis=1, keepdims=True) * unit - hide[j])
        mixed = mixed_ref[h] * twice(jnp.exp2(own - top))
        for j in range(2):
            expo = jnp.exp2(scores[j] * unit - twice(top + hide[j]))
            mixed = mixed + dot(expo.astype(jnp.bfloat16), values[j], NN)
        total = mixed[:, dim:]
        out_t_ref[cols, :] = (mixed[:, :dim] / total).T.astype(jnp.bfloat16)
        lse_ref[h:h + 1, :] = (top + jnp.log2(total)).T[:1]


def away_kernel(facts_ref, q_ref, go_ref, out_t_ref, lse_ref, kv1_ref, kv2_ref, away1_ref, away2_ref, dscore_ref,
                row_dot_ref, acc_ref):
    heads, _, tok, _ = dscore_ref.shape
    dim = kv1_ref.shape[1]
    scale = 1.0 / dim**0.5
    unit = math.log2(math.e) * scale
    hide = [twice(facts_ref[j:j + 1, :]) for j in range(2)]
    keys = [kv_ref[:tok, :] for kv_ref in (kv1_ref, kv2_ref)]
    values = [kv_ref[tok:, :] for kv_ref in (kv1_ref, kv2_ref)]
    for h in range(heads):
        cols = slice(h * dim, (h + 1) * dim)
        qh = q_ref[:, cols]
        gh = go_ref[:, cols]
        out_t = out_t_ref[cols, :].astype(jnp.float32)
        row_dot = jnp.sum(gh.astype(jnp.float32).T * out_t, axis=0, keepdims=True)
        row_dot_ref[h:h + 1, :] = row_dot
        for j in range(2):
            weights = jnp.exp2(dot(keys[j], qh, NT) * unit - (lse_ref[h:h + 1, :] + hide[j]))
            dscore = (weights * (dot(values[j], gh, NT) - row_dot)).astype(jnp.bfloat16)
            dscore_ref[h, j] = dscore
            dk = dot(dscore, qh, NN)
            dv = dot(weights.astype(jnp.bfloat16), gh, NN)
            if h > 0:
                dk = acc_ref[j, 0] + dk
                dv = acc_ref[j, 1] + dv
            if h < heads - 1:
                acc_ref[j, 0] = dk
                acc_ref[j, 1] = dv
            else:
                away_ref = (away1_ref, away2_ref)[j]
                away_ref[0] = (dk * scale).astype(away_ref.dtype)
                away_ref[1] = dv.astype(away_ref.dtype)


def backward_kernel(q_ref, go_ref, out_t_ref, lse_ref, row_dot_ref, dscore_ref, kv0_ref, kv1_ref, kv2_ref,
                    out_ref, dq_ref, kept_ref, acc_ref):
    heads, _, tok, _ = dscore_ref.shape
    dim = kv0_ref.shape[1]
    scale = 1.0 / dim**0.5
    unit = math.log2(math.e) * scale
    key = kv0_ref[:tok, :]
    value = kv0_ref[tok:, :]
    keys_t = [kv_ref[:tok, :].T for kv_ref in (kv0_ref, kv1_ref, kv2_ref)]
    causal = lax.broadcasted_iota(jnp.int32, (tok, tok), 0) <= lax.broadcasted_iota(jnp.int32, (tok, tok), 1)
    for h in range(heads):
        cols = slice(h * dim, (h + 1) * dim)
        qh = q_ref[:, cols]
        gh = go_ref[:, cols]
        scores = jnp.where(causal, dot(key, qh, NT), LOWEST)
        weights = jnp.exp2(scores * unit - lse_ref[h:h + 1, :])
        dscore = (weights * (dot(value, gh, NT) - row_dot_ref[h:h + 1, :])).astype(jnp.bfloat16)
        dq_t = dot(keys_t[0], dscore, NN)
        for j in range(2):
            dq_t = dq_t + dot(keys_t[j + 1], dscore_ref[h, j], NN)
        dq_ref[:, cols] = (dq_t * scale).T.astype(jnp.bfloat16)
        out_ref[:, cols] = out_t_ref[cols, :].T
        dk = dot(dscore, qh, NN)
        dv = dot(weights.astype(jnp.bfloat16), gh, NN)
        if h > 0:
            dk = acc_ref[0] + dk
            dv = acc_ref[1] + dv
        if h < heads - 1:
            acc_ref[0] = dk
            acc_ref[1] = dv
        else:
            kept_ref[0] = dk * scale
            kept_ref[1] = dv


def gram_kernel(facts_ref, mine_ref, other_ref, part_hbm, part_ref, sems):
    core = facts_ref[2:3, :1].astype(jnp.bfloat16)
    planes, rows, cores, unit, tok = mine_ref.shape
    chunks = part_ref.shape[0]
    step = planes // chunks
    wide = step * rows * cores * unit
    picked = [ref[:, :, 0] * (1 - core) + ref[:, :, 1] * core for ref in (mine_ref, other_ref)]
    left = jnp.concatenate([block.reshape(planes * rows * unit, tok) for block in picked], axis=1)
    saves = []
    for i in range(chunks):
        right = jnp.concatenate(
            [ref[i * step:(i + 1) * step].reshape(wide, tok) for ref in (mine_ref, other_ref)], axis=1
        )
        got = dot(left, right, NT).astype(jnp.bfloat16)
        for plane in range(planes):
            block = got[plane * rows * unit:(plane + 1) * rows * unit]
            part_ref[i, :, plane] = block.reshape(rows, unit, wide)
        save = pltpu.make_async_copy(part_ref.at[i], part_hbm.at[:, :, :, pl.ds(i * wide, wide)], sems.at[i])
        save.start()
        saves.append(save)
    for save in saves:
        save.wait()


def row_sum_kernel(part_ref, sum_ref):
    total = part_ref[0].astype(jnp.float32)
    for i in range(1, part_ref.shape[0]):
        total = total + part_ref[i].astype(jnp.float32)
    sum_ref[...] = total.astype(sum_ref.dtype)


def key_value_sum_kernel(kept_ref, back1_ref, back2_ref, total_ref):
    total = kept_ref[...] + back1_ref[...].astype(jnp.float32) + back2_ref[...].astype(jnp.float32)
    total_ref[...] = total.astype(total_ref.dtype)


SMEM = pl.BlockSpec(memory_space=pltpu.SMEM)
VMEM = pl.BlockSpec(memory_space=pltpu.VMEM)
HBM = pl.BlockSpec(memory_space=pltpu.HBM)
PARAMS = pltpu.CompilerParams(vmem_limit_bytes=VMEM_LIMIT)


def own_block(place, order, q, kv0):
    tok, width = q.shape
    dim = kv0.shape[1]
    heads = width // dim
    return pl.pallas_call(
        own_kernel,
        out_shape=(jax.ShapeDtypeStruct(q.shape, q.dtype), jax.ShapeDtypeStruct((heads, tok, 2 * dim), jnp.float32),
                   jax.ShapeDtypeStruct((heads, tok, dim), jnp.float32), jax.ShapeDtypeStruct((8, dim), jnp.float32)),
        in_specs=[SMEM] * 2 + [VMEM] * 2,
        out_specs=(VMEM,) * 4,
        compiler_params=PARAMS,
        cost_estimate=pl.CostEstimate(flops=4 * tok * width * tok, bytes_accessed=6000000, transcendentals=0),
        name="own_block",
    )(place, order, q, kv0)


def forward(facts, q, mixed, top, kv1, kv2):
    tok, width = q.shape
    heads = top.shape[0]
    return pl.pallas_call(
        forward_kernel,
        out_shape=(jax.ShapeDtypeStruct((width, tok), jnp.bfloat16), jax.ShapeDtypeStruct((heads, tok), jnp.float32)),
        in_specs=[VMEM] * 6,
        out_specs=(VMEM,) * 2,
        compiler_params=PARAMS,
        cost_estimate=pl.CostEstimate(flops=8 * tok * width * tok, bytes_accessed=2000000, transcendentals=0),
        name="attention_forward",
    )(facts, q, mixed, top, kv1, kv2)


def away_gradients(facts, q, go, out_t, lse, kv1, kv2):
    tok, width = q.shape
    dim = kv1.shape[1]
    heads = width // dim
    pair = jax.ShapeDtypeStruct((2, tok, dim), jnp.bfloat16)
    return pl.pallas_call(
        away_kernel,
        out_shape=(pair, pair, jax.ShapeDtypeStruct((heads, 2, tok, tok), jnp.bfloat16),
                   jax.ShapeDtypeStruct((heads, tok), jnp.float32)),
        in_specs=[VMEM] * 7,
        out_specs=(VMEM,) * 4,
        scratch_shapes=[pltpu.VMEM((2, 2, tok, dim), jnp.float32)],
        compiler_params=PARAMS,
        cost_estimate=pl.CostEstimate(flops=16 * tok * width * tok, bytes_accessed=3000000, transcendentals=0),
        name="away_gradients",
    )(facts, q, go, out_t, lse, kv1, kv2)


def backward(q, go, out_t, lse, row_dot, dscore, kv0, kv1, kv2):
    tok, width = q.shape
    dim = kv0.shape[1]
    full = jax.ShapeDtypeStruct((tok, width), jnp.bfloat16)
    return pl.pallas_call(
        backward_kernel,
        out_shape=(full, full, jax.ShapeDtypeStruct((2, tok, dim), jnp.float32)),
        in_specs=[VMEM] * 9,
        out_specs=(VMEM,) * 3,
        scratch_shapes=[pltpu.VMEM((2, tok, dim), jnp.float32)],
        compiler_params=PARAMS,
        cost_estimate=pl.CostEstimate(flops=14 * tok * width * tok, bytes_accessed=3000000, transcendentals=0),
        name="attention_backward",
    )(q, go, out_t, lse, row_dot, dscore, kv0, kv1, kv2)


def gram_part(facts, mine, other):
    planes, rows, cores, unit, tok = mine.shape
    feats = planes * rows * cores * unit
    chunks = 4
    return pl.pallas_call(
        gram_kernel,
        out_shape=jax.ShapeDtypeStruct((rows, planes, unit, feats), jnp.bfloat16),
        in_specs=[VMEM] * 3,
        out_specs=HBM,
        scratch_shapes=[pltpu.VMEM((chunks, rows, planes, unit, feats // chunks), jnp.bfloat16),
                        pltpu.SemaphoreType.DMA((chunks,))],
        compiler_params=PARAMS,
        cost_estimate=pl.CostEstimate(flops=2 * feats * feats * tok, bytes_accessed=2000000, transcendentals=0),
        name="gram_part",
    )(facts, mine, other)


def row_sum(part):
    return pl.pallas_call(
        row_sum_kernel,
        out_shape=jax.ShapeDtypeStruct(part.shape[1:], part.dtype),
        in_specs=[VMEM],
        out_specs=VMEM,
        compiler_params=PARAMS,
        cost_estimate=pl.CostEstimate(flops=part.size, bytes_accessed=part.size * 2, transcendentals=0),
        name="row_sum",
    )(part)


def key_value_sum(kept, back1, back2):
    return pl.pallas_call(
        key_value_sum_kernel,
        out_shape=jax.ShapeDtypeStruct(kept.shape, jnp.bfloat16),
        in_specs=[VMEM] * 3,
        out_specs=VMEM,
        compiler_params=PARAMS,
        cost_estimate=pl.CostEstimate(flops=20 * 10**9, bytes_accessed=50 * 10**6, transcendentals=0),
        name="key_value_sum",
    )(kept, back1, back2)


CORES = 2
ROWS = 4


def shifted(block, distance):
    count = lax.axis_size("seq")
    return lax.ppermute(block, "seq", [(i, (i + distance) % count) for i in range(count)])


def local(query, key_in, value_input, output_gradient, block_order):
    tok, width = query.shape
    count = lax.axis_size("seq")
    planes = count // (CORES * ROWS)
    unit = width // count
    me = lax.axis_index("seq").astype(jnp.int32)
    place = jnp.stack([me, me % CORES])
    kv0 = jnp.stack([key_in, value_input]).reshape(2 * tok, -1)
    kv2 = shifted(kv0, 2)
    kv1 = shifted(kv0, 1)
    q_near, mixed, top, facts = own_block(place, block_order, query, kv0)
    out_t, lse = forward(facts, q_near, mixed, top, kv1, kv2)
    other_t = lax.ppermute(out_t, "seq", [(i, i ^ 1) for i in range(count)])
    split = (planes, ROWS, CORES, unit, tok)
    part = gram_part(facts, out_t.reshape(split), other_t.reshape(split))
    row_groups = [[(z * ROWS + y) * CORES + c for y in range(ROWS)] for z in range(planes) for c in range(CORES)]
    plane_groups = [[(z * ROWS + y) * CORES + c for z in range(planes)] for y in range(ROWS) for c in range(CORES)]
    part, lse = lax.optimization_barrier((part, lse))
    part = lax.all_to_all(part, "seq", 0, 0, axis_index_groups=row_groups, tiled=True)
    away1, away2, dscore, row_dot = away_gradients(facts, q_near, output_gradient, out_t, lse, kv1, kv2)
    back2 = shifted(away2, -2)
    back1 = shifted(away1, -1)
    out, d_query, kept = backward(q_near, output_gradient, out_t, lse, row_dot, dscore, kv0, kv1, kv2)
    part = row_sum(part)
    part, row_dot = lax.optimization_barrier((part, row_dot))
    part = lax.all_to_all(part, "seq", 0, 0, axis_index_groups=plane_groups, tiled=True)
    gram = jnp.sum(part.astype(jnp.float32), axis=0) / (tok * count) ** 0.5
    return out, d_query, key_value_sum(kept, back1, back2), gram[None]


def solution(mesh):
    in_specs = (P("seq", "head"), P("seq", "head"), P("seq", "head"), P("seq", "head"), P())
    out_specs = (P("seq", "head"), P("seq", "head"), P(None, "seq", "head"), P("head", "seq", None))
    return jax.shard_map(local, mesh=mesh, in_specs=in_specs, out_specs=out_specs, check_vma=False)
```

time: 85.3 us -> 73 us (0.86)
  the two profiles are of different devices: /device:TPU:510 before, /device:TPU:6 now
where the time goes in v2:
time: 73 us; the launch traced here: 72.4 us
  waiting for transfers between devices  29 us (40%)
  starting transfers between devices  23.7 us (32%)
  Pallas kernels  15.7 us (22%)
  local copies, waits for them, and re-layouts  1.7 us (2%)
  other arithmetic  1.64 us (2%)
  between operations  0.75 us (1%)
    all_to_all x1, waiting for transfers between devices, local(): lax.all_to_all(part, 'seq', 0, 0, axis_index_groups=plane_groups, tiled=T...  15.3 us
    ppermute x4, starting transfers between devices, shifted(): lax.ppermute(block, 'seq', [(i, (i + distance) % count) for i in range(co...  14.8 us
    ppermute x4, waiting for transfers between devices, shifted(): lax.ppermute(block, 'seq', [(i, (i + distance) % count) for i in range(co...  11.8 us
    pallas_call x1, Pallas kernels, away_gradients(): pl.pallas_call(away_kernel, out_shape=(pair, pair, jax.ShapeDtypeStruct((...  4.26 us
    pallas_call x1, Pallas kernels, backward(): pl.pallas_call(backward_kernel, out_shape=(full, full, jax.ShapeDtypeStru...  3.67 us
    all_to_all x1, starting transfers between devices, local(): lax.all_to_all(part, 'seq', 0, 0, axis_index_groups=row_groups, tiled=True)  3.53 us
    all_to_all x1, starting transfers between devices, local(): lax.all_to_all(part, 'seq', 0, 0, axis_index_groups=plane_groups, tiled=T...  3.41 us
    pallas_call x1, Pallas kernels, forward(): pl.pallas_call(forward_kernel, out_shape=(jax.ShapeDtypeStruct((width, to...  2.16 us
  transfers between devices with their start and end apart: 7, of which 4 were waited for; matrix products, arithmetic and copies ran while one was open for 0% of the time, Pallas kernels for 16%

profile of v2, /device:TPU:6, one launch (start us, length us, event | category | flops | bytes accessed | tf_op | source)
XLA Modules:
  0.0 72.4 jit_solution(11851661159602827147)
XLA Ops:
  0.6 0.9 %pad_maximum_fusion = bf16[2,256,128]{2,1,0:T(8,128)(2,1)S(1)} fusion(bf16[1,256,128]{2,1,0:T(8,128)(2,1)} %bitcast.15, bf16[1,256,128]{2,1,0:T(8,128)(2,1)} %bitcast.16), kind=kLoop, calls=%fused_computation.1 | loop fusion | flops 65536 | bytes 262144 | tf_op jit(solution)/shard_map/stack | solution.py:306
  1.5 3.5 %collective-permute-start.1 = (bf16[512,128]{1,0:T(8,128)(2,1)S(1)}, bf16[512,128]{1,0:T(8,128)(2,1)S(1)}, u32[]{:S(2)}, u32[]{:S(2)}) collective-permute-start(bf16[512,128]{1,0:T(8,128)(2,1)S(1)} %bitcast.10), channel_id=1, source_target_pairs={{0,16},{8,24},{16,32},{24,40},{32,48},{40,56},{48,64},{56,72},{64,... | collective-permute-start | bytes 393224 | tf_op jit(solution)/shard_map/ppermute | solution.py:296
  5.0 1.9 %collective-permute-start = (bf16[512,128]{1,0:T(8,128)(2,1)S(1)}, bf16[512,128]{1,0:T(8,128)(2,1)S(1)}, u32[]{:S(2)}, u32[]{:S(2)}) collective-permute-start(bf16[512,128]{1,0:T(8,128)(2,1)S(1)} %bitcast.11), channel_id=1, source_target_pairs={{0,8},{8,16},{16,24},{24,32},{32,40},{40,48},{48,56},{56,64},{64,7... | collective-permute-start | bytes 393224 | tf_op jit(solution)/shard_map/ppermute | solution.py:296
  7.0 0.1 pad_add_fusion.place_ref
  7.0 0.0 copy-start.1
  7.0 1.0 %copy-done.1 = bf16[256,1024]{1,0:T(8,128)(2,1)S(1)} copy-done((bf16[256,1024]{1,0:T(8,128)(2,1)S(1)}, bf16[256,1024]{1,0:T(8,128)(2,1)}, u32[]{:S(2)}) %copy-start.1) | copy-done | bytes 524312
  8.1 0.0 copy-start.2
  8.1 0.7 copy-done.2
  8.7 1.5 %own_block.1 = (bf16[256,1024]{1,0:T(8,128)(2,1)S(1)}, f32[8,256,256]{2,1,0:T(8,128)S(1)}, f32[8,256,128]{2,1,0:T(8,128)S(1)}, f32[8,128]{1,0:T(8,128)S(1)}) custom-call(s32[2]{0:T(128)S(1)} %pad_add_fusion.place_ref, s32[64]{0:T(128)S(1)} %copy-done.2, bf16[256,1024]{1,0:T(8,128)(2,1)S(1)} %copy-done.1, bf16[512,128]{1,0:T(8,128)(2,1)S(1)} %bitcast.12), custom_call_target="tpu_custom_call" | custom-call | flops 268435456 | bytes 6000000 | tf_op jit(solution)/shard_map/own_block/pallas_call | solution.py:189
  10.2 11.2 %collective-permute-done.1.kv2_ref = bf16[512,128]{1,0:T(8,128)(2,1)S(1)} collective-permute-done((bf16[512,128]{1,0:T(8,128)(2,1)S(1)}, bf16[512,128]{1,0:T(8,128)(2,1)S(1)}, u32[]{:S(2)}, u32[]{:S(2)}) %collective-permute-start.1) | collective-permute-done | bytes 131104 | tf_op jit(solution)/shard_map/ppermute | solution.py:296
  21.4 0.6 collective-permute-done.kv1_ref
  22.0 2.2 %attention_forward.1 = (bf16[1024,256]{1,0:T(8,128)(2,1)S(1)}, f32[8,256]{1,0:T(8,128)S(1)}) custom-call(f32[8,128]{1,0:T(8,128)S(1)} %get-tuple-element.21.facts_ref, bf16[256,1024]{1,0:T(8,128)(2,1)S(1)} %get-tuple-element.20.q_ref, f32[8,256,256]{2,1,0:T(8,128)S(1)} %get-tuple-element.22.mixed_ref, f32[8,256,128]{2,1,0:T(8,128)S(1)} %get-tuple-element.23.top_ref, ...), custom_call_target="tpu_custom_call" | custom-call | flops 536870912 | bytes 2000000 | tf_op jit(solution)/shard_map/attention_forward/pallas_call | solution.py:204
  24.2 1.9 %collective-permute-start.2 = (bf16[1024,256]{1,0:T(8,128)(2,1)S(1)}, bf16[1024,256]{1,0:T(8,128)(2,1)S(1)}, u32[]{:S(2)}, u32[]{:S(2)}) collective-permute-start(bf16[1024,256]{1,0:T(8,128)(2,1)S(1)} %get-tuple-element.24.out_t_ref), channel_id=1, source_target_pairs={{0,8},{8,0},{16,24},{24,16},{32,40},{40,32},{48,56},{56,48},{64,72... | collective-permute-start | bytes 1572872 | tf_op jit(solution)/shard_map/ppermute | solution.py:311
  26.1 1.9 %collective-permute-done.2 = bf16[1024,256]{1,0:T(8,128)(2,1)S(1)} collective-permute-done((bf16[1024,256]{1,0:T(8,128)(2,1)S(1)}, bf16[1024,256]{1,0:T(8,128)(2,1)S(1)}, u32[]{:S(2)}, u32[]{:S(2)}) %collective-permute-start.2) | collective-permute-done | bytes 524320 | tf_op jit(solution)/shard_map/ppermute | solution.py:311
  28.0 0.0 copy-start
  28.0 1.7 %gram_part.1 = bf16[4,8,16,1024]{3,2,1,0:T(8,128)(2,1)} custom-call(f32[8,128]{1,0:T(8,128)S(1)} %get-tuple-element.21.facts_ref, bf16[8,4,2,16,256]{4,3,2,1,0:T(8,128)(2,1)S(1)} %bitcast.9, bf16[8,4,2,16,256]{4,3,2,1,0:T(8,128)(2,1)S(1)} %bitcast.14), custom_call_target="tpu_custom_call" | custom-call | flops 536870912 | bytes 2000000 | tf_op jit(solution)/shard_map/gram_part/pallas_call | solution.py:253
  29.7 3.5 %all-to-all-start = ((bf16[4,8,16,1024]{3,2,1,0:T(8,128)(2,1)}), bf16[4,8,16,1024]{3,2,1,0:T(8,128)(2,1)S(1)}, u32[]{:S(2)}, u32[]{:S(2)}) async-start(bf16[4,8,16,1024]{3,2,1,0:T(8,128)(2,1)} %gram_part.1), calls=%async_computation | async-start | bytes 2097152 | tf_op jit(solution)/shard_map/all_to_all | solution.py:317
  33.2 0.0 copy-done
  33.2 4.3 %away_gradients.1 = (bf16[2,256,128]{2,1,0:T(8,128)(2,1)}, bf16[2,256,128]{2,1,0:T(8,128)(2,1)S(1)}, bf16[8,2,256,256]{3,2,1,0:T(8,128)(2,1)S(1)}, f32[8,256]{1,0:T(8,128)S(1)}) custom-call(f32[8,128]{1,0:T(8,128)S(1)} %get-tuple-element.21.facts_ref, bf16[256,1024]{1,0:T(8,128)(2,1)S(1)} %get-tuple-element.20.q_ref, bf16[256,1024]{1,0:T(8,128)(2,1)S(1)} %copy-done, ...), custom_call_target="tpu_custom_call" | custom-call | flops 1073741824 | bytes 3000000 | tf_op jit(solution)/shard_map/away_gradients/pallas_call | solution.py:220
  37.5 6.6 %collective-permute-start.3 = (bf16[2,256,128]{2,1,0:T(8,128)(2,1)}, bf16[2,256,128]{2,1,0:T(8,128)(2,1)S(1)}, u32[]{:S(2)}, u32[]{:S(2)}) collective-permute-start(bf16[2,256,128]{2,1,0:T(8,128)(2,1)} %get-tuple-element.32), channel_id=1, source_target_pairs={{0,504},{8,0},{16,8},{24,16},{32,24},{40,32},{48,40},{56,48},{64,5... | collective-permute-start | bytes 393224 | tf_op jit(solution)/shard_map/ppermute | solution.py:296
  44.1 2.8 %collective-permute-start.4 = (bf16[2,256,128]{2,1,0:T(8,128)(2,1)S(1)}, bf16[2,256,128]{2,1,0:T(8,128)(2,1)}, u32[]{:S(2)}, u32[]{:S(2)}) collective-permute-start(bf16[2,256,128]{2,1,0:T(8,128)(2,1)S(1)} %get-tuple-element.33), channel_id=1, source_target_pairs={{0,496},{8,504},{16,0},{24,8},{32,16},{40,24},{48,32},{56,40},{64,... | collective-permute-start | bytes 393224 | tf_op jit(solution)/shard_map/ppermute | solution.py:296
  46.9 3.7 %attention_backward.1 = (bf16[256,1024]{1,0:T(8,128)(2,1)}, bf16[256,1024]{1,0:T(8,128)(2,1)}, f32[2,256,128]{2,1,0:T(8,128)S(1)}) custom-call(bf16[256,1024]{1,0:T(8,128)(2,1)S(1)} %get-tuple-element.20.q_ref, bf16[256,1024]{1,0:T(8,128)(2,1)S(1)} %copy-done, bf16[1024,256]{1,0:T(8,128)(2,1)S(1)} %get-tuple-element.24.out_t_ref, ...), custom_call_target="tpu_custom_call" | custom-call | flops 939524096 | bytes 3000000 | tf_op jit(solution)/shard_map/attention_backward/pallas_call | solution.py:237
  50.6 0.0 all-to-all-done.part_ref
  50.6 0.8 %row_sum.1 = bf16[8,16,1024]{2,1,0:T(8,128)(2,1)} custom-call(bf16[4,8,16,1024]{3,2,1,0:T(8,128)(2,1)S(1)} %all-to-all-done.part_ref), custom_call_target="tpu_custom_call" | custom-call | flops 524288 | bytes 1048576 | tf_op jit(solution)/shard_map/row_sum/pallas_call | solution.py:267
  51.4 3.4 %all-to-all-start.1 = ((bf16[8,16,1024]{2,1,0:T(8,128)(2,1)}), bf16[8,16,1024]{2,1,0:T(8,128)(2,1)S(1)}, u32[]{:S(2)}, u32[]{:S(2)}) async-start(bf16[8,16,1024]{2,1,0:T(8,128)(2,1)} %row_sum.1), calls=%async_computation.1 | async-start | bytes 524288 | tf_op jit(solution)/shard_map/all_to_all | solution.py:324
  54.8 0.0 collective-permute-done.3.back1_ref
  54.8 0.0 collective-permute-done.4.back2_ref
  54.9 1.6 %key_value_sum.1 = bf16[2,256,128]{2,1,0:T(8,128)(2,1)} custom-call(f32[2,256,128]{2,1,0:T(8,128)S(1)} %get-tuple-element.31.kept_ref, bf16[2,256,128]{2,1,0:T(8,128)(2,1)S(1)} %collective-permute-done.3.back1_ref, bf16[2,256,128]{2,1,0:T(8,128)(2,1)} %collective-permute-done.4.back2_ref), custom_call_target="tpu_custom_call" | custom-call | flops 20000000000 | bytes 50000000 | tf_op jit(solution)/shard_map/key_value_sum/pallas_call | solution.py:279
  56.5 15.3 %all-to-all-done.1 = bf16[8,16,1024]{2,1,0:T(8,128)(2,1)S(1)} async-done(((bf16[8,16,1024]{2,1,0:T(8,128)(2,1)}), bf16[8,16,1024]{2,1,0:T(8,128)(2,1)S(1)}, u32[]{:S(2)}, u32[]{:S(2)}) %all-to-all-start.1) | async-done | bytes 262176 | tf_op jit(solution)/shard_map/all_to_all | solution.py:324
  71.8 0.6 multiply_bitcast_fusion
  (1 shorter events, 0.0 us)
Async XLA Ops:
  1.5 19.9 %collective-permute-start.1 = (bf16[512,128]{1,0:T(8,128)(2,1)S(1)}, bf16[512,128]{1,0:T(8,128)(2,1)S(1)}, u32[]{:S(2)}, u32[]{:S(2)}) collective-permute-start(bf16[512,128]{1,0:T(8,128)(2,1)S(1)} %bitcast.10), channel_id=1, source_target_pairs={{0,16},{8,24},{16,32},{24,40},{32,48},{40,56},{48,64},{56,72},{64,... | collective-permute-start | bytes 393224 | tf_op jit(solution)/shard_map/ppermute | solution.py:296
  5.0 17.0 %collective-permute-start = (bf16[512,128]{1,0:T(8,128)(2,1)S(1)}, bf16[512,128]{1,0:T(8,128)(2,1)S(1)}, u32[]{:S(2)}, u32[]{:S(2)}) collective-permute-start(bf16[512,128]{1,0:T(8,128)(2,1)S(1)} %bitcast.11), channel_id=1, source_target_pairs={{0,8},{8,16},{16,24},{24,32},{32,40},{40,48},{48,56},{56,64},{64,7... | collective-permute-start | bytes 393224 | tf_op jit(solution)/shard_map/ppermute | solution.py:296
  7.0 1.0 %copy-start.1 = (bf16[256,1024]{1,0:T(8,128)(2,1)S(1)}, bf16[256,1024]{1,0:T(8,128)(2,1)}, u32[]{:S(2)}) copy-start(bf16[256,1024]{1,0:T(8,128)(2,1)} %q_ref.1) | copy-start | bytes 1572868
  8.1 0.7 copy-start.2
  24.2 3.8 %collective-permute-start.2 = (bf16[1024,256]{1,0:T(8,128)(2,1)S(1)}, bf16[1024,256]{1,0:T(8,128)(2,1)S(1)}, u32[]{:S(2)}, u32[]{:S(2)}) collective-permute-start(bf16[1024,256]{1,0:T(8,128)(2,1)S(1)} %get-tuple-element.24.out_t_ref), channel_id=1, source_target_pairs={{0,8},{8,0},{16,24},{24,16},{32,40},{40,32},{48,56},{56,48},{64,72... | collective-permute-start | bytes 1572872 | tf_op jit(solution)/shard_map/ppermute | solution.py:311
  28.0 5.2 %copy-start = (bf16[256,1024]{1,0:T(8,128)(2,1)S(1)}, bf16[256,1024]{1,0:T(8,128)(2,1)}, u32[]{:S(2)}) copy-start(bf16[256,1024]{1,0:T(8,128)(2,1)} %go_ref.3) | copy-start | bytes 1572868
  29.7 20.9 %all-to-all-start = ((bf16[4,8,16,1024]{3,2,1,0:T(8,128)(2,1)}), bf16[4,8,16,1024]{3,2,1,0:T(8,128)(2,1)S(1)}, u32[]{:S(2)}, u32[]{:S(2)}) async-start(bf16[4,8,16,1024]{3,2,1,0:T(8,128)(2,1)} %gram_part.1), calls=%async_computation | async-start | bytes 2097152 | tf_op jit(solution)/shard_map/all_to_all | solution.py:317
  37.5 17.3 %collective-permute-start.3 = (bf16[2,256,128]{2,1,0:T(8,128)(2,1)}, bf16[2,256,128]{2,1,0:T(8,128)(2,1)S(1)}, u32[]{:S(2)}, u32[]{:S(2)}) collective-permute-start(bf16[2,256,128]{2,1,0:T(8,128)(2,1)} %get-tuple-element.32), channel_id=1, source_target_pairs={{0,504},{8,0},{16,8},{24,16},{32,24},{40,32},{48,40},{56,48},{64,5... | collective-permute-start | bytes 393224 | tf_op jit(solution)/shard_map/ppermute | solution.py:296
  44.1 10.7 %collective-permute-start.4 = (bf16[2,256,128]{2,1,0:T(8,128)(2,1)S(1)}, bf16[2,256,128]{2,1,0:T(8,128)(2,1)}, u32[]{:S(2)}, u32[]{:S(2)}) collective-permute-start(bf16[2,256,128]{2,1,0:T(8,128)(2,1)S(1)} %get-tuple-element.33), channel_id=1, source_target_pairs={{0,496},{8,504},{16,0},{24,8},{32,16},{40,24},{48,32},{56,40},{64,... | collective-permute-start | bytes 393224 | tf_op jit(solution)/shard_map/ppermute | solution.py:296
  51.4 20.3 %all-to-all-start.1 = ((bf16[8,16,1024]{2,1,0:T(8,128)(2,1)}), bf16[8,16,1024]{2,1,0:T(8,128)(2,1)S(1)}, u32[]{:S(2)}, u32[]{:S(2)}) async-start(bf16[8,16,1024]{2,1,0:T(8,128)(2,1)} %row_sum.1), calls=%async_computation.1 | async-start | bytes 524288 | tf_op jit(solution)/shard_map/all_to_all | solution.py:324

commit v3 on v2

--- a/solution.py
+++ b/solution.py
@@ -71,13 +71,14 @@
         lse_ref[h:h + 1, :] = (top + jnp.log2(total)).T[:1]
 
 
-def away_kernel(facts_ref, q_ref, go_ref, out_t_ref, lse_ref, kv1_ref, kv2_ref, away1_ref, away2_ref, dscore_ref,
-                row_dot_ref, acc_ref):
+def away_kernel(facts_ref, q_ref, go_ref, out_t_ref, lse_ref, kv1_ref, kv2_ref, away1_ref, away2_ref, out_hbm, dscore_ref,
+                row_dot_ref, acc_ref, out_ref, sems):
     heads, _, tok, _ = dscore_ref.shape
     dim = kv1_ref.shape[1]
     scale = 1.0 / dim**0.5
     unit = math.log2(math.e) * scale
     hide = [twice(facts_ref[j:j + 1, :]) for j in range(2)]
+    saves = [pltpu.make_async_copy(out_ref.at[h], out_hbm.at[:, pl.ds(h * dim, dim)], sems.at[h]) for h in range(heads)]
     keys = [kv_ref[:tok, :] for kv_ref in (kv1_ref, kv2_ref)]
     values = [kv_ref[tok:, :] for kv_ref in (kv1_ref, kv2_ref)]
     for h in range(heads):
@@ -87,6 +88,8 @@
         out_t = out_t_ref[cols, :].astype(jnp.float32)
         row_dot = jnp.sum(gh.astype(jnp.float32).T * out_t, axis=0, keepdims=True)
         row_dot_ref[h:h + 1, :] = row_dot
+        out_ref[h] = out_t.T.astype(jnp.bfloat16)
+        saves[h].start()
         for j in range(2):
             weights = jnp.exp2(dot(keys[j], qh, NT) * unit - (lse_ref[h:h + 1, :] + hide[j]))
             dscore = (weights * (dot(values[j], gh, NT) - row_dot)).astype(jnp.bfloat16)
@@ -103,10 +106,11 @@
                 away_ref = (away1_ref, away2_ref)[j]
                 away_ref[0] = (dk * scale).astype(away_ref.dtype)
                 away_ref[1] = dv.astype(away_ref.dtype)
-
-
-def backward_kernel(q_ref, go_ref, out_t_ref, lse_ref, row_dot_ref, dscore_ref, kv0_ref, kv1_ref, kv2_ref,
-                    out_ref, dq_ref, kept_ref, acc_ref):
+    for save in saves:
+        save.wait()
+
+
+def backward_kernel(q_ref, go_ref, lse_ref, row_dot_ref, dscore_ref, kv0_ref, kv1_ref, kv2_ref, after_ref, dq_ref, kept_ref, acc_ref):
     heads, _, tok, _ = dscore_ref.shape
     dim = kv0_ref.shape[1]
     scale = 1.0 / dim**0.5
@@ -126,7 +130,6 @@
         for j in range(2):
             dq_t = dq_t + dot(keys_t[j + 1], dscore_ref[h, j], NN)
         dq_ref[:, cols] = (dq_t * scale).T.astype(jnp.bfloat16)
-        out_ref[:, cols] = out_t_ref[cols, :].T
         dk = dot(dscore, qh, NN)
         dv = dot(weights.astype(jnp.bfloat16), gh, NN)
         if h > 0:
@@ -156,7 +159,8 @@
         got = dot(left, right, NT).astype(jnp.bfloat16)
         for plane in range(planes):
             block = got[plane * rows * unit:(plane + 1) * rows * unit]
-            part_ref[i, :, plane] = block.reshape(rows, unit, wide)
+            first = (plane % 2) * rows
+            part_ref[i, first:first + rows, plane // 2] = block.reshape(rows, unit, wide)
         save = pltpu.make_async_copy(part_ref.at[i], part_hbm.at[:, :, :, pl.ds(i * wide, wide)], sems.at[i])
         save.start()
         saves.append(save)
@@ -219,31 +223,32 @@
     pair = jax.ShapeDtypeStruct((2, tok, dim), jnp.bfloat16)
     return pl.pallas_call(
         away_kernel,
-        out_shape=(pair, pair, jax.ShapeDtypeStruct((heads, 2, tok, tok), jnp.bfloat16),
-                   jax.ShapeDtypeStruct((heads, tok), jnp.float32)),
+        out_shape=(pair, pair, jax.ShapeDtypeStruct((tok, width), jnp.bfloat16),
+                   jax.ShapeDtypeStruct((heads, 2, tok, tok), jnp.bfloat16), jax.ShapeDtypeStruct((heads, tok), jnp.float32)),
         in_specs=[VMEM] * 7,
-        out_specs=(VMEM,) * 4,
-        scratch_shapes=[pltpu.VMEM((2, 2, tok, dim), jnp.float32)],
+        out_specs=(VMEM, VMEM, HBM, VMEM, VMEM),
+        scratch_shapes=[pltpu.VMEM((2, 2, tok, dim), jnp.float32), pltpu.VMEM((heads, tok, dim), jnp.bfloat16),
+                        pltpu.SemaphoreType.DMA((heads,))],
         compiler_params=PARAMS,
         cost_estimate=pl.CostEstimate(flops=16 * tok * width * tok, bytes_accessed=3000000, transcendentals=0),
         name="away_gradients",
     )(facts, q, go, out_t, lse, kv1, kv2)
 
 
-def backward(q, go, out_t, lse, row_dot, dscore, kv0, kv1, kv2):
+def backward(q, go, lse, row_dot, dscore, kv0, kv1, kv2, after):
     tok, width = q.shape
     dim = kv0.shape[1]
     full = jax.ShapeDtypeStruct((tok, width), jnp.bfloat16)
     return pl.pallas_call(
         backward_kernel,
-        out_shape=(full, full, jax.ShapeDtypeStruct((2, tok, dim), jnp.float32)),
-        in_specs=[VMEM] * 9,
-        out_specs=(VMEM,) * 3,
+        out_shape=(full, jax.ShapeDtypeStruct((2, tok, dim), jnp.float32)),
+        in_specs=[VMEM] * 8 + [HBM],
+        out_specs=(VMEM,) * 2,
         scratch_shapes=[pltpu.VMEM((2, tok, dim), jnp.float32)],
         compiler_params=PARAMS,
         cost_estimate=pl.CostEstimate(flops=14 * tok * width * tok, bytes_accessed=3000000, transcendentals=0),
         name="attention_backward",
-    )(q, go, out_t, lse, row_dot, dscore, kv0, kv1, kv2)
+    )(q, go, lse, row_dot, dscore, kv0, kv1, kv2, after)
 
 
 def gram_part(facts, mine, other):
@@ -252,10 +257,10 @@
     chunks = 4
     return pl.pallas_call(
         gram_kernel,
-        out_shape=jax.ShapeDtypeStruct((rows, planes, unit, feats), jnp.bfloat16),
+        out_shape=jax.ShapeDtypeStruct((2 * rows, planes // 2, unit, feats), jnp.bfloat16),
         in_specs=[VMEM] * 3,
         out_specs=HBM,
-        scratch_shapes=[pltpu.VMEM((chunks, rows, planes, unit, feats // chunks), jnp.bfloat16),
+        scratch_shapes=[pltpu.VMEM((chunks, 2 * rows, planes // 2, unit, feats // chunks), jnp.bfloat16),
                         pltpu.SemaphoreType.DMA((chunks,))],
         compiler_params=PARAMS,
         cost_estimate=pl.CostEstimate(flops=2 * feats * feats * tok, bytes_accessed=2000000, transcendentals=0),
@@ -311,17 +316,23 @@
     other_t = lax.ppermute(out_t, "seq", [(i, i ^ 1) for i in range(count)])
     split = (planes, ROWS, CORES, unit, tok)
     part = gram_part(facts, out_t.reshape(split), other_t.reshape(split))
-    row_groups = [[(z * ROWS + y) * CORES + c for y in range(ROWS)] for z in range(planes) for c in range(CORES)]
-    plane_groups = [[(z * ROWS + y) * CORES + c for z in range(planes)] for y in range(ROWS) for c in range(CORES)]
+    seat = lambda z, y, c: (z * ROWS + y) * CORES + c
+    near_groups = [
+        [seat(2 * half + side, y, c) for side in range(2) for y in range(ROWS)]
+        for half in range(planes // 2) for c in range(CORES)
+    ]
+    far_groups = [
+        [seat(2 * half + side, y, c) for half in range(planes // 2)]
+        for side in range(2) for y in range(ROWS) for c in range(CORES)
+    ]
     part, lse = lax.optimization_barrier((part, lse))
-    part = lax.all_to_all(part, "seq", 0, 0, axis_index_groups=row_groups, tiled=True)
-    away1, away2, dscore, row_dot = away_gradients(facts, q_near, output_gradient, out_t, lse, kv1, kv2)
+    part = lax.all_to_all(part, "seq", 0, 0, axis_index_groups=near_groups, tiled=True)
+    away1, away2, out, dscore, row_dot = away_gradients(facts, q_near, output_gradient, out_t, lse, kv1, kv2)
     back2 = shifted(away2, -2)
     back1 = shifted(away1, -1)
-    out, d_query, kept = backward(q_near, output_gradient, out_t, lse, row_dot, dscore, kv0, kv1, kv2)
     part = row_sum(part)
-    part, row_dot = lax.optimization_barrier((part, row_dot))
-    part = lax.all_to_all(part, "seq", 0, 0, axis_index_groups=plane_groups, tiled=True)
+    d_query, kept = backward(q_near, output_gradient, lse, row_dot, dscore, kv0, kv1, kv2, part)
+    part = lax.all_to_all(part, "seq", 0, 0, axis_index_groups=far_groups, tiled=True)
     gram = jnp.sum(part.astype(jnp.float32), axis=0) / (tok * count) ** 0.5
     return out, d_query, key_value_sum(kept, back1, back2), gram[None]
 

time: 73 us -> 67.2 us (0.921)
  the two profiles are of different devices: /device:TPU:6 before, /device:TPU:8 now
where the time goes in v3:
time: 67.2 us; the launch traced here: 66.7 us
  starting transfers between devices  33 us (49%)
  Pallas kernels  14.8 us (22%)
  waiting for transfers between devices  11.9 us (18%)
  local copies, waits for them, and re-layouts  4.61 us (7%)
  other arithmetic  1.62 us (2%)
  between operations  0.75 us (1%)
    all_to_all x1, starting transfers between devices, local(): lax.all_to_all(part, 'seq', 0, 0, axis_index_groups=near_groups, tiled=True)  15.1 us
    ppermute x4, starting transfers between devices, shifted(): lax.ppermute(block, 'seq', [(i, (i + distance) % count) for i in range(co...  12.7 us
    all_to_all x1, waiting for transfers between devices, local(): lax.all_to_all(part, 'seq', 0, 0, axis_index_groups=far_groups, tiled=True)  5.77 us
    unnamed x10, local copies, waits for them, and re-layouts  4.61 us
    pallas_call x1, Pallas kernels, away_gradients(): pl.pallas_call(away_kernel, out_shape=(pair, pair, jax.ShapeDtypeStruct((...  4.42 us
    pallas_call x1, Pallas kernels, backward(): pl.pallas_call(backward_kernel, out_shape=(full, jax.ShapeDtypeStruct((2,...  3.57 us
    all_to_all x1, starting transfers between devices, local(): lax.all_to_all(part, 'seq', 0, 0, axis_index_groups=far_groups, tiled=True)  3.32 us
    ppermute x4, waiting for transfers between devices, shifted(): lax.ppermute(block, 'seq', [(i, (i + distance) % count) for i in range(co...  2.51 us
  transfers between devices with their start and end apart: 7, of which 4 were waited for; matrix products, arithmetic and copies ran while one was open for 0% of the time, Pallas kernels for 16%

profile of v3, /device:TPU:8, one launch (start us, length us, event | category | flops | bytes accessed | tf_op | source)
XLA Modules:
  0.0 66.7 jit_solution(10781145483337362262)
XLA Ops:
  0.6 0.9 %pad_maximum_fusion = bf16[2,256,128]{2,1,0:T(8,128)(2,1)S(1)} fusion(bf16[1,256,128]{2,1,0:T(8,128)(2,1)} %bitcast.15, bf16[1,256,128]{2,1,0:T(8,128)(2,1)} %bitcast.16), kind=kLoop, calls=%fused_computation.1 | loop fusion | flops 65536 | bytes 262144 | tf_op jit(solution)/shard_map/stack | solution.py:311
  1.5 3.5 %collective-permute-start.1 = (bf16[512,128]{1,0:T(8,128)(2,1)S(1)}, bf16[512,128]{1,0:T(8,128)(2,1)S(1)}, u32[]{:S(2)}, u32[]{:S(2)}) collective-permute-start(bf16[512,128]{1,0:T(8,128)(2,1)S(1)} %bitcast.9), channel_id=1, source_target_pairs={{0,16},{8,24},{16,32},{24,40},{32,48},{40,56},{48,64},{56,72},{64,... | collective-permute-start | bytes 393224 | tf_op jit(solution)/shard_map/ppermute | solution.py:301
  5.0 1.9 %collective-permute-start = (bf16[512,128]{1,0:T(8,128)(2,1)S(1)}, bf16[512,128]{1,0:T(8,128)(2,1)S(1)}, u32[]{:S(2)}, u32[]{:S(2)}) collective-permute-start(bf16[512,128]{1,0:T(8,128)(2,1)S(1)} %bitcast.10), channel_id=1, source_target_pairs={{0,8},{8,16},{16,24},{24,32},{32,40},{40,48},{48,56},{56,64},{64,7... | collective-permute-start | bytes 393224 | tf_op jit(solution)/shard_map/ppermute | solution.py:301
  7.0 0.1 pad_add_fusion.place_ref
  7.0 0.0 copy-start.3
  7.0 1.0 %copy-done.3 = bf16[256,1024]{1,0:T(8,128)(2,1)S(1)} copy-done((bf16[256,1024]{1,0:T(8,128)(2,1)S(1)}, bf16[256,1024]{1,0:T(8,128)(2,1)}, u32[]{:S(2)}) %copy-start.3) | copy-done | bytes 524312
  8.1 0.0 copy-start.4
  8.1 0.7 copy-done.4
  8.7 1.5 %own_block.1 = (bf16[256,1024]{1,0:T(8,128)(2,1)S(1)}, f32[8,256,256]{2,1,0:T(8,128)S(1)}, f32[8,256,128]{2,1,0:T(8,128)S(1)}, f32[8,128]{1,0:T(8,128)S(1)}) custom-call(s32[2]{0:T(128)S(1)} %pad_add_fusion.place_ref, s32[64]{0:T(128)S(1)} %copy-done.4, bf16[256,1024]{1,0:T(8,128)(2,1)S(1)} %copy-done.3, bf16[512,128]{1,0:T(8,128)(2,1)S(1)} %bitcast.11), custom_call_target="tpu_custom_call" | custom-call | flops 268435456 | bytes 6000000 | tf_op jit(solution)/shard_map/own_block/pallas_call | solution.py:193
  10.2 2.5 %collective-permute-done.1.kv2_ref = bf16[512,128]{1,0:T(8,128)(2,1)S(1)} collective-permute-done((bf16[512,128]{1,0:T(8,128)(2,1)S(1)}, bf16[512,128]{1,0:T(8,128)(2,1)S(1)}, u32[]{:S(2)}, u32[]{:S(2)}) %collective-permute-start.1) | collective-permute-done | bytes 131104 | tf_op jit(solution)/shard_map/ppermute | solution.py:301
  12.7 0.0 collective-permute-done.kv1_ref
  12.7 2.2 %attention_forward.1 = (bf16[1024,256]{1,0:T(8,128)(2,1)S(1)}, f32[8,256]{1,0:T(8,128)S(1)}) custom-call(f32[8,128]{1,0:T(8,128)S(1)} %get-tuple-element.19.facts_ref, bf16[256,1024]{1,0:T(8,128)(2,1)S(1)} %get-tuple-element.20.q_ref, f32[8,256,256]{2,1,0:T(8,128)S(1)} %get-tuple-element.21.mixed_ref, f32[8,256,128]{2,1,0:T(8,128)S(1)} %get-tuple-element.22.top_ref, ...), custom_call_target="tpu_custom_call" | custom-call | flops 536870912 | bytes 2000000 | tf_op jit(solution)/shard_map/attention_forward/pallas_call | solution.py:208
  14.9 1.9 %collective-permute-start.2 = (bf16[1024,256]{1,0:T(8,128)(2,1)S(1)}, bf16[1024,256]{1,0:T(8,128)(2,1)S(1)}, u32[]{:S(2)}, u32[]{:S(2)}) collective-permute-start(bf16[1024,256]{1,0:T(8,128)(2,1)S(1)} %get-tuple-element.23.out_t_ref), channel_id=1, source_target_pairs={{0,8},{8,0},{16,24},{24,16},{32,40},{40,32},{48,56},{56,48},{64,72... | collective-permute-start | bytes 1572872 | tf_op jit(solution)/shard_map/ppermute | solution.py:316
  16.8 1.9 %collective-permute-done.2 = bf16[1024,256]{1,0:T(8,128)(2,1)S(1)} collective-permute-done((bf16[1024,256]{1,0:T(8,128)(2,1)S(1)}, bf16[1024,256]{1,0:T(8,128)(2,1)S(1)}, u32[]{:S(2)}, u32[]{:S(2)}) %collective-permute-start.2) | collective-permute-done | bytes 524320 | tf_op jit(solution)/shard_map/ppermute | solution.py:316
  18.7 0.0 copy-start.2
  18.7 1.7 %gram_part.1 = bf16[8,4,16,1024]{3,2,1,0:T(8,128)(2,1)} custom-call(f32[8,128]{1,0:T(8,128)S(1)} %get-tuple-element.19.facts_ref, bf16[8,4,2,16,256]{4,3,2,1,0:T(8,128)(2,1)S(1)} %bitcast.13, bf16[8,4,2,16,256]{4,3,2,1,0:T(8,128)(2,1)S(1)} %bitcast.14), custom_call_target="tpu_custom_call" | custom-call | flops 536870912 | bytes 2000000 | tf_op jit(solution)/shard_map/gram_part/pallas_call | solution.py:258
  20.4 15.1 %all-to-all-start = ((bf16[8,4,16,1024]{3,2,1,0:T(8,128)(2,1)}), bf16[8,4,16,1024]{3,2,1,0:T(8,128)(2,1)S(1)}, u32[]{:S(2)}, u32[]{:S(2)}) async-start(bf16[8,4,16,1024]{3,2,1,0:T(8,128)(2,1)} %gram_part.1), calls=%async_computation | async-start | bytes 2097152 | tf_op jit(solution)/shard_map/all_to_all | solution.py:329
  35.5 0.0 copy-done.2
  35.5 4.4 %away_gradients.1 = (bf16[2,256,128]{2,1,0:T(8,128)(2,1)S(1)}, bf16[2,256,128]{2,1,0:T(8,128)(2,1)S(1)}, bf16[256,1024]{1,0:T(8,128)(2,1)}, bf16[8,2,256,256]{3,2,1,0:T(8,128)(2,1)S(1)}, f32[8,256]{1,0:T(8,128)S(1)}) custom-call(f32[8,128]{1,0:T(8,128)S(1)} %get-tuple-element.19.facts_ref, bf16[256,1024]{1,0:T(8,128)(2,1)S(1)} %get-tuple-element.20.q_ref, ...), custom_call_target="tpu_custom_call" | custom-call | flops 1073741824 | bytes 3000000 | tf_op jit(solution)/shard_map/away_gradients/pallas_call | solution.py:224
  39.9 0.0 copy-start
  39.9 1.3 %copy-done = bf16[8,2,256,256]{3,2,1,0:T(8,128)(2,1)} copy-done((bf16[8,2,256,256]{3,2,1,0:T(8,128)(2,1)}, bf16[8,2,256,256]{3,2,1,0:T(8,128)(2,1)S(1)}, u32[]{:S(2)}) %copy-start) | copy-done | bytes 2097176
  41.2 1.9 %collective-permute-start.3 = (bf16[2,256,128]{2,1,0:T(8,128)(2,1)S(1)}, bf16[2,256,128]{2,1,0:T(8,128)(2,1)S(1)}, u32[]{:S(2)}, u32[]{:S(2)}) collective-permute-start(bf16[2,256,128]{2,1,0:T(8,128)(2,1)S(1)} %get-tuple-element.32), channel_id=1, source_target_pairs={{0,504},{8,0},{16,8},{24,16},{32,24},{40,32},{48,40},{56,48},{64,5... | collective-permute-start | bytes 393224 | tf_op jit(solution)/shard_map/ppermute | solution.py:301
  43.1 5.4 %collective-permute-start.4 = (bf16[2,256,128]{2,1,0:T(8,128)(2,1)S(1)}, bf16[2,256,128]{2,1,0:T(8,128)(2,1)S(1)}, u32[]{:S(2)}, u32[]{:S(2)}) collective-permute-start(bf16[2,256,128]{2,1,0:T(8,128)(2,1)S(1)} %get-tuple-element.33), channel_id=1, source_target_pairs={{0,496},{8,504},{16,0},{24,8},{32,16},{40,24},{48,32},{56,40},{64,... | collective-permute-start | bytes 393224 | tf_op jit(solution)/shard_map/ppermute | solution.py:301
  48.5 1.8 %all-to-all-done.part_ref = bf16[8,4,16,1024]{3,2,1,0:T(8,128)(2,1)S(1)} async-done(((bf16[8,4,16,1024]{3,2,1,0:T(8,128)(2,1)}), bf16[8,4,16,1024]{3,2,1,0:T(8,128)(2,1)S(1)}, u32[]{:S(2)}, u32[]{:S(2)}) %all-to-all-start) | async-done | bytes 1048608 | tf_op jit(solution)/shard_map/all_to_all | solution.py:329
  50.3 0.8 %row_sum.1.after_ref = bf16[4,16,1024]{2,1,0:T(8,128)(2,1)} custom-call(bf16[8,4,16,1024]{3,2,1,0:T(8,128)(2,1)S(1)} %all-to-all-done.part_ref), custom_call_target="tpu_custom_call" | custom-call | flops 524288 | bytes 1048576 | tf_op jit(solution)/shard_map/row_sum/pallas_call | solution.py:272
  51.0 3.3 %all-to-all-start.1 = ((bf16[4,16,1024]{2,1,0:T(8,128)(2,1)}), bf16[4,16,1024]{2,1,0:T(8,128)(2,1)S(1)}, u32[]{:S(2)}, u32[]{:S(2)}) async-start(bf16[4,16,1024]{2,1,0:T(8,128)(2,1)} %row_sum.1.after_ref), calls=%async_computation.1 | async-start | bytes 262144 | tf_op jit(solution)/shard_map/all_to_all | solution.py:335
  54.4 0.0 copy-start.1
  54.4 1.6 %copy-done.1 = bf16[8,2,256,256]{3,2,1,0:T(8,128)(2,1)S(1)} copy-done((bf16[8,2,256,256]{3,2,1,0:T(8,128)(2,1)S(1)}, bf16[8,2,256,256]{3,2,1,0:T(8,128)(2,1)}, u32[]{:S(2)}) %copy-start.1) | copy-done | bytes 2097176
  56.0 3.6 %attention_backward.1 = (bf16[256,1024]{1,0:T(8,128)(2,1)}, f32[2,256,128]{2,1,0:T(8,128)S(1)}) custom-call(bf16[256,1024]{1,0:T(8,128)(2,1)S(1)} %get-tuple-element.20.q_ref, bf16[256,1024]{1,0:T(8,128)(2,1)S(1)} %copy-done.2, f32[8,256]{1,0:T(8,128)S(1)} %get-tuple-element.25.lse_ref, f32[8,256]{1,0:T(8,128)S(1)} %get-tuple-element.27.row_dot_ref, ...), custom_call_target="tpu_custom_call" | custom-call | flops 939524096 | bytes 3000000 | tf_op jit(solution)/shard_map/attention_backward/pallas_call | solution.py:242
  59.5 0.0 collective-permute-done.3.back1_ref
  59.5 0.0 collective-permute-done.4.back2_ref
  59.5 0.7 %key_value_sum.1 = bf16[2,256,128]{2,1,0:T(8,128)(2,1)} custom-call(f32[2,256,128]{2,1,0:T(8,128)S(1)} %get-tuple-element.31.kept_ref, bf16[2,256,128]{2,1,0:T(8,128)(2,1)S(1)} %collective-permute-done.3.back1_ref, bf16[2,256,128]{2,1,0:T(8,128)(2,1)S(1)} %collective-permute-done.4.back2_ref), custom_call_target="tpu_custom_call" | custom-call | flops 20000000000 | bytes 50000000 | tf_op jit(solution)/shard_map/key_value_sum/pallas_call | solution.py:284
  60.2 5.8 %all-to-all-done.1 = bf16[4,16,1024]{2,1,0:T(8,128)(2,1)S(1)} async-done(((bf16[4,16,1024]{2,1,0:T(8,128)(2,1)}), bf16[4,16,1024]{2,1,0:T(8,128)(2,1)S(1)}, u32[]{:S(2)}, u32[]{:S(2)}) %all-to-all-start.1) | async-done | bytes 131104 | tf_op jit(solution)/shard_map/all_to_all | solution.py:335
  66.0 0.6 multiply_bitcast_fusion
  (1 shorter events, 0.0 us)
Async XLA Ops:
  1.5 11.2 %collective-permute-start.1 = (bf16[512,128]{1,0:T(8,128)(2,1)S(1)}, bf16[512,128]{1,0:T(8,128)(2,1)S(1)}, u32[]{:S(2)}, u32[]{:S(2)}) collective-permute-start(bf16[512,128]{1,0:T(8,128)(2,1)S(1)} %bitcast.9), channel_id=1, source_target_pairs={{0,16},{8,24},{16,32},{24,40},{32,48},{40,56},{48,64},{56,72},{64,... | collective-permute-start | bytes 393224 | tf_op jit(solution)/shard_map/ppermute | solution.py:301
  5.0 7.7 %collective-permute-start = (bf16[512,128]{1,0:T(8,128)(2,1)S(1)}, bf16[512,128]{1,0:T(8,128)(2,1)S(1)}, u32[]{:S(2)}, u32[]{:S(2)}) collective-permute-start(bf16[512,128]{1,0:T(8,128)(2,1)S(1)} %bitcast.10), channel_id=1, source_target_pairs={{0,8},{8,16},{16,24},{24,32},{32,40},{40,48},{48,56},{56,64},{64,7... | collective-permute-start | bytes 393224 | tf_op jit(solution)/shard_map/ppermute | solution.py:301
  7.0 1.0 %copy-start.3 = (bf16[256,1024]{1,0:T(8,128)(2,1)S(1)}, bf16[256,1024]{1,0:T(8,128)(2,1)}, u32[]{:S(2)}) copy-start(bf16[256,1024]{1,0:T(8,128)(2,1)} %q_ref.1) | copy-start | bytes 1572868
  8.1 0.7 copy-start.4
  14.9 3.8 %collective-permute-start.2 = (bf16[1024,256]{1,0:T(8,128)(2,1)S(1)}, bf16[1024,256]{1,0:T(8,128)(2,1)S(1)}, u32[]{:S(2)}, u32[]{:S(2)}) collective-permute-start(bf16[1024,256]{1,0:T(8,128)(2,1)S(1)} %get-tuple-element.23.out_t_ref), channel_id=1, source_target_pairs={{0,8},{8,0},{16,24},{24,16},{32,40},{40,32},{48,56},{56,48},{64,72... | collective-permute-start | bytes 1572872 | tf_op jit(solution)/shard_map/ppermute | solution.py:316
  18.7 16.8 %copy-start.2 = (bf16[256,1024]{1,0:T(8,128)(2,1)S(1)}, bf16[256,1024]{1,0:T(8,128)(2,1)}, u32[]{:S(2)}) copy-start(bf16[256,1024]{1,0:T(8,128)(2,1)} %go_ref.3) | copy-start | bytes 1572868
  20.4 29.9 %all-to-all-start = ((bf16[8,4,16,1024]{3,2,1,0:T(8,128)(2,1)}), bf16[8,4,16,1024]{3,2,1,0:T(8,128)(2,1)S(1)}, u32[]{:S(2)}, u32[]{:S(2)}) async-start(bf16[8,4,16,1024]{3,2,1,0:T(8,128)(2,1)} %gram_part.1), calls=%async_computation | async-start | bytes 2097152 | tf_op jit(solution)/shard_map/all_to_all | solution.py:329
  39.9 1.3 %copy-start = (bf16[8,2,256,256]{3,2,1,0:T(8,128)(2,1)}, bf16[8,2,256,256]{3,2,1,0:T(8,128)(2,1)S(1)}, u32[]{:S(2)}) copy-start(bf16[8,2,256,256]{3,2,1,0:T(8,128)(2,1)S(1)} %get-tuple-element.28.dscore_ref) | copy-start | bytes 6291460
  41.2 18.3 %collective-permute-start.3 = (bf16[2,256,128]{2,1,0:T(8,128)(2,1)S(1)}, bf16[2,256,128]{2,1,0:T(8,128)(2,1)S(1)}, u32[]{:S(2)}, u32[]{:S(2)}) collective-permute-start(bf16[2,256,128]{2,1,0:T(8,128)(2,1)S(1)} %get-tuple-element.32), channel_id=1, source_target_pairs={{0,504},{8,0},{16,8},{24,16},{32,24},{40,32},{48,40},{56,48},{64,5... | collective-permute-start | bytes 393224 | tf_op jit(solution)/shard_map/ppermute | solution.py:301
  43.1 16.4 %collective-permute-start.4 = (bf16[2,256,128]{2,1,0:T(8,128)(2,1)S(1)}, bf16[2,256,128]{2,1,0:T(8,128)(2,1)S(1)}, u32[]{:S(2)}, u32[]{:S(2)}) collective-permute-start(bf16[2,256,128]{2,1,0:T(8,128)(2,1)S(1)} %get-tuple-element.33), channel_id=1, source_target_pairs={{0,496},{8,504},{16,0},{24,8},{32,16},{40,24},{48,32},{56,40},{64,... | collective-permute-start | bytes 393224 | tf_op jit(solution)/shard_map/ppermute | solution.py:301
  51.0 15.0 %all-to-all-start.1 = ((bf16[4,16,1024]{2,1,0:T(8,128)(2,1)}), bf16[4,16,1024]{2,1,0:T(8,128)(2,1)S(1)}, u32[]{:S(2)}, u32[]{:S(2)}) async-start(bf16[4,16,1024]{2,1,0:T(8,128)(2,1)} %row_sum.1.after_ref), calls=%async_computation.1 | async-start | bytes 262144 | tf_op jit(solution)/shard_map/all_to_all | solution.py:335
  54.4 1.6 %copy-start.1 = (bf16[8,2,256,256]{3,2,1,0:T(8,128)(2,1)S(1)}, bf16[8,2,256,256]{3,2,1,0:T(8,128)(2,1)}, u32[]{:S(2)}) copy-start(bf16[8,2,256,256]{3,2,1,0:T(8,128)(2,1)} %copy-done) | copy-start | bytes 6291460

commit v4 on v3

--- a/solution.py
+++ b/solution.py
@@ -143,18 +143,18 @@
             kept_ref[1] = dv
 
 
-def gram_kernel(facts_ref, mine_ref, other_ref, part_hbm, part_ref, sems):
+def gram_kernel(facts_ref, both_ref, part_hbm, part_ref, sems):
     core = facts_ref[2:3, :1].astype(jnp.bfloat16)
-    planes, rows, cores, unit, tok = mine_ref.shape
+    _, planes, rows, cores, unit, tok = both_ref.shape
     chunks = part_ref.shape[0]
     step = planes // chunks
     wide = step * rows * cores * unit
-    picked = [ref[:, :, 0] * (1 - core) + ref[:, :, 1] * core for ref in (mine_ref, other_ref)]
+    picked = [both_ref[i, :, :, 0] * (1 - core) + both_ref[i, :, :, 1] * core for i in range(2)]
     left = jnp.concatenate([block.reshape(planes * rows * unit, tok) for block in picked], axis=1)
     saves = []
     for i in range(chunks):
         right = jnp.concatenate(
-            [ref[i * step:(i + 1) * step].reshape(wide, tok) for ref in (mine_ref, other_ref)], axis=1
+            [both_ref[j, i * step:(i + 1) * step].reshape(wide, tok) for j in range(2)], axis=1
         )
         got = dot(left, right, NT).astype(jnp.bfloat16)
         for plane in range(planes):
@@ -251,21 +251,21 @@
     )(q, go, lse, row_dot, dscore, kv0, kv1, kv2, after)
 
 
-def gram_part(facts, mine, other):
-    planes, rows, cores, unit, tok = mine.shape
+def gram_part(facts, both):
+    _, planes, rows, cores, unit, tok = both.shape
     feats = planes * rows * cores * unit
-    chunks = 4
+    chunks = 2
     return pl.pallas_call(
         gram_kernel,
         out_shape=jax.ShapeDtypeStruct((2 * rows, planes // 2, unit, feats), jnp.bfloat16),
-        in_specs=[VMEM] * 3,
+        in_specs=[VMEM] * 2,
         out_specs=HBM,
         scratch_shapes=[pltpu.VMEM((chunks, 2 * rows, planes // 2, unit, feats // chunks), jnp.bfloat16),
                         pltpu.SemaphoreType.DMA((chunks,))],
         compiler_params=PARAMS,
         cost_estimate=pl.CostEstimate(flops=2 * feats * feats * tok, bytes_accessed=2000000, transcendentals=0),
         name="gram_part",
-    )(facts, mine, other)
+    )(facts, both)
 
 
 def row_sum(part):
@@ -313,9 +313,9 @@
     kv1 = shifted(kv0, 1)
     q_near, mixed, top, facts = own_block(place, block_order, query, kv0)
     out_t, lse = forward(facts, q_near, mixed, top, kv1, kv2)
-    other_t = lax.ppermute(out_t, "seq", [(i, i ^ 1) for i in range(count)])
-    split = (planes, ROWS, CORES, unit, tok)
-    part = gram_part(facts, out_t.reshape(split), other_t.reshape(split))
+    pairs = [[i, i + 1] for i in range(0, count, CORES)]
+    both = lax.all_gather(out_t, "seq", axis_index_groups=pairs)
+    part = gram_part(facts, both.reshape(CORES, planes, ROWS, CORES, unit, tok))
     seat = lambda z, y, c: (z * ROWS + y) * CORES + c
     near_groups = [
         [seat(2 * half + side, y, c) for side in range(2) for y in range(ROWS)]

time: 67.2 us -> 105 us (1.56)
  the two profiles are of different devices: /device:TPU:8 before, /device:TPU:2 now
where the time goes in v4:
time: 105 us; the launch traced here: 104 us
  waiting for transfers between devices  36.7 us (35%)
  starting transfers between devices  29.4 us (28%)
  Pallas kernels  16.6 us (16%)
  between operations  14.1 us (13%)
  local copies, waits for them, and re-layouts  5.84 us (6%)
  other arithmetic  1.62 us (2%)
    ppermute x4, starting transfers between devices, shifted(): lax.ppermute(block, 'seq', [(i, (i + distance) % count) for i in range(co...  20.7 us
    all_gather x1, waiting for transfers between devices, local(): both = lax.all_gather(out_t, 'seq', axis_index_groups=pairs)  19.5 us
    ppermute x4, waiting for transfers between devices, shifted(): lax.ppermute(block, 'seq', [(i, (i + distance) % count) for i in range(co...  11.8 us
    unnamed x12, local copies, waits for them, and re-layouts  5.84 us
    pallas_call x1, Pallas kernels, away_gradients(): pl.pallas_call(away_kernel, out_shape=(pair, pair, jax.ShapeDtypeStruct((...  5.47 us
    all_to_all x1, waiting for transfers between devices, local(): lax.all_to_all(part, 'seq', 0, 0, axis_index_groups=far_groups, tiled=True)  5.36 us
    all_to_all x1, starting transfers between devices, local(): lax.all_to_all(part, 'seq', 0, 0, axis_index_groups=near_groups, tiled=True)  5.29 us
    pallas_call x1, Pallas kernels, backward(): pl.pallas_call(backward_kernel, out_shape=(full, jax.ShapeDtypeStruct((2,...  3.57 us
  transfers between devices with their start and end apart: 7, of which 4 were waited for; matrix products, arithmetic and copies ran while one was open for 0% of the time, Pallas kernels for 12%

profile of v4, /device:TPU:2, one launch (start us, length us, event | category | flops | bytes accessed | tf_op | source)
XLA Modules:
  0.0 104.2 jit_solution(16319813696431331632)
XLA Ops:
  7.2 0.0 all-gather.3.cloned.1.call-start
  7.2 0.9 pad_maximum_fusion
  8.1 3.5 %collective-permute-start.1 = (bf16[512,128]{1,0:T(8,128)(2,1)S(1)}, bf16[512,128]{1,0:T(8,128)(2,1)S(1)}, u32[]{:S(2)}, u32[]{:S(2)}) collective-permute-start(bf16[512,128]{1,0:T(8,128)(2,1)S(1)} %bitcast.9), channel_id=1, source_target_pairs={{0,16},{8,24},{16,32},{24,40},{32,48},{40,56},{48,64},{56,72},{64,... | collective-permute-start | bytes 393224 | tf_op jit(solution)/shard_map/ppermute | solution.py:301
  11.6 1.9 %collective-permute-start = (bf16[512,128]{1,0:T(8,128)(2,1)S(1)}, bf16[512,128]{1,0:T(8,128)(2,1)S(1)}, u32[]{:S(2)}, u32[]{:S(2)}) collective-permute-start(bf16[512,128]{1,0:T(8,128)(2,1)S(1)} %bitcast.10), channel_id=1, source_target_pairs={{0,8},{8,16},{16,24},{24,32},{32,40},{40,48},{48,56},{56,64},{64,7... | collective-permute-start | bytes 393224 | tf_op jit(solution)/shard_map/ppermute | solution.py:301
  13.5 0.1 pad_add_fusion.place_ref
  13.6 0.0 copy-start.4
  13.6 1.0 copy-done.4
  14.6 0.0 copy-start.5
  14.7 0.7 copy-done.5
  15.3 1.5 %own_block.1 = (bf16[256,1024]{1,0:T(8,128)(2,1)S(1)}, f32[8,256,256]{2,1,0:T(8,128)S(1)}, f32[8,256,128]{2,1,0:T(8,128)S(1)}, f32[8,128]{1,0:T(8,128)S(1)}) custom-call(s32[2]{0:T(128)S(1)} %pad_add_fusion.place_ref, s32[64]{0:T(128)S(1)} %copy-done.5, bf16[256,1024]{1,0:T(8,128)(2,1)S(1)} %copy-done.4, bf16[512,128]{1,0:T(8,128)(2,1)S(1)} %bitcast.11), custom_call_target="tpu_custom_call" | custom-call | flops 268435456 | bytes 6000000 | tf_op jit(solution)/shard_map/own_block/pallas_call | solution.py:193
  16.8 11.2 %collective-permute-done.1.kv2_ref = bf16[512,128]{1,0:T(8,128)(2,1)S(1)} collective-permute-done((bf16[512,128]{1,0:T(8,128)(2,1)S(1)}, bf16[512,128]{1,0:T(8,128)(2,1)S(1)}, u32[]{:S(2)}, u32[]{:S(2)}) %collective-permute-start.1) | collective-permute-done | bytes 131104 | tf_op jit(solution)/shard_map/ppermute | solution.py:301
  28.0 0.6 collective-permute-done.kv1_ref
  28.6 3.0 %attention_forward.1 = (bf16[1024,256]{1,0:T(8,128)(2,1)}, f32[8,256]{1,0:T(8,128)S(1)}) custom-call(f32[8,128]{1,0:T(8,128)S(1)} %get-tuple-element.19.facts_ref, bf16[256,1024]{1,0:T(8,128)(2,1)S(1)} %get-tuple-element.20.q_ref, f32[8,256,256]{2,1,0:T(8,128)S(1)} %get-tuple-element.21.mixed_ref, f32[8,256,128]{2,1,0:T(8,128)S(1)} %get-tuple-element.22.top_ref, ...), custom_call_target="tpu_custom_call" | custom-call | flops 536870912 | bytes 2000000 | tf_op jit(solution)/shard_map/attention_forward/pallas_call | solution.py:208
  31.6 0.0 all-gather.3.cloned.1.call-update
  31.6 19.5 %all-gather.3.cloned.1.call-done = bf16[2048,256]{1,0:T(8,128)(2,1)} async-done(((bf16[1024,256]{1,0:T(8,128)(2,1)}), bf16[2048,256]{1,0:T(8,128)(2,1)}) %all-gather.3.cloned.1.call-update) | async-done | bytes 1048592 | tf_op jit(solution)/shard_map/all_gather | solution.py:317
  51.1 0.0 copy-start.2
  51.1 1.2 %copy-done.2 = bf16[2048,256]{1,0:T(8,128)(2,1)S(1)} copy-done((bf16[2048,256]{1,0:T(8,128)(2,1)S(1)}, bf16[2048,256]{1,0:T(8,128)(2,1)}, u32[]{:S(2)}) %copy-start.2) | copy-done | bytes 1048600
  52.3 0.0 copy-start.3
  52.3 1.6 %gram_part.1 = bf16[8,4,16,1024]{3,2,1,0:T(8,128)(2,1)} custom-call(f32[8,128]{1,0:T(8,128)S(1)} %get-tuple-element.19.facts_ref, bf16[2,8,4,2,16,256]{5,4,3,2,1,0:T(8,128)(2,1)S(1)} %bitcast.8), custom_call_target="tpu_custom_call" | custom-call | flops 536870912 | bytes 2000000 | tf_op jit(solution)/shard_map/gram_part/pallas_call | solution.py:258
  53.9 5.3 %all-to-all-start = ((bf16[8,4,16,1024]{3,2,1,0:T(8,128)(2,1)}), bf16[8,4,16,1024]{3,2,1,0:T(8,128)(2,1)S(1)}, u32[]{:S(2)}, u32[]{:S(2)}) async-start(bf16[8,4,16,1024]{3,2,1,0:T(8,128)(2,1)} %gram_part.1), calls=%async_computation | async-start | bytes 2097152 | tf_op jit(solution)/shard_map/all_to_all | solution.py:329
  59.2 0.0 copy-done.3
  59.2 5.5 %away_gradients.1 = (bf16[2,256,128]{2,1,0:T(8,128)(2,1)S(1)}, bf16[2,256,128]{2,1,0:T(8,128)(2,1)S(1)}, bf16[256,1024]{1,0:T(8,128)(2,1)}, bf16[8,2,256,256]{3,2,1,0:T(8,128)(2,1)S(1)}, f32[8,256]{1,0:T(8,128)S(1)}) custom-call(f32[8,128]{1,0:T(8,128)S(1)} %get-tuple-element.19.facts_ref, bf16[256,1024]{1,0:T(8,128)(2,1)S(1)} %get-tuple-element.20.q_ref, ...), custom_call_target="tpu_custom_call" | custom-call | flops 1073741824 | bytes 3000000 | tf_op jit(solution)/shard_map/away_gradients/pallas_call | solution.py:224
  64.7 0.0 copy-start
  64.7 1.3 %copy-done = bf16[8,2,256,256]{3,2,1,0:T(8,128)(2,1)} copy-done((bf16[8,2,256,256]{3,2,1,0:T(8,128)(2,1)}, bf16[8,2,256,256]{3,2,1,0:T(8,128)(2,1)S(1)}, u32[]{:S(2)}) %copy-start) | copy-done | bytes 2097176
  66.0 12.5 %collective-permute-start.2 = (bf16[2,256,128]{2,1,0:T(8,128)(2,1)S(1)}, bf16[2,256,128]{2,1,0:T(8,128)(2,1)S(1)}, u32[]{:S(2)}, u32[]{:S(2)}) collective-permute-start(bf16[2,256,128]{2,1,0:T(8,128)(2,1)S(1)} %get-tuple-element.32), channel_id=1, source_target_pairs={{0,504},{8,0},{16,8},{24,16},{32,24},{40,32},{48,40},{56,48},{64,5... | collective-permute-start | bytes 393224 | tf_op jit(solution)/shard_map/ppermute | solution.py:301
  78.6 2.8 %collective-permute-start.3 = (bf16[2,256,128]{2,1,0:T(8,128)(2,1)S(1)}, bf16[2,256,128]{2,1,0:T(8,128)(2,1)S(1)}, u32[]{:S(2)}, u32[]{:S(2)}) collective-permute-start(bf16[2,256,128]{2,1,0:T(8,128)(2,1)S(1)} %get-tuple-element.33), channel_id=1, source_target_pairs={{0,496},{8,504},{16,0},{24,8},{32,16},{40,24},{48,32},{56,40},{64,... | collective-permute-start | bytes 393224 | tf_op jit(solution)/shard_map/ppermute | solution.py:301
  81.3 0.0 all-to-all-done.part_ref
  81.4 0.8 row_sum.1.after_ref
  82.1 3.3 %all-to-all-start.1 = ((bf16[4,16,1024]{2,1,0:T(8,128)(2,1)}), bf16[4,16,1024]{2,1,0:T(8,128)(2,1)S(1)}, u32[]{:S(2)}, u32[]{:S(2)}) async-start(bf16[4,16,1024]{2,1,0:T(8,128)(2,1)} %row_sum.1.after_ref), calls=%async_computation.1 | async-start | bytes 262144 | tf_op jit(solution)/shard_map/all_to_all | solution.py:335
  85.5 0.0 copy-start.1
  85.5 1.6 %copy-done.1 = bf16[8,2,256,256]{3,2,1,0:T(8,128)(2,1)S(1)} copy-done((bf16[8,2,256,256]{3,2,1,0:T(8,128)(2,1)S(1)}, bf16[8,2,256,256]{3,2,1,0:T(8,128)(2,1)}, u32[]{:S(2)}) %copy-start.1) | copy-done | bytes 2097176
  87.1 3.6 %attention_backward.1 = (bf16[256,1024]{1,0:T(8,128)(2,1)}, f32[2,256,128]{2,1,0:T(8,128)S(1)}) custom-call(bf16[256,1024]{1,0:T(8,128)(2,1)S(1)} %get-tuple-element.20.q_ref, bf16[256,1024]{1,0:T(8,128)(2,1)S(1)} %copy-done.3, f32[8,256]{1,0:T(8,128)S(1)} %get-tuple-element.25.lse_ref, f32[8,256]{1,0:T(8,128)S(1)} %get-tuple-element.27.row_dot_ref, ...), custom_call_target="tpu_custom_call" | custom-call | flops 939524096 | bytes 3000000 | tf_op jit(solution)/shard_map/attention_backward/pallas_call | solution.py:242
  90.6 0.0 collective-permute-done.2.back1_ref
  90.6 0.0 collective-permute-done.3.back2_ref
  90.6 0.7 key_value_sum.1
  91.3 5.4 %all-to-all-done.1 = bf16[4,16,1024]{2,1,0:T(8,128)(2,1)S(1)} async-done(((bf16[4,16,1024]{2,1,0:T(8,128)(2,1)}), bf16[4,16,1024]{2,1,0:T(8,128)(2,1)S(1)}, u32[]{:S(2)}, u32[]{:S(2)}) %all-to-all-start.1) | async-done | bytes 131104 | tf_op jit(solution)/shard_map/all_to_all | solution.py:335
  96.7 0.6 multiply_bitcast_fusion
  (1 shorter events, 0.0 us)
Async XLA Ops:
  7.2 43.9 %all-gather.3.cloned.1.call-start = ((), (), s32[]{:S(2)}) async-start(), calls=%async_computation.2 | async-start | bytes 1572864 | tf_op jit(solution)/shard_map/all_gather | solution.py:317
  8.1 19.9 %collective-permute-start.1 = (bf16[512,128]{1,0:T(8,128)(2,1)S(1)}, bf16[512,128]{1,0:T(8,128)(2,1)S(1)}, u32[]{:S(2)}, u32[]{:S(2)}) collective-permute-start(bf16[512,128]{1,0:T(8,128)(2,1)S(1)} %bitcast.9), channel_id=1, source_target_pairs={{0,16},{8,24},{16,32},{24,40},{32,48},{40,56},{48,64},{56,72},{64,... | collective-permute-start | bytes 393224 | tf_op jit(solution)/shard_map/ppermute | solution.py:301
  11.6 17.0 %collective-permute-start = (bf16[512,128]{1,0:T(8,128)(2,1)S(1)}, bf16[512,128]{1,0:T(8,128)(2,1)S(1)}, u32[]{:S(2)}, u32[]{:S(2)}) collective-permute-start(bf16[512,128]{1,0:T(8,128)(2,1)S(1)} %bitcast.10), channel_id=1, source_target_pairs={{0,8},{8,16},{16,24},{24,32},{32,40},{40,48},{48,56},{56,64},{64,7... | collective-permute-start | bytes 393224 | tf_op jit(solution)/shard_map/ppermute | solution.py:301
  13.6 1.0 copy-start.4
  14.6 0.7 copy-start.5
  51.1 1.2 %copy-start.2 = (bf16[2048,256]{1,0:T(8,128)(2,1)S(1)}, bf16[2048,256]{1,0:T(8,128)(2,1)}, u32[]{:S(2)}) copy-start(bf16[2048,256]{1,0:T(8,128)(2,1)} %all-gather.3.cloned.1.call-done) | copy-start | bytes 3145732
  52.3 6.9 %copy-start.3 = (bf16[256,1024]{1,0:T(8,128)(2,1)S(1)}, bf16[256,1024]{1,0:T(8,128)(2,1)}, u32[]{:S(2)}) copy-start(bf16[256,1024]{1,0:T(8,128)(2,1)} %go_ref.3) | copy-start | bytes 1572868
  53.9 27.4 %all-to-all-start = ((bf16[8,4,16,1024]{3,2,1,0:T(8,128)(2,1)}), bf16[8,4,16,1024]{3,2,1,0:T(8,128)(2,1)S(1)}, u32[]{:S(2)}, u32[]{:S(2)}) async-start(bf16[8,4,16,1024]{3,2,1,0:T(8,128)(2,1)} %gram_part.1), calls=%async_computation | async-start | bytes 2097152 | tf_op jit(solution)/shard_map/all_to_all | solution.py:329
  64.7 1.3 %copy-start = (bf16[8,2,256,256]{3,2,1,0:T(8,128)(2,1)}, bf16[8,2,256,256]{3,2,1,0:T(8,128)(2,1)S(1)}, u32[]{:S(2)}) copy-start(bf16[8,2,256,256]{3,2,1,0:T(8,128)(2,1)S(1)} %get-tuple-element.28.dscore_ref) | copy-start | bytes 6291460
  66.0 24.6 %collective-permute-start.2 = (bf16[2,256,128]{2,1,0:T(8,128)(2,1)S(1)}, bf16[2,256,128]{2,1,0:T(8,128)(2,1)S(1)}, u32[]{:S(2)}, u32[]{:S(2)}) collective-permute-start(bf16[2,256,128]{2,1,0:T(8,128)(2,1)S(1)} %get-tuple-element.32), channel_id=1, source_target_pairs={{0,504},{8,0},{16,8},{24,16},{32,24},{40,32},{48,40},{56,48},{64,5... | collective-permute-start | bytes 393224 | tf_op jit(solution)/shard_map/ppermute | solution.py:301
  78.6 12.1 %collective-permute-start.3 = (bf16[2,256,128]{2,1,0:T(8,128)(2,1)S(1)}, bf16[2,256,128]{2,1,0:T(8,128)(2,1)S(1)}, u32[]{:S(2)}, u32[]{:S(2)}) collective-permute-start(bf16[2,256,128]{2,1,0:T(8,128)(2,1)S(1)} %get-tuple-element.33), channel_id=1, source_target_pairs={{0,496},{8,504},{16,0},{24,8},{32,16},{40,24},{48,32},{56,40},{64,... | collective-permute-start | bytes 393224 | tf_op jit(solution)/shard_map/ppermute | solution.py:301
  82.1 14.6 %all-to-all-start.1 = ((bf16[4,16,1024]{2,1,0:T(8,128)(2,1)}), bf16[4,16,1024]{2,1,0:T(8,128)(2,1)S(1)}, u32[]{:S(2)}, u32[]{:S(2)}) async-start(bf16[4,16,1024]{2,1,0:T(8,128)(2,1)} %row_sum.1.after_ref), calls=%async_computation.1 | async-start | bytes 262144 | tf_op jit(solution)/shard_map/all_to_all | solution.py:335
  85.5 1.6 %copy-start.1 = (bf16[8,2,256,256]{3,2,1,0:T(8,128)(2,1)S(1)}, bf16[8,2,256,256]{3,2,1,0:T(8,128)(2,1)}, u32[]{:S(2)}) copy-start(bf16[8,2,256,256]{3,2,1,0:T(8,128)(2,1)} %copy-done) | copy-start | bytes 6291460
Sparse Core Ops, SparseCore 0:
  31.7 19.2 all-gather.2

commit v5 on v3

--- a/solution.py
+++ b/solution.py
@@ -48,8 +48,11 @@
         top_ref[h] = jnp.broadcast_to(top, (tok, dim))
 
 
-def forward_kernel(facts_ref, q_ref, mixed_ref, top_ref, kv1_ref, kv2_ref, out_t_ref, lse_ref):
+def forward_kernel(facts_ref, q_ref, mixed_ref, top_ref, pair_ref, even2_ref, out_t_ref, lse_ref, kv1_ref, kv2_ref):
     heads, tok, dim = top_ref.shape
+    core = facts_ref[2:3, :1].astype(jnp.bfloat16)
+    kv1_ref[...] = pair_ref[0] * core + pair_ref[1] * (1 - core)
+    kv2_ref[...] = pair_ref[1] * core + even2_ref[...] * (1 - core)
     unit = math.log2(math.e) / dim**0.5
     hide = [facts_ref[j:j + 1, :] for j in range(2)]
     keys = [kv_ref[:tok, :] for kv_ref in (kv1_ref, kv2_ref)]
@@ -202,18 +205,19 @@
     )(place, order, q, kv0)
 
 
-def forward(facts, q, mixed, top, kv1, kv2):
+def forward(facts, q, mixed, top, pair, even2):
     tok, width = q.shape
     heads = top.shape[0]
     return pl.pallas_call(
         forward_kernel,
-        out_shape=(jax.ShapeDtypeStruct((width, tok), jnp.bfloat16), jax.ShapeDtypeStruct((heads, tok), jnp.float32)),
+        out_shape=(jax.ShapeDtypeStruct((width, tok), jnp.bfloat16), jax.ShapeDtypeStruct((heads, tok), jnp.float32),
+                   jax.ShapeDtypeStruct(even2.shape, even2.dtype), jax.ShapeDtypeStruct(even2.shape, even2.dtype)),
         in_specs=[VMEM] * 6,
-        out_specs=(VMEM,) * 2,
+        out_specs=(VMEM,) * 4,
         compiler_params=PARAMS,
         cost_estimate=pl.CostEstimate(flops=8 * tok * width * tok, bytes_accessed=2000000, transcendentals=0),
         name="attention_forward",
-    )(facts, q, mixed, top, kv1, kv2)
+    )(facts, q, mixed, top, pair, even2)
 
 
 def away_gradients(facts, q, go, out_t, lse, kv1, kv2):
@@ -296,9 +300,9 @@
 ROWS = 4
 
 
-def shifted(block, distance):
+def shifted(block, distance, cores=range(CORES)):
     count = lax.axis_size("seq")
-    return lax.ppermute(block, "seq", [(i, (i + distance) % count) for i in range(count)])
+    return lax.ppermute(block, "seq", [(i, (i + distance) % count) for i in range(count) if i % CORES in cores])
 
 
 def local(query, key_in, value_input, output_gradient, block_order):
@@ -309,10 +313,13 @@
     me = lax.axis_index("seq").astype(jnp.int32)
     place = jnp.stack([me, me % CORES])
     kv0 = jnp.stack([key_in, value_input]).reshape(2 * tok, -1)
-    kv2 = shifted(kv0, 2)
-    kv1 = shifted(kv0, 1)
+    odd2 = shifted(kv0, 2, (1,))
+    even2 = shifted(kv0, 2, (0,))
     q_near, mixed, top, facts = own_block(place, block_order, query, kv0)
-    out_t, lse = forward(facts, q_near, mixed, top, kv1, kv2)
+    core = me % CORES
+    pairs = [[i, i + 1] for i in range(0, count, CORES)]
+    pair = lax.all_gather(jnp.where(core == 0, kv0, odd2), "seq", axis_index_groups=pairs)
+    out_t, lse, kv1, kv2 = forward(facts, q_near, mixed, top, pair, even2)
     other_t = lax.ppermute(out_t, "seq", [(i, i ^ 1) for i in range(count)])
     split = (planes, ROWS, CORES, unit, tok)
     part = gram_part(facts, out_t.reshape(split), other_t.reshape(split))
@@ -328,8 +335,11 @@
     part, lse = lax.optimization_barrier((part, lse))
     part = lax.all_to_all(part, "seq", 0, 0, axis_index_groups=near_groups, tiled=True)
     away1, away2, out, dscore, row_dot = away_gradients(facts, q_near, output_gradient, out_t, lse, kv1, kv2)
-    back2 = shifted(away2, -2)
-    back1 = shifted(away1, -1)
+    pair = lax.all_gather(away1, "seq", axis_index_groups=pairs)
+    other = jnp.where(core == 0, pair[1], pair[0])
+    sent = jnp.where(core == 0, away2, away2 + other)
+    back1 = jnp.where(core == 0, other, jnp.zeros_like(other))
+    back2 = shifted(sent, -2)
     part = row_sum(part)
     d_query, kept = backward(q_near, output_gradient, lse, row_dot, dscore, kv0, kv1, kv2, part)
     part = lax.all_to_all(part, "seq", 0, 0, axis_index_groups=far_groups, tiled=True)

time: 67.2 us -> 66.9 us (level)
  the two profiles are of different devices: /device:TPU:8 before, /device:TPU:6 now
where the time goes in v5:
time: 66.9 us; the launch traced here: 66.4 us
  starting transfers between devices  18.8 us (28%)
  blocking collectives  15.9 us (24%)
  Pallas kernels  14.9 us (22%)
  waiting for transfers between devices  9.86 us (15%)
  local copies, waits for them, and re-layouts  4.61 us (7%)
  other arithmetic  1.67 us (2%)
  between operations  0.78 us (1%)
    all_gather x1, blocking collectives, local(): lax.all_gather(jnp.where(core == 0, kv0, odd2), 'seq', axis_index_groups=...  13.9 us
    ppermute x3, starting transfers between devices, shifted(): lax.ppermute(block, 'seq', [(i, (i + distance) % count) for i in range(co...  9.61 us
    all_to_all x1, waiting for transfers between devices, local(): lax.all_to_all(part, 'seq', 0, 0, axis_index_groups=far_groups, tiled=True)  6.08 us
    unnamed x10, local copies, waits for them, and re-layouts  4.61 us
    pallas_call x1, Pallas kernels, away_gradients(): pl.pallas_call(away_kernel, out_shape=(pair, pair, jax.ShapeDtypeStruct((...  4.44 us
    pallas_call x1, Pallas kernels, backward(): pl.pallas_call(backward_kernel, out_shape=(full, jax.ShapeDtypeStruct((2,...  3.57 us
    all_to_all x1, starting transfers between devices, local(): lax.all_to_all(part, 'seq', 0, 0, axis_index_groups=near_groups, tiled=True)  3.57 us
    all_to_all x1, starting transfers between devices, local(): lax.all_to_all(part, 'seq', 0, 0, axis_index_groups=far_groups, tiled=True)  3.32 us
  transfers between devices with their start and end apart: 6, of which 3 were waited for; matrix products, arithmetic and copies ran while one was open for 0% of the time, Pallas kernels for 17%

profile of v5, /device:TPU:6, one launch (start us, length us, event | category | flops | bytes accessed | tf_op | source)
XLA Modules:
  0.0 66.4 jit_solution(5339981998612834900)
XLA Ops:
  0.6 0.9 %pad_maximum_fusion = bf16[2,256,128]{2,1,0:T(8,128)(2,1)S(1)} fusion(bf16[1,256,128]{2,1,0:T(8,128)(2,1)} %bitcast.18, bf16[1,256,128]{2,1,0:T(8,128)(2,1)} %bitcast.19), kind=kLoop, calls=%fused_computation.3 | loop fusion | flops 65536 | bytes 262144 | tf_op jit(solution)/shard_map/stack | solution.py:315
  1.5 3.5 %collective-permute-start.1 = (bf16[512,128]{1,0:T(8,128)(2,1)S(1)}, bf16[512,128]{1,0:T(8,128)(2,1)S(1)}, u32[]{:S(2)}, u32[]{:S(2)}) collective-permute-start(bf16[512,128]{1,0:T(8,128)(2,1)S(1)} %bitcast.11), channel_id=1, source_target_pairs={{0,16},{16,32},{32,48},{48,64},{64,80},{80,96},{96,112},{112,128},... | collective-permute-start | bytes 393224 | tf_op jit(solution)/shard_map/ppermute | solution.py:305
  5.0 0.7 %collective-permute-start = (bf16[512,128]{1,0:T(8,128)(2,1)S(1)}, bf16[512,128]{1,0:T(8,128)(2,1)S(1)}, u32[]{:S(2)}, u32[]{:S(2)}) collective-permute-start(bf16[512,128]{1,0:T(8,128)(2,1)S(1)} %bitcast.12), channel_id=1, source_target_pairs={{8,24},{24,40},{40,56},{56,72},{72,88},{88,104},{104,120},{120,136... | collective-permute-start | bytes 393224 | tf_op jit(solution)/shard_map/ppermute | solution.py:305
  5.7 0.1 pad_add_fusion.place_ref
  5.8 0.0 copy-start.3
  5.8 1.0 %copy-done.3 = bf16[256,1024]{1,0:T(8,128)(2,1)S(1)} copy-done((bf16[256,1024]{1,0:T(8,128)(2,1)S(1)}, bf16[256,1024]{1,0:T(8,128)(2,1)}, u32[]{:S(2)}) %copy-start.3) | copy-done | bytes 524312
  6.8 0.0 copy-start.4
  6.8 0.7 copy-done.4
  7.5 1.5 %own_block.1 = (bf16[256,1024]{1,0:T(8,128)(2,1)S(1)}, f32[8,256,256]{2,1,0:T(8,128)S(1)}, f32[8,256,128]{2,1,0:T(8,128)S(1)}, f32[8,128]{1,0:T(8,128)S(1)}) custom-call(s32[2]{0:T(128)S(1)} %pad_add_fusion.place_ref, s32[64]{0:T(128)S(1)} %copy-done.4, bf16[256,1024]{1,0:T(8,128)(2,1)S(1)} %copy-done.3, bf16[512,128]{1,0:T(8,128)(2,1)S(1)} %bitcast.13), custom_call_target="tpu_custom_call" | custom-call | flops 268435456 | bytes 6000000 | tf_op jit(solution)/shard_map/own_block/pallas_call | solution.py:196
  9.0 0.0 collective-permute-done
  9.0 13.9 %all-gather = bf16[1024,128]{1,0:T(8,128)(2,1)S(1)} all-gather(bf16[512,128]{1,0:T(8,128)(2,1)S(1)} %broadcast_select_fusion.1), channel_id=2, replica_groups={{0,8},{16,24},{32,40},{48,56},{64,72},{80,88},{96,104},{112,120},{128,1..., dimensions={0}, use_global_device_ids=true | all-gather | bytes 393216 | tf_op jit(solution)/shard_map/all_gather | solution.py:321
  22.9 0.0 collective-permute-done.1.even2_ref
  22.9 2.2 %attention_forward.1 = (bf16[1024,256]{1,0:T(8,128)(2,1)S(1)}, f32[8,256]{1,0:T(8,128)S(1)}, bf16[512,128]{1,0:T(8,128)(2,1)S(1)}, bf16[512,128]{1,0:T(8,128)(2,1)S(1)}) custom-call(f32[8,128]{1,0:T(8,128)S(1)} %get-tuple-element.21.facts_ref, bf16[256,1024]{1,0:T(8,128)(2,1)S(1)} %get-tuple-element.22.q_ref, ...), custom_call_target="tpu_custom_call" | custom-call | flops 536870912 | bytes 2000000 | tf_op jit(solution)/shard_map/attention_forward/pallas_call | solution.py:211
  25.1 2.3 %collective-permute-start.2 = (bf16[1024,256]{1,0:T(8,128)(2,1)S(1)}, bf16[1024,256]{1,0:T(8,128)(2,1)S(1)}, u32[]{:S(2)}, u32[]{:S(2)}) collective-permute-start(bf16[1024,256]{1,0:T(8,128)(2,1)S(1)} %get-tuple-element.25.out_t_ref), channel_id=1, source_target_pairs={{0,8},{8,0},{16,24},{24,16},{32,40},{40,32},{48,56},{56,48},{64,72... | collective-permute-start | bytes 1572872 | tf_op jit(solution)/shard_map/ppermute | solution.py:323
  27.4 1.5 %collective-permute-done.2 = bf16[1024,256]{1,0:T(8,128)(2,1)S(1)} collective-permute-done((bf16[1024,256]{1,0:T(8,128)(2,1)S(1)}, bf16[1024,256]{1,0:T(8,128)(2,1)S(1)}, u32[]{:S(2)}, u32[]{:S(2)}) %collective-permute-start.2) | collective-permute-done | bytes 524320 | tf_op jit(solution)/shard_map/ppermute | solution.py:323
  28.9 0.0 copy-start.2
  28.9 1.7 %gram_part.1 = bf16[8,4,16,1024]{3,2,1,0:T(8,128)(2,1)} custom-call(f32[8,128]{1,0:T(8,128)S(1)} %get-tuple-element.21.facts_ref, bf16[8,4,2,16,256]{4,3,2,1,0:T(8,128)(2,1)S(1)} %bitcast.16, bf16[8,4,2,16,256]{4,3,2,1,0:T(8,128)(2,1)S(1)} %bitcast.17), custom_call_target="tpu_custom_call" | custom-call | flops 536870912 | bytes 2000000 | tf_op jit(solution)/shard_map/gram_part/pallas_call | solution.py:262
  30.6 3.6 %all-to-all-start = ((bf16[8,4,16,1024]{3,2,1,0:T(8,128)(2,1)}), bf16[8,4,16,1024]{3,2,1,0:T(8,128)(2,1)S(1)}, u32[]{:S(2)}, u32[]{:S(2)}) async-start(bf16[8,4,16,1024]{3,2,1,0:T(8,128)(2,1)} %gram_part.1), calls=%async_computation | async-start | bytes 2097152 | tf_op jit(solution)/shard_map/all_to_all | solution.py:336
  34.2 0.0 copy-done.2
  34.2 4.4 %away_gradients.1 = (bf16[2,256,128]{2,1,0:T(8,128)(2,1)S(1)}, bf16[2,256,128]{2,1,0:T(8,128)(2,1)S(1)}, bf16[256,1024]{1,0:T(8,128)(2,1)}, bf16[8,2,256,256]{3,2,1,0:T(8,128)(2,1)S(1)}, f32[8,256]{1,0:T(8,128)S(1)}) custom-call(f32[8,128]{1,0:T(8,128)S(1)} %get-tuple-element.21.facts_ref, bf16[256,1024]{1,0:T(8,128)(2,1)S(1)} %get-tuple-element.22.q_ref, ...), custom_call_target="tpu_custom_call" | custom-call | flops 1073741824 | bytes 3000000 | tf_op jit(solution)/shard_map/away_gradients/pallas_call | solution.py:228
  38.7 0.0 copy-start
  38.7 1.3 %copy-done = bf16[8,2,256,256]{3,2,1,0:T(8,128)(2,1)} copy-done((bf16[8,2,256,256]{3,2,1,0:T(8,128)(2,1)}, bf16[8,2,256,256]{3,2,1,0:T(8,128)(2,1)S(1)}, u32[]{:S(2)}) %copy-start) | copy-done | bytes 2097176
  40.0 2.0 %all-gather.1 = bf16[4,256,128]{2,1,0:T(8,128)(2,1)S(1)} all-gather(bf16[2,256,128]{2,1,0:T(8,128)(2,1)S(1)} %get-tuple-element.36), channel_id=3, replica_groups={{0,8},{16,24},{32,40},{48,56},{64,72},{80,88},{96,104},{112,120},{128,1..., dimensions={0}, use_global_device_ids=true | all-gather | bytes 393216 | tf_op jit(solution)/shard_map/all_gather | solution.py:338
  42.0 5.5 %collective-permute-start.3 = (bf16[2,256,128]{2,1,0:T(8,128)(2,1)S(1)}, bf16[2,256,128]{2,1,0:T(8,128)(2,1)S(1)}, u32[]{:S(2)}, u32[]{:S(2)}) collective-permute-start(bf16[2,256,128]{2,1,0:T(8,128)(2,1)S(1)} %get-tuple-element.38), channel_id=1, source_target_pairs={{0,496},{8,504},{16,0},{24,8},{32,16},{40,24},{48,32},{56,40},{64,... | collective-permute-start | bytes 393224 | tf_op jit(solution)/shard_map/ppermute | solution.py:305
  47.5 2.2 %all-to-all-done.part_ref = bf16[8,4,16,1024]{3,2,1,0:T(8,128)(2,1)S(1)} async-done(((bf16[8,4,16,1024]{3,2,1,0:T(8,128)(2,1)}), bf16[8,4,16,1024]{3,2,1,0:T(8,128)(2,1)S(1)}, u32[]{:S(2)}, u32[]{:S(2)}) %all-to-all-start) | async-done | bytes 1048608 | tf_op jit(solution)/shard_map/all_to_all | solution.py:336
  49.7 0.8 %row_sum.1.after_ref = bf16[4,16,1024]{2,1,0:T(8,128)(2,1)} custom-call(bf16[8,4,16,1024]{3,2,1,0:T(8,128)(2,1)S(1)} %all-to-all-done.part_ref), custom_call_target="tpu_custom_call" | custom-call | flops 524288 | bytes 1048576 | tf_op jit(solution)/shard_map/row_sum/pallas_call | solution.py:276
  50.5 3.3 %all-to-all-start.1 = ((bf16[4,16,1024]{2,1,0:T(8,128)(2,1)}), bf16[4,16,1024]{2,1,0:T(8,128)(2,1)S(1)}, u32[]{:S(2)}, u32[]{:S(2)}) async-start(bf16[4,16,1024]{2,1,0:T(8,128)(2,1)} %row_sum.1.after_ref), calls=%async_computation.1 | async-start | bytes 262144 | tf_op jit(solution)/shard_map/all_to_all | solution.py:345
  53.8 0.0 copy-start.1
  53.9 1.6 %copy-done.1 = bf16[8,2,256,256]{3,2,1,0:T(8,128)(2,1)S(1)} copy-done((bf16[8,2,256,256]{3,2,1,0:T(8,128)(2,1)S(1)}, bf16[8,2,256,256]{3,2,1,0:T(8,128)(2,1)}, u32[]{:S(2)}) %copy-start.1) | copy-done | bytes 2097176
  55.4 3.6 %attention_backward.1 = (bf16[256,1024]{1,0:T(8,128)(2,1)}, f32[2,256,128]{2,1,0:T(8,128)S(1)}) custom-call(bf16[256,1024]{1,0:T(8,128)(2,1)S(1)} %get-tuple-element.22.q_ref, bf16[256,1024]{1,0:T(8,128)(2,1)S(1)} %copy-done.2, f32[8,256]{1,0:T(8,128)S(1)} %get-tuple-element.27.lse_ref, f32[8,256]{1,0:T(8,128)S(1)} %get-tuple-element.31.row_dot_ref, ...), custom_call_target="tpu_custom_call" | custom-call | flops 939524096 | bytes 3000000 | tf_op jit(solution)/shard_map/attention_backward/pallas_call | solution.py:246
  59.0 0.0 collective-permute-done.3.back2_ref
  59.0 0.7 %key_value_sum.1 = bf16[2,256,128]{2,1,0:T(8,128)(2,1)} custom-call(f32[2,256,128]{2,1,0:T(8,128)S(1)} %get-tuple-element.35.kept_ref, bf16[2,256,128]{2,1,0:T(8,128)(2,1)S(1)} %get-tuple-element.39.back1_ref, bf16[2,256,128]{2,1,0:T(8,128)(2,1)S(1)} %collective-permute-done.3.back2_ref), custom_call_target="tpu_custom_call" | custom-call | flops 20000000000 | bytes 50000000 | tf_op jit(solution)/shard_map/key_value_sum/pallas_call | solution.py:288
  59.7 6.1 %all-to-all-done.1 = bf16[4,16,1024]{2,1,0:T(8,128)(2,1)S(1)} async-done(((bf16[4,16,1024]{2,1,0:T(8,128)(2,1)}), bf16[4,16,1024]{2,1,0:T(8,128)(2,1)S(1)}, u32[]{:S(2)}, u32[]{:S(2)}) %all-to-all-start.1) | async-done | bytes 131104 | tf_op jit(solution)/shard_map/all_to_all | solution.py:345
  65.8 0.6 multiply_bitcast_fusion
  (3 shorter events, 0.1 us)
Async XLA Ops:
  1.5 21.4 %collective-permute-start.1 = (bf16[512,128]{1,0:T(8,128)(2,1)S(1)}, bf16[512,128]{1,0:T(8,128)(2,1)S(1)}, u32[]{:S(2)}, u32[]{:S(2)}) collective-permute-start(bf16[512,128]{1,0:T(8,128)(2,1)S(1)} %bitcast.11), channel_id=1, source_target_pairs={{0,16},{16,32},{32,48},{48,64},{64,80},{80,96},{96,112},{112,128},... | collective-permute-start | bytes 393224 | tf_op jit(solution)/shard_map/ppermute | solution.py:305
  5.0 4.0 %collective-permute-start = (bf16[512,128]{1,0:T(8,128)(2,1)S(1)}, bf16[512,128]{1,0:T(8,128)(2,1)S(1)}, u32[]{:S(2)}, u32[]{:S(2)}) collective-permute-start(bf16[512,128]{1,0:T(8,128)(2,1)S(1)} %bitcast.12), channel_id=1, source_target_pairs={{8,24},{24,40},{40,56},{56,72},{72,88},{88,104},{104,120},{120,136... | collective-permute-start | bytes 393224 | tf_op jit(solution)/shard_map/ppermute | solution.py:305
  5.8 1.0 %copy-start.3 = (bf16[256,1024]{1,0:T(8,128)(2,1)S(1)}, bf16[256,1024]{1,0:T(8,128)(2,1)}, u32[]{:S(2)}) copy-start(bf16[256,1024]{1,0:T(8,128)(2,1)} %q_ref.1) | copy-start | bytes 1572868
  6.8 0.7 copy-start.4
  25.1 3.8 %collective-permute-start.2 = (bf16[1024,256]{1,0:T(8,128)(2,1)S(1)}, bf16[1024,256]{1,0:T(8,128)(2,1)S(1)}, u32[]{:S(2)}, u32[]{:S(2)}) collective-permute-start(bf16[1024,256]{1,0:T(8,128)(2,1)S(1)} %get-tuple-element.25.out_t_ref), channel_id=1, source_target_pairs={{0,8},{8,0},{16,24},{24,16},{32,40},{40,32},{48,56},{56,48},{64,72... | collective-permute-start | bytes 1572872 | tf_op jit(solution)/shard_map/ppermute | solution.py:323
  28.9 5.3 %copy-start.2 = (bf16[256,1024]{1,0:T(8,128)(2,1)S(1)}, bf16[256,1024]{1,0:T(8,128)(2,1)}, u32[]{:S(2)}) copy-start(bf16[256,1024]{1,0:T(8,128)(2,1)} %go_ref.3) | copy-start | bytes 1572868
  30.6 19.1 %all-to-all-start = ((bf16[8,4,16,1024]{3,2,1,0:T(8,128)(2,1)}), bf16[8,4,16,1024]{3,2,1,0:T(8,128)(2,1)S(1)}, u32[]{:S(2)}, u32[]{:S(2)}) async-start(bf16[8,4,16,1024]{3,2,1,0:T(8,128)(2,1)} %gram_part.1), calls=%async_computation | async-start | bytes 2097152 | tf_op jit(solution)/shard_map/all_to_all | solution.py:336
  38.7 1.3 %copy-start = (bf16[8,2,256,256]{3,2,1,0:T(8,128)(2,1)}, bf16[8,2,256,256]{3,2,1,0:T(8,128)(2,1)S(1)}, u32[]{:S(2)}) copy-start(bf16[8,2,256,256]{3,2,1,0:T(8,128)(2,1)S(1)} %get-tuple-element.32.dscore_ref) | copy-start | bytes 6291460
  42.0 17.0 %collective-permute-start.3 = (bf16[2,256,128]{2,1,0:T(8,128)(2,1)S(1)}, bf16[2,256,128]{2,1,0:T(8,128)(2,1)S(1)}, u32[]{:S(2)}, u32[]{:S(2)}) collective-permute-start(bf16[2,256,128]{2,1,0:T(8,128)(2,1)S(1)} %get-tuple-element.38), channel_id=1, source_target_pairs={{0,496},{8,504},{16,0},{24,8},{32,16},{40,24},{48,32},{56,40},{64,... | collective-permute-start | bytes 393224 | tf_op jit(solution)/shard_map/ppermute | solution.py:305
  50.5 15.3 %all-to-all-start.1 = ((bf16[4,16,1024]{2,1,0:T(8,128)(2,1)}), bf16[4,16,1024]{2,1,0:T(8,128)(2,1)S(1)}, u32[]{:S(2)}, u32[]{:S(2)}) async-start(bf16[4,16,1024]{2,1,0:T(8,128)(2,1)} %row_sum.1.after_ref), calls=%async_computation.1 | async-start | bytes 262144 | tf_op jit(solution)/shard_map/all_to_all | solution.py:345
  53.8 1.6 %copy-start.1 = (bf16[8,2,256,256]{3,2,1,0:T(8,128)(2,1)S(1)}, bf16[8,2,256,256]{3,2,1,0:T(8,128)(2,1)}, u32[]{:S(2)}) copy-start(bf16[8,2,256,256]{3,2,1,0:T(8,128)(2,1)} %copy-done) | copy-start | bytes 6291460

commit v6 on v5

--- a/solution.py
+++ b/solution.py
@@ -48,7 +48,7 @@
         top_ref[h] = jnp.broadcast_to(top, (tok, dim))
 
 
-def forward_kernel(facts_ref, q_ref, mixed_ref, top_ref, pair_ref, even2_ref, out_t_ref, lse_ref, kv1_ref, kv2_ref):
+def forward_kernel(facts_ref, even2_ref, q_ref, mixed_ref, top_ref, pair_ref, out_t_ref, lse_ref, kv1_ref, kv2_ref):
     heads, tok, dim = top_ref.shape
     core = facts_ref[2:3, :1].astype(jnp.bfloat16)
     kv1_ref[...] = pair_ref[0] * core + pair_ref[1] * (1 - core)
@@ -205,7 +205,7 @@
     )(place, order, q, kv0)
 
 
-def forward(facts, q, mixed, top, pair, even2):
+def forward(facts, even2, q, mixed, top, pair):
     tok, width = q.shape
     heads = top.shape[0]
     return pl.pallas_call(
@@ -217,7 +217,7 @@
         compiler_params=PARAMS,
         cost_estimate=pl.CostEstimate(flops=8 * tok * width * tok, bytes_accessed=2000000, transcendentals=0),
         name="attention_forward",
-    )(facts, q, mixed, top, pair, even2)
+    )(facts, even2, q, mixed, top, pair)
 
 
 def away_gradients(facts, q, go, out_t, lse, kv1, kv2):
@@ -258,7 +258,7 @@
 def gram_part(facts, mine, other):
     planes, rows, cores, unit, tok = mine.shape
     feats = planes * rows * cores * unit
-    chunks = 4
+    chunks = 2
     return pl.pallas_call(
         gram_kernel,
         out_shape=jax.ShapeDtypeStruct((2 * rows, planes // 2, unit, feats), jnp.bfloat16),
@@ -319,7 +319,7 @@
     core = me % CORES
     pairs = [[i, i + 1] for i in range(0, count, CORES)]
     pair = lax.all_gather(jnp.where(core == 0, kv0, odd2), "seq", axis_index_groups=pairs)
-    out_t, lse, kv1, kv2 = forward(facts, q_near, mixed, top, pair, even2)
+    out_t, lse, kv1, kv2 = forward(facts, even2, q_near, mixed, top, pair)
     other_t = lax.ppermute(out_t, "seq", [(i, i ^ 1) for i in range(count)])
     split = (planes, ROWS, CORES, unit, tok)
     part = gram_part(facts, out_t.reshape(split), other_t.reshape(split))

time: 66.9 us -> 67 us (level)
  the two profiles are of different devices: /device:TPU:6 before, /device:TPU:8 now
where the time goes in v6:
time: 67 us; the launch traced here: 66.5 us
  starting transfers between devices  25.6 us (38%)
  waiting for transfers between devices  15.1 us (23%)
  Pallas kernels  14.8 us (22%)
  local copies, waits for them, and re-layouts  4.61 us (7%)
  blocking collectives  3.98 us (6%)
  other arithmetic  1.67 us (2%)
  between operations  0.76 us (1%)
    all_to_all x1, starting transfers between devices, local(): lax.all_to_all(part, 'seq', 0, 0, axis_index_groups=near_groups, tiled=True)  14.2 us
    ppermute x3, starting transfers between devices, shifted(): lax.ppermute(block, 'seq', [(i, (i + distance) % count) for i in range(co...  6.18 us
    all_to_all x1, waiting for transfers between devices, local(): lax.all_to_all(part, 'seq', 0, 0, axis_index_groups=far_groups, tiled=True)  6.11 us
    all_to_all x1, waiting for transfers between devices, local(): lax.all_to_all(part, 'seq', 0, 0, axis_index_groups=near_groups, tiled=True)  5.2 us
    unnamed x10, local copies, waits for them, and re-layouts  4.61 us
    pallas_call x1, Pallas kernels, away_gradients(): pl.pallas_call(away_kernel, out_shape=(pair, pair, jax.ShapeDtypeStruct((...  4.44 us
    pallas_call x1, Pallas kernels, backward(): pl.pallas_call(backward_kernel, out_shape=(full, jax.ShapeDtypeStruct((2,...  3.57 us
    all_to_all x1, starting transfers between devices, local(): lax.all_to_all(part, 'seq', 0, 0, axis_index_groups=far_groups, tiled=True)  3.32 us
  transfers between devices with their start and end apart: 6, of which 4 were waited for; matrix products, arithmetic and copies ran while one was open for 0% of the time, Pallas kernels for 16%

profile of v6, /device:TPU:8, one launch (start us, length us, event | category | flops | bytes accessed | tf_op | source)
XLA Modules:
  0.0 66.5 jit_solution(13953809147946056908)
XLA Ops:
  0.6 0.9 %pad_maximum_fusion = bf16[2,256,128]{2,1,0:T(8,128)(2,1)S(1)} fusion(bf16[1,256,128]{2,1,0:T(8,128)(2,1)} %bitcast.18, bf16[1,256,128]{2,1,0:T(8,128)(2,1)} %bitcast.19), kind=kLoop, calls=%fused_computation.3 | loop fusion | flops 65536 | bytes 262144 | tf_op jit(solution)/shard_map/stack | solution.py:315
  1.5 0.7 %collective-permute-start.1 = (bf16[512,128]{1,0:T(8,128)(2,1)S(1)}, bf16[512,128]{1,0:T(8,128)(2,1)S(1)}, u32[]{:S(2)}, u32[]{:S(2)}) collective-permute-start(bf16[512,128]{1,0:T(8,128)(2,1)S(1)} %bitcast.11), channel_id=1, source_target_pairs={{8,24},{24,40},{40,56},{56,72},{72,88},{88,104},{104,120},{120,136... | collective-permute-start | bytes 393224 | tf_op jit(solution)/shard_map/ppermute | solution.py:305
  2.2 3.5 %collective-permute-start = (bf16[512,128]{1,0:T(8,128)(2,1)S(1)}, bf16[512,128]{1,0:T(8,128)(2,1)S(1)}, u32[]{:S(2)}, u32[]{:S(2)}) collective-permute-start(bf16[512,128]{1,0:T(8,128)(2,1)S(1)} %bitcast.12), channel_id=1, source_target_pairs={{0,16},{16,32},{32,48},{48,64},{64,80},{80,96},{96,112},{112,128},... | collective-permute-start | bytes 393224 | tf_op jit(solution)/shard_map/ppermute | solution.py:305
  5.7 0.1 pad_add_fusion.place_ref
  5.8 0.0 copy-start.3
  5.8 1.0 %copy-done.3 = bf16[256,1024]{1,0:T(8,128)(2,1)S(1)} copy-done((bf16[256,1024]{1,0:T(8,128)(2,1)S(1)}, bf16[256,1024]{1,0:T(8,128)(2,1)}, u32[]{:S(2)}) %copy-start.3) | copy-done | bytes 524312
  6.8 0.0 copy-start.4
  6.8 0.7 copy-done.4
  7.5 1.5 %own_block.1 = (bf16[256,1024]{1,0:T(8,128)(2,1)S(1)}, f32[8,256,256]{2,1,0:T(8,128)S(1)}, f32[8,256,128]{2,1,0:T(8,128)S(1)}, f32[8,128]{1,0:T(8,128)S(1)}) custom-call(s32[2]{0:T(128)S(1)} %pad_add_fusion.place_ref, s32[64]{0:T(128)S(1)} %copy-done.4, bf16[256,1024]{1,0:T(8,128)(2,1)S(1)} %copy-done.3, bf16[512,128]{1,0:T(8,128)(2,1)S(1)} %bitcast.13), custom_call_target="tpu_custom_call" | custom-call | flops 268435456 | bytes 6000000 | tf_op jit(solution)/shard_map/own_block/pallas_call | solution.py:196
  9.0 0.0 collective-permute-done.1
  9.0 2.0 %all-gather = bf16[1024,128]{1,0:T(8,128)(2,1)S(1)} all-gather(bf16[512,128]{1,0:T(8,128)(2,1)S(1)} %broadcast_select_fusion.1), channel_id=2, replica_groups={{0,8},{16,24},{32,40},{48,56},{64,72},{80,88},{96,104},{112,120},{128,1..., dimensions={0}, use_global_device_ids=true | all-gather | bytes 393216 | tf_op jit(solution)/shard_map/all_gather | solution.py:321
  11.0 1.9 %collective-permute-done.even2_ref = bf16[512,128]{1,0:T(8,128)(2,1)S(1)} collective-permute-done((bf16[512,128]{1,0:T(8,128)(2,1)S(1)}, bf16[512,128]{1,0:T(8,128)(2,1)S(1)}, u32[]{:S(2)}, u32[]{:S(2)}) %collective-permute-start) | collective-permute-done | bytes 131104 | tf_op jit(solution)/shard_map/ppermute | solution.py:305
  12.9 2.2 %attention_forward.1 = (bf16[1024,256]{1,0:T(8,128)(2,1)S(1)}, f32[8,256]{1,0:T(8,128)S(1)}, bf16[512,128]{1,0:T(8,128)(2,1)S(1)}, bf16[512,128]{1,0:T(8,128)(2,1)S(1)}) custom-call(f32[8,128]{1,0:T(8,128)S(1)} %get-tuple-element.21.facts_ref, bf16[512,128]{1,0:T(8,128)(2,1)S(1)} %collective-permute-done.even2_ref, ...), custom_call_target="tpu_custom_call" | custom-call | flops 536870912 | bytes 2000000 | tf_op jit(solution)/shard_map/attention_forward/pallas_call | solution.py:211
  15.1 1.9 %collective-permute-start.2 = (bf16[1024,256]{1,0:T(8,128)(2,1)S(1)}, bf16[1024,256]{1,0:T(8,128)(2,1)S(1)}, u32[]{:S(2)}, u32[]{:S(2)}) collective-permute-start(bf16[1024,256]{1,0:T(8,128)(2,1)S(1)} %get-tuple-element.25.out_t_ref), channel_id=1, source_target_pairs={{0,8},{8,0},{16,24},{24,16},{32,40},{40,32},{48,56},{56,48},{64,72... | collective-permute-start | bytes 1572872 | tf_op jit(solution)/shard_map/ppermute | solution.py:323
  17.0 1.9 %collective-permute-done.2 = bf16[1024,256]{1,0:T(8,128)(2,1)S(1)} collective-permute-done((bf16[1024,256]{1,0:T(8,128)(2,1)S(1)}, bf16[1024,256]{1,0:T(8,128)(2,1)S(1)}, u32[]{:S(2)}, u32[]{:S(2)}) %collective-permute-start.2) | collective-permute-done | bytes 524320 | tf_op jit(solution)/shard_map/ppermute | solution.py:323
  18.9 0.0 copy-start.2
  18.9 1.6 %gram_part.1 = bf16[8,4,16,1024]{3,2,1,0:T(8,128)(2,1)} custom-call(f32[8,128]{1,0:T(8,128)S(1)} %get-tuple-element.21.facts_ref, bf16[8,4,2,16,256]{4,3,2,1,0:T(8,128)(2,1)S(1)} %bitcast.16, bf16[8,4,2,16,256]{4,3,2,1,0:T(8,128)(2,1)S(1)} %bitcast.17), custom_call_target="tpu_custom_call" | custom-call | flops 536870912 | bytes 2000000 | tf_op jit(solution)/shard_map/gram_part/pallas_call | solution.py:262
  20.6 14.2 %all-to-all-start = ((bf16[8,4,16,1024]{3,2,1,0:T(8,128)(2,1)}), bf16[8,4,16,1024]{3,2,1,0:T(8,128)(2,1)S(1)}, u32[]{:S(2)}, u32[]{:S(2)}) async-start(bf16[8,4,16,1024]{3,2,1,0:T(8,128)(2,1)} %gram_part.1), calls=%async_computation | async-start | bytes 2097152 | tf_op jit(solution)/shard_map/all_to_all | solution.py:336
  34.8 0.0 copy-done.2
  34.8 4.4 %away_gradients.1 = (bf16[2,256,128]{2,1,0:T(8,128)(2,1)S(1)}, bf16[2,256,128]{2,1,0:T(8,128)(2,1)S(1)}, bf16[256,1024]{1,0:T(8,128)(2,1)}, bf16[8,2,256,256]{3,2,1,0:T(8,128)(2,1)S(1)}, f32[8,256]{1,0:T(8,128)S(1)}) custom-call(f32[8,128]{1,0:T(8,128)S(1)} %get-tuple-element.21.facts_ref, bf16[256,1024]{1,0:T(8,128)(2,1)S(1)} %get-tuple-element.22.q_ref, ...), custom_call_target="tpu_custom_call" | custom-call | flops 1073741824 | bytes 3000000 | tf_op jit(solution)/shard_map/away_gradients/pallas_call | solution.py:228
  39.2 0.0 copy-start
  39.2 1.3 %copy-done = bf16[8,2,256,256]{3,2,1,0:T(8,128)(2,1)} copy-done((bf16[8,2,256,256]{3,2,1,0:T(8,128)(2,1)}, bf16[8,2,256,256]{3,2,1,0:T(8,128)(2,1)S(1)}, u32[]{:S(2)}) %copy-start) | copy-done | bytes 2097176
  40.6 2.0 %all-gather.1 = bf16[4,256,128]{2,1,0:T(8,128)(2,1)S(1)} all-gather(bf16[2,256,128]{2,1,0:T(8,128)(2,1)S(1)} %get-tuple-element.36), channel_id=3, replica_groups={{0,8},{16,24},{32,40},{48,56},{64,72},{80,88},{96,104},{112,120},{128,1..., dimensions={0}, use_global_device_ids=true | all-gather | bytes 393216 | tf_op jit(solution)/shard_map/all_gather | solution.py:338
  42.6 2.0 %collective-permute-start.3 = (bf16[2,256,128]{2,1,0:T(8,128)(2,1)S(1)}, bf16[2,256,128]{2,1,0:T(8,128)(2,1)S(1)}, u32[]{:S(2)}, u32[]{:S(2)}) collective-permute-start(bf16[2,256,128]{2,1,0:T(8,128)(2,1)S(1)} %get-tuple-element.38), channel_id=1, source_target_pairs={{0,496},{8,504},{16,0},{24,8},{32,16},{40,24},{48,32},{56,40},{64,... | collective-permute-start | bytes 393224 | tf_op jit(solution)/shard_map/ppermute | solution.py:305
  44.6 5.2 %all-to-all-done.part_ref = bf16[8,4,16,1024]{3,2,1,0:T(8,128)(2,1)S(1)} async-done(((bf16[8,4,16,1024]{3,2,1,0:T(8,128)(2,1)}), bf16[8,4,16,1024]{3,2,1,0:T(8,128)(2,1)S(1)}, u32[]{:S(2)}, u32[]{:S(2)}) %all-to-all-start) | async-done | bytes 1048608 | tf_op jit(solution)/shard_map/all_to_all | solution.py:336
  49.8 0.8 %row_sum.1.after_ref = bf16[4,16,1024]{2,1,0:T(8,128)(2,1)} custom-call(bf16[8,4,16,1024]{3,2,1,0:T(8,128)(2,1)S(1)} %all-to-all-done.part_ref), custom_call_target="tpu_custom_call" | custom-call | flops 524288 | bytes 1048576 | tf_op jit(solution)/shard_map/row_sum/pallas_call | solution.py:276
  50.6 3.3 %all-to-all-start.1 = ((bf16[4,16,1024]{2,1,0:T(8,128)(2,1)}), bf16[4,16,1024]{2,1,0:T(8,128)(2,1)S(1)}, u32[]{:S(2)}, u32[]{:S(2)}) async-start(bf16[4,16,1024]{2,1,0:T(8,128)(2,1)} %row_sum.1.after_ref), calls=%async_computation.1 | async-start | bytes 262144 | tf_op jit(solution)/shard_map/all_to_all | solution.py:345
  53.9 0.0 copy-start.1
  53.9 1.6 %copy-done.1 = bf16[8,2,256,256]{3,2,1,0:T(8,128)(2,1)S(1)} copy-done((bf16[8,2,256,256]{3,2,1,0:T(8,128)(2,1)S(1)}, bf16[8,2,256,256]{3,2,1,0:T(8,128)(2,1)}, u32[]{:S(2)}) %copy-start.1) | copy-done | bytes 2097176
  55.5 3.6 %attention_backward.1 = (bf16[256,1024]{1,0:T(8,128)(2,1)}, f32[2,256,128]{2,1,0:T(8,128)S(1)}) custom-call(bf16[256,1024]{1,0:T(8,128)(2,1)S(1)} %get-tuple-element.22.q_ref, bf16[256,1024]{1,0:T(8,128)(2,1)S(1)} %copy-done.2, f32[8,256]{1,0:T(8,128)S(1)} %get-tuple-element.27.lse_ref, f32[8,256]{1,0:T(8,128)S(1)} %get-tuple-element.31.row_dot_ref, ...), custom_call_target="tpu_custom_call" | custom-call | flops 939524096 | bytes 3000000 | tf_op jit(solution)/shard_map/attention_backward/pallas_call | solution.py:246
  59.1 0.0 collective-permute-done.3.back2_ref
  59.1 0.7 %key_value_sum.1 = bf16[2,256,128]{2,1,0:T(8,128)(2,1)} custom-call(f32[2,256,128]{2,1,0:T(8,128)S(1)} %get-tuple-element.35.kept_ref, bf16[2,256,128]{2,1,0:T(8,128)(2,1)S(1)} %get-tuple-element.39.back1_ref, bf16[2,256,128]{2,1,0:T(8,128)(2,1)S(1)} %collective-permute-done.3.back2_ref), custom_call_target="tpu_custom_call" | custom-call | flops 20000000000 | bytes 50000000 | tf_op jit(solution)/shard_map/key_value_sum/pallas_call | solution.py:288
  59.8 6.1 %all-to-all-done.1 = bf16[4,16,1024]{2,1,0:T(8,128)(2,1)S(1)} async-done(((bf16[4,16,1024]{2,1,0:T(8,128)(2,1)}), bf16[4,16,1024]{2,1,0:T(8,128)(2,1)S(1)}, u32[]{:S(2)}, u32[]{:S(2)}) %all-to-all-start.1) | async-done | bytes 131104 | tf_op jit(solution)/shard_map/all_to_all | solution.py:345
  65.9 0.6 multiply_bitcast_fusion
  (3 shorter events, 0.1 us)
Async XLA Ops:
  1.5 7.4 %collective-permute-start.1 = (bf16[512,128]{1,0:T(8,128)(2,1)S(1)}, bf16[512,128]{1,0:T(8,128)(2,1)S(1)}, u32[]{:S(2)}, u32[]{:S(2)}) collective-permute-start(bf16[512,128]{1,0:T(8,128)(2,1)S(1)} %bitcast.11), channel_id=1, source_target_pairs={{8,24},{24,40},{40,56},{56,72},{72,88},{88,104},{104,120},{120,136... | collective-permute-start | bytes 393224 | tf_op jit(solution)/shard_map/ppermute | solution.py:305
  2.2 10.7 %collective-permute-start = (bf16[512,128]{1,0:T(8,128)(2,1)S(1)}, bf16[512,128]{1,0:T(8,128)(2,1)S(1)}, u32[]{:S(2)}, u32[]{:S(2)}) collective-permute-start(bf16[512,128]{1,0:T(8,128)(2,1)S(1)} %bitcast.12), channel_id=1, source_target_pairs={{0,16},{16,32},{32,48},{48,64},{64,80},{80,96},{96,112},{112,128},... | collective-permute-start | bytes 393224 | tf_op jit(solution)/shard_map/ppermute | solution.py:305
  5.8 1.0 %copy-start.3 = (bf16[256,1024]{1,0:T(8,128)(2,1)S(1)}, bf16[256,1024]{1,0:T(8,128)(2,1)}, u32[]{:S(2)}) copy-start(bf16[256,1024]{1,0:T(8,128)(2,1)} %q_ref.1) | copy-start | bytes 1572868
  6.8 0.7 copy-start.4
  15.1 3.8 %collective-permute-start.2 = (bf16[1024,256]{1,0:T(8,128)(2,1)S(1)}, bf16[1024,256]{1,0:T(8,128)(2,1)S(1)}, u32[]{:S(2)}, u32[]{:S(2)}) collective-permute-start(bf16[1024,256]{1,0:T(8,128)(2,1)S(1)} %get-tuple-element.25.out_t_ref), channel_id=1, source_target_pairs={{0,8},{8,0},{16,24},{24,16},{32,40},{40,32},{48,56},{56,48},{64,72... | collective-permute-start | bytes 1572872 | tf_op jit(solution)/shard_map/ppermute | solution.py:323
  18.9 15.9 %copy-start.2 = (bf16[256,1024]{1,0:T(8,128)(2,1)S(1)}, bf16[256,1024]{1,0:T(8,128)(2,1)}, u32[]{:S(2)}) copy-start(bf16[256,1024]{1,0:T(8,128)(2,1)} %go_ref.3) | copy-start | bytes 1572868
  20.6 29.2 %all-to-all-start = ((bf16[8,4,16,1024]{3,2,1,0:T(8,128)(2,1)}), bf16[8,4,16,1024]{3,2,1,0:T(8,128)(2,1)S(1)}, u32[]{:S(2)}, u32[]{:S(2)}) async-start(bf16[8,4,16,1024]{3,2,1,0:T(8,128)(2,1)} %gram_part.1), calls=%async_computation | async-start | bytes 2097152 | tf_op jit(solution)/shard_map/all_to_all | solution.py:336
  39.2 1.3 %copy-start = (bf16[8,2,256,256]{3,2,1,0:T(8,128)(2,1)}, bf16[8,2,256,256]{3,2,1,0:T(8,128)(2,1)S(1)}, u32[]{:S(2)}) copy-start(bf16[8,2,256,256]{3,2,1,0:T(8,128)(2,1)S(1)} %get-tuple-element.32.dscore_ref) | copy-start | bytes 6291460
  42.6 16.5 %collective-permute-start.3 = (bf16[2,256,128]{2,1,0:T(8,128)(2,1)S(1)}, bf16[2,256,128]{2,1,0:T(8,128)(2,1)S(1)}, u32[]{:S(2)}, u32[]{:S(2)}) collective-permute-start(bf16[2,256,128]{2,1,0:T(8,128)(2,1)S(1)} %get-tuple-element.38), channel_id=1, source_target_pairs={{0,496},{8,504},{16,0},{24,8},{32,16},{40,24},{48,32},{56,40},{64,... | collective-permute-start | bytes 393224 | tf_op jit(solution)/shard_map/ppermute | solution.py:305
  50.6 15.3 %all-to-all-start.1 = ((bf16[4,16,1024]{2,1,0:T(8,128)(2,1)}), bf16[4,16,1024]{2,1,0:T(8,128)(2,1)S(1)}, u32[]{:S(2)}, u32[]{:S(2)}) async-start(bf16[4,16,1024]{2,1,0:T(8,128)(2,1)} %row_sum.1.after_ref), calls=%async_computation.1 | async-start | bytes 262144 | tf_op jit(solution)/shard_map/all_to_all | solution.py:345
  53.9 1.6 %copy-start.1 = (bf16[8,2,256,256]{3,2,1,0:T(8,128)(2,1)S(1)}, bf16[8,2,256,256]{3,2,1,0:T(8,128)(2,1)}, u32[]{:S(2)}) copy-start(bf16[8,2,256,256]{3,2,1,0:T(8,128)(2,1)} %copy-done) | copy-start | bytes 6291460

commit v7 on v6

--- a/solution.py
+++ b/solution.py
@@ -48,27 +48,35 @@
         top_ref[h] = jnp.broadcast_to(top, (tok, dim))
 
 
-def forward_kernel(facts_ref, even2_ref, q_ref, mixed_ref, top_ref, pair_ref, out_t_ref, lse_ref, kv1_ref, kv2_ref):
+def merged(scores, own, hide, mixed, value, unit):
+    top = jnp.maximum(own, jnp.max(scores, axis=1, keepdims=True) * unit - hide)
+    expo = jnp.exp2(scores * unit - twice(top + hide))
+    return top, mixed * twice(jnp.exp2(own - top)) + dot(expo.astype(jnp.bfloat16), value, NN)
+
+
+def next_kernel(facts_ref, q_ref, mixed_ref, top_ref, pair_ref, mixed_out_ref, top_out_ref, kv1_ref):
     heads, tok, dim = top_ref.shape
+    unit = math.log2(math.e) / dim**0.5
     core = facts_ref[2:3, :1].astype(jnp.bfloat16)
-    kv1_ref[...] = pair_ref[0] * core + pair_ref[1] * (1 - core)
-    kv2_ref[...] = pair_ref[1] * core + even2_ref[...] * (1 - core)
+    kv1 = pair_ref[0] * core + pair_ref[1] * (1 - core)
+    kv1_ref[...] = kv1
+    key, value = kv1[:tok], widened(kv1[tok:])
+    for h in range(heads):
+        scores = dot(q_ref[:, h * dim:(h + 1) * dim], key, NT)
+        top_out_ref[h], mixed_out_ref[h] = merged(scores, top_ref[h], facts_ref[0:1, :], mixed_ref[h], value, unit)
+
+
+def last_kernel(facts_ref, even2_ref, q_ref, mixed_ref, top_ref, pair_ref, out_t_ref, lse_ref, kv2_ref):
+    heads, tok, dim = top_ref.shape
     unit = math.log2(math.e) / dim**0.5
-    hide = [facts_ref[j:j + 1, :] for j in range(2)]
-    keys = [kv_ref[:tok, :] for kv_ref in (kv1_ref, kv2_ref)]
-    values = [widened(kv_ref[tok:, :]) for kv_ref in (kv1_ref, kv2_ref)]
+    core = facts_ref[2:3, :1].astype(jnp.bfloat16)
+    kv2 = pair_ref[1] * core + even2_ref[...] * (1 - core)
+    kv2_ref[...] = kv2
+    key, value = kv2[:tok], widened(kv2[tok:])
     for h in range(heads):
         cols = slice(h * dim, (h + 1) * dim)
-        qh = q_ref[:, cols]
-        scores = [dot(qh, key, NT) for key in keys]
-        own = top_ref[h]
-        top = own
-        for j in range(2):
-            top = jnp.maximum(top, jnp.max(scores[j], axis=1, keepdims=True) * unit - hide[j])
-        mixed = mixed_ref[h] * twice(jnp.exp2(own - top))
-        for j in range(2):
-            expo = jnp.exp2(scores[j] * unit - twice(top + hide[j]))
-            mixed = mixed + dot(expo.astype(jnp.bfloat16), values[j], NN)
+        scores = dot(q_ref[:, cols], key, NT)
+        top, mixed = merged(scores, top_ref[h], facts_ref[1:2, :], mixed_ref[h], value, unit)
         total = mixed[:, dim:]
         out_t_ref[cols, :] = (mixed[:, :dim] / total).T.astype(jnp.bfloat16)
         lse_ref[h:h + 1, :] = (top + jnp.log2(total)).T[:1]
@@ -205,18 +213,32 @@
     )(place, order, q, kv0)
 
 
-def forward(facts, even2, q, mixed, top, pair):
+def next_block(facts, q, mixed, top, pair):
+    tok, width = q.shape
+    return pl.pallas_call(
+        next_kernel,
+        out_shape=(jax.ShapeDtypeStruct(mixed.shape, mixed.dtype), jax.ShapeDtypeStruct(top.shape, top.dtype),
+                   jax.ShapeDtypeStruct(pair.shape[1:], pair.dtype)),
+        in_specs=[VMEM] * 5,
+        out_specs=(VMEM,) * 3,
+        compiler_params=PARAMS,
+        cost_estimate=pl.CostEstimate(flops=4 * tok * width * tok, bytes_accessed=2000000, transcendentals=0),
+        name="next_block",
+    )(facts, q, mixed, top, pair)
+
+
+def last_block(facts, even2, q, mixed, top, pair):
     tok, width = q.shape
     heads = top.shape[0]
     return pl.pallas_call(
-        forward_kernel,
+        last_kernel,
         out_shape=(jax.ShapeDtypeStruct((width, tok), jnp.bfloat16), jax.ShapeDtypeStruct((heads, tok), jnp.float32),
-                   jax.ShapeDtypeStruct(even2.shape, even2.dtype), jax.ShapeDtypeStruct(even2.shape, even2.dtype)),
+                   jax.ShapeDtypeStruct(even2.shape, even2.dtype)),
         in_specs=[VMEM] * 6,
-        out_specs=(VMEM,) * 4,
-        compiler_params=PARAMS,
-        cost_estimate=pl.CostEstimate(flops=8 * tok * width * tok, bytes_accessed=2000000, transcendentals=0),
-        name="attention_forward",
+        out_specs=(VMEM,) * 3,
+        compiler_params=PARAMS,
+        cost_estimate=pl.CostEstimate(flops=4 * tok * width * tok, bytes_accessed=2000000, transcendentals=0),
+        name="last_block",
     )(facts, even2, q, mixed, top, pair)
 
 
@@ -319,7 +341,8 @@
     core = me % CORES
     pairs = [[i, i + 1] for i in range(0, count, CORES)]
     pair = lax.all_gather(jnp.where(core == 0, kv0, odd2), "seq", axis_index_groups=pairs)
-    out_t, lse, kv1, kv2 = forward(facts, even2, q_near, mixed, top, pair)
+    mixed, top, kv1 = next_block(facts, q_near, mixed, top, pair)
+    out_t, lse, kv2 = last_block(facts, even2, q_near, mixed, top, pair)
     other_t = lax.ppermute(out_t, "seq", [(i, i ^ 1) for i in range(count)])
     split = (planes, ROWS, CORES, unit, tok)
     part = gram_part(facts, out_t.reshape(split), other_t.reshape(split))

time: 67 us -> 66.3 us (0.990)
  waiting for transfers between devices: 15.1 us -> 13.9 us
    ppermute x3, waiting for transfers between devices: 1.87 us -> 0.72 us  [shifted(): lax.ppermute(block, 'seq', [(i, (i + distance) % count) for i in range(co...]
    pallas_call x1 -> x2, Pallas kernels: 2.24 us -> 2.66 us  [the longest x1 1.5 us: last_block(): pl.pallas_call(last_kernel, out_shape=(jax.ShapeDtypeStruct((width, tok),...]
  transfers between devices with their start and end apart: 6 -> 6, of which waited for: 4 -> 4; matrix products, arithmetic and copies ran while one was open for 0% -> 0% of each run, Pallas kernels for 16% -> 18%
where the time goes in v7:
time: 66.3 us; the launch traced here: 65.8 us
  starting transfers between devices  25.6 us (39%)
  Pallas kernels  15.2 us (23%)
  waiting for transfers between devices  13.9 us (21%)
  local copies, waits for them, and re-layouts  4.61 us (7%)
  blocking collectives  3.98 us (6%)
  other arithmetic  1.67 us (3%)
  between operations  0.76 us (1%)
    all_to_all x1, starting transfers between devices, local(): lax.all_to_all(part, 'seq', 0, 0, axis_index_groups=near_groups, tiled=True)  14.2 us
    ppermute x3, starting transfers between devices, shifted(): lax.ppermute(block, 'seq', [(i, (i + distance) % count) for i in range(co...  6.17 us
    all_to_all x1, waiting for transfers between devices, local(): lax.all_to_all(part, 'seq', 0, 0, axis_index_groups=far_groups, tiled=True)  6.11 us
    all_to_all x1, waiting for transfers between devices, local(): lax.all_to_all(part, 'seq', 0, 0, axis_index_groups=near_groups, tiled=True)  5.23 us
    unnamed x10, local copies, waits for them, and re-layouts  4.61 us
    pallas_call x1, Pallas kernels, away_gradients(): pl.pallas_call(away_kernel, out_shape=(pair, pair, jax.ShapeDtypeStruct((...  4.44 us
    pallas_call x1, Pallas kernels, backward(): pl.pallas_call(backward_kernel, out_shape=(full, jax.ShapeDtypeStruct((2,...  3.57 us
    all_to_all x1, starting transfers between devices, local(): lax.all_to_all(part, 'seq', 0, 0, axis_index_groups=far_groups, tiled=True)  3.32 us
  transfers between devices with their start and end apart: 6, of which 4 were waited for; matrix products, arithmetic and copies ran while one was open for 0% of the time, Pallas kernels for 18%

profile of v7, /device:TPU:8, one launch (start us, length us, event | category | flops | bytes accessed | tf_op | source)
XLA Modules:
  0.0 65.8 jit_solution(18430034801685092638)
XLA Ops:
  0.6 0.9 %pad_maximum_fusion = bf16[2,256,128]{2,1,0:T(8,128)(2,1)S(1)} fusion(bf16[1,256,128]{2,1,0:T(8,128)(2,1)} %bitcast.19, bf16[1,256,128]{2,1,0:T(8,128)(2,1)} %bitcast.20), kind=kLoop, calls=%fused_computation.3 | loop fusion | flops 65536 | bytes 262144 | tf_op jit(solution)/shard_map/stack | solution.py:337
  1.5 0.7 %collective-permute-start.1 = (bf16[512,128]{1,0:T(8,128)(2,1)S(1)}, bf16[512,128]{1,0:T(8,128)(2,1)S(1)}, u32[]{:S(2)}, u32[]{:S(2)}) collective-permute-start(bf16[512,128]{1,0:T(8,128)(2,1)S(1)} %bitcast.13), channel_id=1, source_target_pairs={{8,24},{24,40},{40,56},{56,72},{72,88},{88,104},{104,120},{120,136... | collective-permute-start | bytes 393224 | tf_op jit(solution)/shard_map/ppermute | solution.py:327
  2.2 3.5 %collective-permute-start = (bf16[512,128]{1,0:T(8,128)(2,1)S(1)}, bf16[512,128]{1,0:T(8,128)(2,1)S(1)}, u32[]{:S(2)}, u32[]{:S(2)}) collective-permute-start(bf16[512,128]{1,0:T(8,128)(2,1)S(1)} %bitcast.14), channel_id=1, source_target_pairs={{0,16},{16,32},{32,48},{48,64},{64,80},{80,96},{96,112},{112,128},... | collective-permute-start | bytes 393224 | tf_op jit(solution)/shard_map/ppermute | solution.py:327
  5.7 0.1 pad_add_fusion.place_ref
  5.8 0.0 copy-start.3
  5.8 1.0 %copy-done.3 = bf16[256,1024]{1,0:T(8,128)(2,1)S(1)} copy-done((bf16[256,1024]{1,0:T(8,128)(2,1)S(1)}, bf16[256,1024]{1,0:T(8,128)(2,1)}, u32[]{:S(2)}) %copy-start.3) | copy-done | bytes 524312
  6.8 0.0 copy-start.4
  6.8 0.7 copy-done.4
  7.5 1.5 %own_block.1 = (bf16[256,1024]{1,0:T(8,128)(2,1)S(1)}, f32[8,256,256]{2,1,0:T(8,128)S(1)}, f32[8,256,128]{2,1,0:T(8,128)S(1)}, f32[8,128]{1,0:T(8,128)S(1)}) custom-call(s32[2]{0:T(128)S(1)} %pad_add_fusion.place_ref, s32[64]{0:T(128)S(1)} %copy-done.4, bf16[256,1024]{1,0:T(8,128)(2,1)S(1)} %copy-done.3, bf16[512,128]{1,0:T(8,128)(2,1)S(1)} %bitcast.15), custom_call_target="tpu_custom_call" | custom-call | flops 268435456 | bytes 6000000 | tf_op jit(solution)/shard_map/own_block/pallas_call | solution.py:204
  9.0 0.0 collective-permute-done.1
  9.0 2.0 %all-gather = bf16[1024,128]{1,0:T(8,128)(2,1)S(1)} all-gather(bf16[512,128]{1,0:T(8,128)(2,1)S(1)} %broadcast_select_fusion.1), channel_id=2, replica_groups={{0,8},{16,24},{32,40},{48,56},{64,72},{80,88},{96,104},{112,120},{128,1..., dimensions={0}, use_global_device_ids=true | all-gather | bytes 393216 | tf_op jit(solution)/shard_map/all_gather | solution.py:343
  11.0 1.2 %next_block.1 = (f32[8,256,256]{2,1,0:T(8,128)S(1)}, f32[8,256,128]{2,1,0:T(8,128)S(1)}, bf16[512,128]{1,0:T(8,128)(2,1)S(1)}) custom-call(f32[8,128]{1,0:T(8,128)S(1)} %get-tuple-element.23.facts_ref, bf16[256,1024]{1,0:T(8,128)(2,1)S(1)} %get-tuple-element.24.q_ref, f32[8,256,256]{2,1,0:T(8,128)S(1)} %get-tuple-element.25.mixed_ref, ...), custom_call_target="tpu_custom_call" | custom-call | flops 268435456 | bytes 2000000 | tf_op jit(solution)/shard_map/next_block/pallas_call | solution.py:218
  12.2 0.7 %collective-permute-done.even2_ref = bf16[512,128]{1,0:T(8,128)(2,1)S(1)} collective-permute-done((bf16[512,128]{1,0:T(8,128)(2,1)S(1)}, bf16[512,128]{1,0:T(8,128)(2,1)S(1)}, u32[]{:S(2)}, u32[]{:S(2)}) %collective-permute-start) | collective-permute-done | bytes 131104 | tf_op jit(solution)/shard_map/ppermute | solution.py:327
  12.9 1.5 %last_block.1 = (bf16[1024,256]{1,0:T(8,128)(2,1)S(1)}, f32[8,256]{1,0:T(8,128)S(1)}, bf16[512,128]{1,0:T(8,128)(2,1)S(1)}) custom-call(f32[8,128]{1,0:T(8,128)S(1)} %get-tuple-element.23.facts_ref, bf16[512,128]{1,0:T(8,128)(2,1)S(1)} %collective-permute-done.even2_ref, bf16[256,1024]{1,0:T(8,128)(2,1)S(1)} %get-tuple-element.24.q_ref, ...), custom_call_target="tpu_custom_call" | custom-call | flops 268435456 | bytes 2000000 | tf_op jit(solution)/shard_map/last_block/pallas_call | solution.py:233
  14.4 1.9 %collective-permute-start.2 = (bf16[1024,256]{1,0:T(8,128)(2,1)S(1)}, bf16[1024,256]{1,0:T(8,128)(2,1)S(1)}, u32[]{:S(2)}, u32[]{:S(2)}) collective-permute-start(bf16[1024,256]{1,0:T(8,128)(2,1)S(1)} %get-tuple-element.29.out_t_ref), channel_id=1, source_target_pairs={{0,8},{8,0},{16,24},{24,16},{32,40},{40,32},{48,56},{56,48},{64,72... | collective-permute-start | bytes 1572872 | tf_op jit(solution)/shard_map/ppermute | solution.py:346
  16.3 1.9 %collective-permute-done.2 = bf16[1024,256]{1,0:T(8,128)(2,1)S(1)} collective-permute-done((bf16[1024,256]{1,0:T(8,128)(2,1)S(1)}, bf16[1024,256]{1,0:T(8,128)(2,1)S(1)}, u32[]{:S(2)}, u32[]{:S(2)}) %collective-permute-start.2) | collective-permute-done | bytes 524320 | tf_op jit(solution)/shard_map/ppermute | solution.py:346
  18.2 0.0 copy-start.2
  18.2 1.6 %gram_part.1 = bf16[8,4,16,1024]{3,2,1,0:T(8,128)(2,1)} custom-call(f32[8,128]{1,0:T(8,128)S(1)} %get-tuple-element.23.facts_ref, bf16[8,4,2,16,256]{4,3,2,1,0:T(8,128)(2,1)S(1)} %bitcast.17, bf16[8,4,2,16,256]{4,3,2,1,0:T(8,128)(2,1)S(1)} %bitcast.18), custom_call_target="tpu_custom_call" | custom-call | flops 536870912 | bytes 2000000 | tf_op jit(solution)/shard_map/gram_part/pallas_call | solution.py:284
  19.8 14.2 %all-to-all-start = ((bf16[8,4,16,1024]{3,2,1,0:T(8,128)(2,1)}), bf16[8,4,16,1024]{3,2,1,0:T(8,128)(2,1)S(1)}, u32[]{:S(2)}, u32[]{:S(2)}) async-start(bf16[8,4,16,1024]{3,2,1,0:T(8,128)(2,1)} %gram_part.1), calls=%async_computation | async-start | bytes 2097152 | tf_op jit(solution)/shard_map/all_to_all | solution.py:359
  34.0 0.0 copy-done.2
  34.0 4.4 %away_gradients.1 = (bf16[2,256,128]{2,1,0:T(8,128)(2,1)S(1)}, bf16[2,256,128]{2,1,0:T(8,128)(2,1)S(1)}, bf16[256,1024]{1,0:T(8,128)(2,1)}, bf16[8,2,256,256]{3,2,1,0:T(8,128)(2,1)S(1)}, f32[8,256]{1,0:T(8,128)S(1)}) custom-call(f32[8,128]{1,0:T(8,128)S(1)} %get-tuple-element.23.facts_ref, bf16[256,1024]{1,0:T(8,128)(2,1)S(1)} %get-tuple-element.24.q_ref, ...), custom_call_target="tpu_custom_call" | custom-call | flops 1073741824 | bytes 3000000 | tf_op jit(solution)/shard_map/away_gradients/pallas_call | solution.py:250
  38.5 0.0 copy-start
  38.5 1.3 %copy-done = bf16[8,2,256,256]{3,2,1,0:T(8,128)(2,1)} copy-done((bf16[8,2,256,256]{3,2,1,0:T(8,128)(2,1)}, bf16[8,2,256,256]{3,2,1,0:T(8,128)(2,1)S(1)}, u32[]{:S(2)}) %copy-start) | copy-done | bytes 2097176
  39.8 2.0 %all-gather.1 = bf16[4,256,128]{2,1,0:T(8,128)(2,1)S(1)} all-gather(bf16[2,256,128]{2,1,0:T(8,128)(2,1)S(1)} %get-tuple-element.40), channel_id=3, replica_groups={{0,8},{16,24},{32,40},{48,56},{64,72},{80,88},{96,104},{112,120},{128,1..., dimensions={0}, use_global_device_ids=true | all-gather | bytes 393216 | tf_op jit(solution)/shard_map/all_gather | solution.py:361
  41.8 2.0 %collective-permute-start.3 = (bf16[2,256,128]{2,1,0:T(8,128)(2,1)S(1)}, bf16[2,256,128]{2,1,0:T(8,128)(2,1)S(1)}, u32[]{:S(2)}, u32[]{:S(2)}) collective-permute-start(bf16[2,256,128]{2,1,0:T(8,128)(2,1)S(1)} %get-tuple-element.42), channel_id=1, source_target_pairs={{0,496},{8,504},{16,0},{24,8},{32,16},{40,24},{48,32},{56,40},{64,... | collective-permute-start | bytes 393224 | tf_op jit(solution)/shard_map/ppermute | solution.py:327
  43.8 5.2 %all-to-all-done.part_ref = bf16[8,4,16,1024]{3,2,1,0:T(8,128)(2,1)S(1)} async-done(((bf16[8,4,16,1024]{3,2,1,0:T(8,128)(2,1)}), bf16[8,4,16,1024]{3,2,1,0:T(8,128)(2,1)S(1)}, u32[]{:S(2)}, u32[]{:S(2)}) %all-to-all-start) | async-done | bytes 1048608 | tf_op jit(solution)/shard_map/all_to_all | solution.py:359
  49.1 0.8 %row_sum.1.after_ref = bf16[4,16,1024]{2,1,0:T(8,128)(2,1)} custom-call(bf16[8,4,16,1024]{3,2,1,0:T(8,128)(2,1)S(1)} %all-to-all-done.part_ref), custom_call_target="tpu_custom_call" | custom-call | flops 524288 | bytes 1048576 | tf_op jit(solution)/shard_map/row_sum/pallas_call | solution.py:298
  49.8 3.3 %all-to-all-start.1 = ((bf16[4,16,1024]{2,1,0:T(8,128)(2,1)}), bf16[4,16,1024]{2,1,0:T(8,128)(2,1)S(1)}, u32[]{:S(2)}, u32[]{:S(2)}) async-start(bf16[4,16,1024]{2,1,0:T(8,128)(2,1)} %row_sum.1.after_ref), calls=%async_computation.1 | async-start | bytes 262144 | tf_op jit(solution)/shard_map/all_to_all | solution.py:368
  53.2 0.0 copy-start.1
  53.2 1.6 %copy-done.1 = bf16[8,2,256,256]{3,2,1,0:T(8,128)(2,1)S(1)} copy-done((bf16[8,2,256,256]{3,2,1,0:T(8,128)(2,1)S(1)}, bf16[8,2,256,256]{3,2,1,0:T(8,128)(2,1)}, u32[]{:S(2)}) %copy-start.1) | copy-done | bytes 2097176
  54.8 3.6 %attention_backward.1 = (bf16[256,1024]{1,0:T(8,128)(2,1)}, f32[2,256,128]{2,1,0:T(8,128)S(1)}) custom-call(bf16[256,1024]{1,0:T(8,128)(2,1)S(1)} %get-tuple-element.24.q_ref, bf16[256,1024]{1,0:T(8,128)(2,1)S(1)} %copy-done.2, f32[8,256]{1,0:T(8,128)S(1)} %get-tuple-element.31.lse_ref, f32[8,256]{1,0:T(8,128)S(1)} %get-tuple-element.35.row_dot_ref, ...), custom_call_target="tpu_custom_call" | custom-call | flops 939524096 | bytes 3000000 | tf_op jit(solution)/shard_map/attention_backward/pallas_call | solution.py:268
  58.3 0.0 collective-permute-done.3.back2_ref
  58.3 0.7 %key_value_sum.1 = bf16[2,256,128]{2,1,0:T(8,128)(2,1)} custom-call(f32[2,256,128]{2,1,0:T(8,128)S(1)} %get-tuple-element.39.kept_ref, bf16[2,256,128]{2,1,0:T(8,128)(2,1)S(1)} %get-tuple-element.43.back1_ref, bf16[2,256,128]{2,1,0:T(8,128)(2,1)S(1)} %collective-permute-done.3.back2_ref), custom_call_target="tpu_custom_call" | custom-call | flops 20000000000 | bytes 50000000 | tf_op jit(solution)/shard_map/key_value_sum/pallas_call | solution.py:310
  59.0 6.1 %all-to-all-done.1 = bf16[4,16,1024]{2,1,0:T(8,128)(2,1)S(1)} async-done(((bf16[4,16,1024]{2,1,0:T(8,128)(2,1)}), bf16[4,16,1024]{2,1,0:T(8,128)(2,1)S(1)}, u32[]{:S(2)}, u32[]{:S(2)}) %all-to-all-start.1) | async-done | bytes 131104 | tf_op jit(solution)/shard_map/all_to_all | solution.py:368
  65.2 0.6 multiply_bitcast_fusion
  (3 shorter events, 0.1 us)
Async XLA Ops:
  1.5 7.4 %collective-permute-start.1 = (bf16[512,128]{1,0:T(8,128)(2,1)S(1)}, bf16[512,128]{1,0:T(8,128)(2,1)S(1)}, u32[]{:S(2)}, u32[]{:S(2)}) collective-permute-start(bf16[512,128]{1,0:T(8,128)(2,1)S(1)} %bitcast.13), channel_id=1, source_target_pairs={{8,24},{24,40},{40,56},{56,72},{72,88},{88,104},{104,120},{120,136... | collective-permute-start | bytes 393224 | tf_op jit(solution)/shard_map/ppermute | solution.py:327
  2.2 10.7 %collective-permute-start = (bf16[512,128]{1,0:T(8,128)(2,1)S(1)}, bf16[512,128]{1,0:T(8,128)(2,1)S(1)}, u32[]{:S(2)}, u32[]{:S(2)}) collective-permute-start(bf16[512,128]{1,0:T(8,128)(2,1)S(1)} %bitcast.14), channel_id=1, source_target_pairs={{0,16},{16,32},{32,48},{48,64},{64,80},{80,96},{96,112},{112,128},... | collective-permute-start | bytes 393224 | tf_op jit(solution)/shard_map/ppermute | solution.py:327
  5.8 1.0 %copy-start.3 = (bf16[256,1024]{1,0:T(8,128)(2,1)S(1)}, bf16[256,1024]{1,0:T(8,128)(2,1)}, u32[]{:S(2)}) copy-start(bf16[256,1024]{1,0:T(8,128)(2,1)} %q_ref.1) | copy-start | bytes 1572868
  6.8 0.7 copy-start.4
  14.4 3.8 %collective-permute-start.2 = (bf16[1024,256]{1,0:T(8,128)(2,1)S(1)}, bf16[1024,256]{1,0:T(8,128)(2,1)S(1)}, u32[]{:S(2)}, u32[]{:S(2)}) collective-permute-start(bf16[1024,256]{1,0:T(8,128)(2,1)S(1)} %get-tuple-element.29.out_t_ref), channel_id=1, source_target_pairs={{0,8},{8,0},{16,24},{24,16},{32,40},{40,32},{48,56},{56,48},{64,72... | collective-permute-start | bytes 1572872 | tf_op jit(solution)/shard_map/ppermute | solution.py:346
  18.2 15.9 %copy-start.2 = (bf16[256,1024]{1,0:T(8,128)(2,1)S(1)}, bf16[256,1024]{1,0:T(8,128)(2,1)}, u32[]{:S(2)}) copy-start(bf16[256,1024]{1,0:T(8,128)(2,1)} %go_ref.3) | copy-start | bytes 1572868
  19.8 29.2 %all-to-all-start = ((bf16[8,4,16,1024]{3,2,1,0:T(8,128)(2,1)}), bf16[8,4,16,1024]{3,2,1,0:T(8,128)(2,1)S(1)}, u32[]{:S(2)}, u32[]{:S(2)}) async-start(bf16[8,4,16,1024]{3,2,1,0:T(8,128)(2,1)} %gram_part.1), calls=%async_computation | async-start | bytes 2097152 | tf_op jit(solution)/shard_map/all_to_all | solution.py:359
  38.5 1.3 %copy-start = (bf16[8,2,256,256]{3,2,1,0:T(8,128)(2,1)}, bf16[8,2,256,256]{3,2,1,0:T(8,128)(2,1)S(1)}, u32[]{:S(2)}) copy-start(bf16[8,2,256,256]{3,2,1,0:T(8,128)(2,1)S(1)} %get-tuple-element.36.dscore_ref) | copy-start | bytes 6291460
  41.8 16.5 %collective-permute-start.3 = (bf16[2,256,128]{2,1,0:T(8,128)(2,1)S(1)}, bf16[2,256,128]{2,1,0:T(8,128)(2,1)S(1)}, u32[]{:S(2)}, u32[]{:S(2)}) collective-permute-start(bf16[2,256,128]{2,1,0:T(8,128)(2,1)S(1)} %get-tuple-element.42), channel_id=1, source_target_pairs={{0,496},{8,504},{16,0},{24,8},{32,16},{40,24},{48,32},{56,40},{64,... | collective-permute-start | bytes 393224 | tf_op jit(solution)/shard_map/ppermute | solution.py:327
  49.8 15.3 %all-to-all-start.1 = ((bf16[4,16,1024]{2,1,0:T(8,128)(2,1)}), bf16[4,16,1024]{2,1,0:T(8,128)(2,1)S(1)}, u32[]{:S(2)}, u32[]{:S(2)}) async-start(bf16[4,16,1024]{2,1,0:T(8,128)(2,1)} %row_sum.1.after_ref), calls=%async_computation.1 | async-start | bytes 262144 | tf_op jit(solution)/shard_map/all_to_all | solution.py:368
  53.2 1.6 %copy-start.1 = (bf16[8,2,256,256]{3,2,1,0:T(8,128)(2,1)S(1)}, bf16[8,2,256,256]{3,2,1,0:T(8,128)(2,1)}, u32[]{:S(2)}) copy-start(bf16[8,2,256,256]{3,2,1,0:T(8,128)(2,1)} %copy-done) | copy-start | bytes 6291460

commit v8 on v7

--- a/solution.py
+++ b/solution.py
@@ -154,20 +154,31 @@
             kept_ref[1] = dv
 
 
-def gram_kernel(facts_ref, mine_ref, other_ref, part_hbm, part_ref, sems):
+def picked(facts_ref, ref):
+    planes, rows, _, unit, tok = ref.shape
     core = facts_ref[2:3, :1].astype(jnp.bfloat16)
+    return (ref[:, :, 0] * (1 - core) + ref[:, :, 1] * core).reshape(planes * rows * unit, tok)
+
+
+def own_gram_kernel(facts_ref, mine_ref, own_ref):
     planes, rows, cores, unit, tok = mine_ref.shape
+    chunks = own_ref.shape[0]
+    step = planes // chunks
+    left = picked(facts_ref, mine_ref)
+    for i in range(chunks):
+        own_ref[i] = dot(left, mine_ref[i * step:(i + 1) * step].reshape(step * rows * cores * unit, tok), NT)
+
+
+def gram_kernel(facts_ref, own_ref, other_ref, part_hbm, part_ref, sems):
+    planes, rows, cores, unit, tok = other_ref.shape
     chunks = part_ref.shape[0]
     step = planes // chunks
     wide = step * rows * cores * unit
-    picked = [ref[:, :, 0] * (1 - core) + ref[:, :, 1] * core for ref in (mine_ref, other_ref)]
-    left = jnp.concatenate([block.reshape(planes * rows * unit, tok) for block in picked], axis=1)
+    left = picked(facts_ref, other_ref)
     saves = []
     for i in range(chunks):
-        right = jnp.concatenate(
-            [ref[i * step:(i + 1) * step].reshape(wide, tok) for ref in (mine_ref, other_ref)], axis=1
-        )
-        got = dot(left, right, NT).astype(jnp.bfloat16)
+        right = other_ref[i * step:(i + 1) * step].reshape(wide, tok)
+        got = (own_ref[i] + dot(left, right, NT)).astype(jnp.bfloat16)
         for plane in range(planes):
             block = got[plane * rows * unit:(plane + 1) * rows * unit]
             first = (plane % 2) * rows
@@ -277,10 +288,24 @@
     )(q, go, lse, row_dot, dscore, kv0, kv1, kv2, after)
 
 
-def gram_part(facts, mine, other):
+def own_gram(facts, mine):
     planes, rows, cores, unit, tok = mine.shape
     feats = planes * rows * cores * unit
-    chunks = 2
+    return pl.pallas_call(
+        own_gram_kernel,
+        out_shape=jax.ShapeDtypeStruct((2, feats // cores, feats // 2), jnp.float32),
+        in_specs=[VMEM] * 2,
+        out_specs=VMEM,
+        compiler_params=PARAMS,
+        cost_estimate=pl.CostEstimate(flops=feats * feats * tok, bytes_accessed=2000000, transcendentals=0),
+        name="own_gram",
+    )(facts, mine)
+
+
+def gram_part(facts, own, other):
+    planes, rows, cores, unit, tok = other.shape
+    feats = planes * rows * cores * unit
+    chunks = own.shape[0]
     return pl.pallas_call(
         gram_kernel,
         out_shape=jax.ShapeDtypeStruct((2 * rows, planes // 2, unit, feats), jnp.bfloat16),
@@ -289,9 +314,9 @@
         scratch_shapes=[pltpu.VMEM((chunks, 2 * rows, planes // 2, unit, feats // chunks), jnp.bfloat16),
                         pltpu.SemaphoreType.DMA((chunks,))],
         compiler_params=PARAMS,
-        cost_estimate=pl.CostEstimate(flops=2 * feats * feats * tok, bytes_accessed=2000000, transcendentals=0),
+        cost_estimate=pl.CostEstimate(flops=feats * feats * tok, bytes_accessed=2000000, transcendentals=0),
         name="gram_part",
-    )(facts, mine, other)
+    )(facts, own, other)
 
 
 def row_sum(part):
@@ -345,7 +370,7 @@
     out_t, lse, kv2 = last_block(facts, even2, q_near, mixed, top, pair)
     other_t = lax.ppermute(out_t, "seq", [(i, i ^ 1) for i in range(count)])
     split = (planes, ROWS, CORES, unit, tok)
-    part = gram_part(facts, out_t.reshape(split), other_t.reshape(split))
+    part = gram_part(facts, own_gram(facts, out_t.reshape(split)), other_t.reshape(split))
     seat = lambda z, y, c: (z * ROWS + y) * CORES + c
     near_groups = [
         [seat(2 * half + side, y, c) for side in range(2) for y in range(ROWS)]

time: 66.3 us -> 66 us (level)
  transfers between devices with their start and end apart: 6 -> 6, of which waited for: 4 -> 4; matrix products, arithmetic and copies ran while one was open for 0% -> 0% of each run, Pallas kernels for 18% -> 19%
where the time goes in v8:
time: 66 us; the launch traced here: 65.5 us
  starting transfers between devices  25.6 us (39%)
  Pallas kernels  15.5 us (23%)
  waiting for transfers between devices  13.4 us (20%)
  local copies, waits for them, and re-layouts  4.61 us (7%)
  blocking collectives  3.98 us (6%)
  other arithmetic  1.67 us (3%)
  between operations  0.76 us (1%)
    all_to_all x1, starting transfers between devices, local(): lax.all_to_all(part, 'seq', 0, 0, axis_index_groups=near_groups, tiled=True)  14.2 us
    ppermute x3, starting transfers between devices, shifted(): lax.ppermute(block, 'seq', [(i, (i + distance) % count) for i in range(co...  6.18 us
    all_to_all x1, waiting for transfers between devices, local(): lax.all_to_all(part, 'seq', 0, 0, axis_index_groups=far_groups, tiled=True)  6.08 us
    all_to_all x1, waiting for transfers between devices, local(): lax.all_to_all(part, 'seq', 0, 0, axis_index_groups=near_groups, tiled=True)  5.2 us
    unnamed x10, local copies, waits for them, and re-layouts  4.61 us
    pallas_call x1, Pallas kernels, away_gradients(): pl.pallas_call(away_kernel, out_shape=(pair, pair, jax.ShapeDtypeStruct((...  4.44 us
    pallas_call x1, Pallas kernels, backward(): pl.pallas_call(backward_kernel, out_shape=(full, jax.ShapeDtypeStruct((2,...  3.57 us
    all_to_all x1, starting transfers between devices, local(): lax.all_to_all(part, 'seq', 0, 0, axis_index_groups=far_groups, tiled=True)  3.32 us
  transfers between devices with their start and end apart: 6, of which 4 were waited for; matrix products, arithmetic and copies ran while one was open for 0% of the time, Pallas kernels for 19%

profile of v8, /device:TPU:8, one launch (start us, length us, event | category | flops | bytes accessed | tf_op | source)
XLA Modules:
  0.0 65.5 jit_solution(4119916604002568457)
XLA Ops:
  0.6 0.9 %pad_maximum_fusion = bf16[2,256,128]{2,1,0:T(8,128)(2,1)S(1)} fusion(bf16[1,256,128]{2,1,0:T(8,128)(2,1)} %bitcast.19, bf16[1,256,128]{2,1,0:T(8,128)(2,1)} %bitcast.20), kind=kLoop, calls=%fused_computation.3 | loop fusion | flops 65536 | bytes 262144 | tf_op jit(solution)/shard_map/stack | solution.py:362
  1.5 0.7 %collective-permute-start.1 = (bf16[512,128]{1,0:T(8,128)(2,1)S(1)}, bf16[512,128]{1,0:T(8,128)(2,1)S(1)}, u32[]{:S(2)}, u32[]{:S(2)}) collective-permute-start(bf16[512,128]{1,0:T(8,128)(2,1)S(1)} %bitcast.13), channel_id=1, source_target_pairs={{8,24},{24,40},{40,56},{56,72},{72,88},{88,104},{104,120},{120,136... | collective-permute-start | bytes 393224 | tf_op jit(solution)/shard_map/ppermute | solution.py:352
  2.2 3.5 %collective-permute-start = (bf16[512,128]{1,0:T(8,128)(2,1)S(1)}, bf16[512,128]{1,0:T(8,128)(2,1)S(1)}, u32[]{:S(2)}, u32[]{:S(2)}) collective-permute-start(bf16[512,128]{1,0:T(8,128)(2,1)S(1)} %bitcast.14), channel_id=1, source_target_pairs={{0,16},{16,32},{32,48},{48,64},{64,80},{80,96},{96,112},{112,128},... | collective-permute-start | bytes 393224 | tf_op jit(solution)/shard_map/ppermute | solution.py:352
  5.7 0.1 pad_add_fusion.place_ref
  5.8 0.0 copy-start.3
  5.8 1.0 %copy-done.3 = bf16[256,1024]{1,0:T(8,128)(2,1)S(1)} copy-done((bf16[256,1024]{1,0:T(8,128)(2,1)S(1)}, bf16[256,1024]{1,0:T(8,128)(2,1)}, u32[]{:S(2)}) %copy-start.3) | copy-done | bytes 524312
  6.8 0.0 copy-start.4
  6.8 0.7 copy-done.4
  7.5 1.5 %own_block.1 = (bf16[256,1024]{1,0:T(8,128)(2,1)S(1)}, f32[8,256,256]{2,1,0:T(8,128)S(1)}, f32[8,256,128]{2,1,0:T(8,128)S(1)}, f32[8,128]{1,0:T(8,128)S(1)}) custom-call(s32[2]{0:T(128)S(1)} %pad_add_fusion.place_ref, s32[64]{0:T(128)S(1)} %copy-done.4, bf16[256,1024]{1,0:T(8,128)(2,1)S(1)} %copy-done.3, bf16[512,128]{1,0:T(8,128)(2,1)S(1)} %bitcast.15), custom_call_target="tpu_custom_call" | custom-call | flops 268435456 | bytes 6000000 | tf_op jit(solution)/shard_map/own_block/pallas_call | solution.py:215
  9.0 0.0 collective-permute-done.1
  9.0 2.0 %all-gather = bf16[1024,128]{1,0:T(8,128)(2,1)S(1)} all-gather(bf16[512,128]{1,0:T(8,128)(2,1)S(1)} %broadcast_select_fusion.1), channel_id=2, replica_groups={{0,8},{16,24},{32,40},{48,56},{64,72},{80,88},{96,104},{112,120},{128,1..., dimensions={0}, use_global_device_ids=true | all-gather | bytes 393216 | tf_op jit(solution)/shard_map/all_gather | solution.py:368
  11.0 1.2 %next_block.1 = (f32[8,256,256]{2,1,0:T(8,128)S(1)}, f32[8,256,128]{2,1,0:T(8,128)S(1)}, bf16[512,128]{1,0:T(8,128)(2,1)S(1)}) custom-call(f32[8,128]{1,0:T(8,128)S(1)} %get-tuple-element.23.facts_ref, bf16[256,1024]{1,0:T(8,128)(2,1)S(1)} %get-tuple-element.24.q_ref, f32[8,256,256]{2,1,0:T(8,128)S(1)} %get-tuple-element.25.mixed_ref, ...), custom_call_target="tpu_custom_call" | custom-call | flops 268435456 | bytes 2000000 | tf_op jit(solution)/shard_map/next_block/pallas_call | solution.py:229
  12.2 0.7 %collective-permute-done.even2_ref = bf16[512,128]{1,0:T(8,128)(2,1)S(1)} collective-permute-done((bf16[512,128]{1,0:T(8,128)(2,1)S(1)}, bf16[512,128]{1,0:T(8,128)(2,1)S(1)}, u32[]{:S(2)}, u32[]{:S(2)}) %collective-permute-start) | collective-permute-done | bytes 131104 | tf_op jit(solution)/shard_map/ppermute | solution.py:352
  12.9 1.5 %last_block.1 = (bf16[1024,256]{1,0:T(8,128)(2,1)S(1)}, f32[8,256]{1,0:T(8,128)S(1)}, bf16[512,128]{1,0:T(8,128)(2,1)S(1)}) custom-call(f32[8,128]{1,0:T(8,128)S(1)} %get-tuple-element.23.facts_ref, bf16[512,128]{1,0:T(8,128)(2,1)S(1)} %collective-permute-done.even2_ref, bf16[256,1024]{1,0:T(8,128)(2,1)S(1)} %get-tuple-element.24.q_ref, ...), custom_call_target="tpu_custom_call" | custom-call | flops 268435456 | bytes 2000000 | tf_op jit(solution)/shard_map/last_block/pallas_call | solution.py:244
  14.4 1.9 %collective-permute-start.2 = (bf16[1024,256]{1,0:T(8,128)(2,1)S(1)}, bf16[1024,256]{1,0:T(8,128)(2,1)S(1)}, u32[]{:S(2)}, u32[]{:S(2)}) collective-permute-start(bf16[1024,256]{1,0:T(8,128)(2,1)S(1)} %get-tuple-element.29.out_t_ref), channel_id=1, source_target_pairs={{0,8},{8,0},{16,24},{24,16},{32,40},{40,32},{48,56},{56,48},{64,72... | collective-permute-start | bytes 1572872 | tf_op jit(solution)/shard_map/ppermute | solution.py:371
  16.3 0.5 own_gram.1.own_ref
  16.8 1.4 %collective-permute-done.2 = bf16[1024,256]{1,0:T(8,128)(2,1)S(1)} collective-permute-done((bf16[1024,256]{1,0:T(8,128)(2,1)S(1)}, bf16[1024,256]{1,0:T(8,128)(2,1)S(1)}, u32[]{:S(2)}, u32[]{:S(2)}) %collective-permute-start.2) | collective-permute-done | bytes 524320 | tf_op jit(solution)/shard_map/ppermute | solution.py:371
  18.2 0.0 copy-start.2
  18.2 1.4 %gram_part.1 = bf16[8,4,16,1024]{3,2,1,0:T(8,128)(2,1)} custom-call(f32[8,128]{1,0:T(8,128)S(1)} %get-tuple-element.23.facts_ref, f32[2,512,512]{2,1,0:T(8,128)S(1)} %own_gram.1.own_ref, bf16[8,4,2,16,256]{4,3,2,1,0:T(8,128)(2,1)S(1)} %bitcast.18), custom_call_target="tpu_custom_call" | custom-call | flops 268435456 | bytes 2000000 | tf_op jit(solution)/shard_map/gram_part/pallas_call | solution.py:309
  19.6 14.2 %all-to-all-start = ((bf16[8,4,16,1024]{3,2,1,0:T(8,128)(2,1)}), bf16[8,4,16,1024]{3,2,1,0:T(8,128)(2,1)S(1)}, u32[]{:S(2)}, u32[]{:S(2)}) async-start(bf16[8,4,16,1024]{3,2,1,0:T(8,128)(2,1)} %gram_part.1), calls=%async_computation | async-start | bytes 2097152 | tf_op jit(solution)/shard_map/all_to_all | solution.py:384
  33.8 0.0 copy-done.2
  33.8 4.4 %away_gradients.1 = (bf16[2,256,128]{2,1,0:T(8,128)(2,1)S(1)}, bf16[2,256,128]{2,1,0:T(8,128)(2,1)S(1)}, bf16[256,1024]{1,0:T(8,128)(2,1)}, bf16[8,2,256,256]{3,2,1,0:T(8,128)(2,1)S(1)}, f32[8,256]{1,0:T(8,128)S(1)}) custom-call(f32[8,128]{1,0:T(8,128)S(1)} %get-tuple-element.23.facts_ref, bf16[256,1024]{1,0:T(8,128)(2,1)S(1)} %get-tuple-element.24.q_ref, ...), custom_call_target="tpu_custom_call" | custom-call | flops 1073741824 | bytes 3000000 | tf_op jit(solution)/shard_map/away_gradients/pallas_call | solution.py:261
  38.2 0.0 copy-start
  38.2 1.3 %copy-done = bf16[8,2,256,256]{3,2,1,0:T(8,128)(2,1)} copy-done((bf16[8,2,256,256]{3,2,1,0:T(8,128)(2,1)}, bf16[8,2,256,256]{3,2,1,0:T(8,128)(2,1)S(1)}, u32[]{:S(2)}) %copy-start) | copy-done | bytes 2097176
  39.5 2.0 %all-gather.1 = bf16[4,256,128]{2,1,0:T(8,128)(2,1)S(1)} all-gather(bf16[2,256,128]{2,1,0:T(8,128)(2,1)S(1)} %get-tuple-element.40), channel_id=3, replica_groups={{0,8},{16,24},{32,40},{48,56},{64,72},{80,88},{96,104},{112,120},{128,1..., dimensions={0}, use_global_device_ids=true | all-gather | bytes 393216 | tf_op jit(solution)/shard_map/all_gather | solution.py:386
  41.5 2.0 %collective-permute-start.3 = (bf16[2,256,128]{2,1,0:T(8,128)(2,1)S(1)}, bf16[2,256,128]{2,1,0:T(8,128)(2,1)S(1)}, u32[]{:S(2)}, u32[]{:S(2)}) collective-permute-start(bf16[2,256,128]{2,1,0:T(8,128)(2,1)S(1)} %get-tuple-element.42), channel_id=1, source_target_pairs={{0,496},{8,504},{16,0},{24,8},{32,16},{40,24},{48,32},{56,40},{64,... | collective-permute-start | bytes 393224 | tf_op jit(solution)/shard_map/ppermute | solution.py:352
  43.6 5.2 %all-to-all-done.part_ref = bf16[8,4,16,1024]{3,2,1,0:T(8,128)(2,1)S(1)} async-done(((bf16[8,4,16,1024]{3,2,1,0:T(8,128)(2,1)}), bf16[8,4,16,1024]{3,2,1,0:T(8,128)(2,1)S(1)}, u32[]{:S(2)}, u32[]{:S(2)}) %all-to-all-start) | async-done | bytes 1048608 | tf_op jit(solution)/shard_map/all_to_all | solution.py:384
  48.8 0.8 %row_sum.1.after_ref = bf16[4,16,1024]{2,1,0:T(8,128)(2,1)} custom-call(bf16[8,4,16,1024]{3,2,1,0:T(8,128)(2,1)S(1)} %all-to-all-done.part_ref), custom_call_target="tpu_custom_call" | custom-call | flops 524288 | bytes 1048576 | tf_op jit(solution)/shard_map/row_sum/pallas_call | solution.py:323
  49.6 3.3 %all-to-all-start.1 = ((bf16[4,16,1024]{2,1,0:T(8,128)(2,1)}), bf16[4,16,1024]{2,1,0:T(8,128)(2,1)S(1)}, u32[]{:S(2)}, u32[]{:S(2)}) async-start(bf16[4,16,1024]{2,1,0:T(8,128)(2,1)} %row_sum.1.after_ref), calls=%async_computation.1 | async-start | bytes 262144 | tf_op jit(solution)/shard_map/all_to_all | solution.py:393
  52.9 0.0 copy-start.1
  52.9 1.6 %copy-done.1 = bf16[8,2,256,256]{3,2,1,0:T(8,128)(2,1)S(1)} copy-done((bf16[8,2,256,256]{3,2,1,0:T(8,128)(2,1)S(1)}, bf16[8,2,256,256]{3,2,1,0:T(8,128)(2,1)}, u32[]{:S(2)}) %copy-start.1) | copy-done | bytes 2097176
  54.5 3.6 %attention_backward.1 = (bf16[256,1024]{1,0:T(8,128)(2,1)}, f32[2,256,128]{2,1,0:T(8,128)S(1)}) custom-call(bf16[256,1024]{1,0:T(8,128)(2,1)S(1)} %get-tuple-element.24.q_ref, bf16[256,1024]{1,0:T(8,128)(2,1)S(1)} %copy-done.2, f32[8,256]{1,0:T(8,128)S(1)} %get-tuple-element.31.lse_ref, f32[8,256]{1,0:T(8,128)S(1)} %get-tuple-element.35.row_dot_ref, ...), custom_call_target="tpu_custom_call" | custom-call | flops 939524096 | bytes 3000000 | tf_op jit(solution)/shard_map/attention_backward/pallas_call | solution.py:279
  58.1 0.0 collective-permute-done.3.back2_ref
  58.1 0.7 %key_value_sum.1 = bf16[2,256,128]{2,1,0:T(8,128)(2,1)} custom-call(f32[2,256,128]{2,1,0:T(8,128)S(1)} %get-tuple-element.39.kept_ref, bf16[2,256,128]{2,1,0:T(8,128)(2,1)S(1)} %get-tuple-element.43.back1_ref, bf16[2,256,128]{2,1,0:T(8,128)(2,1)S(1)} %collective-permute-done.3.back2_ref), custom_call_target="tpu_custom_call" | custom-call | flops 20000000000 | bytes 50000000 | tf_op jit(solution)/shard_map/key_value_sum/pallas_call | solution.py:335
  58.8 6.1 %all-to-all-done.1 = bf16[4,16,1024]{2,1,0:T(8,128)(2,1)S(1)} async-done(((bf16[4,16,1024]{2,1,0:T(8,128)(2,1)}), bf16[4,16,1024]{2,1,0:T(8,128)(2,1)S(1)}, u32[]{:S(2)}, u32[]{:S(2)}) %all-to-all-start.1) | async-done | bytes 131104 | tf_op jit(solution)/shard_map/all_to_all | solution.py:393
  64.9 0.6 multiply_bitcast_fusion
  (3 shorter events, 0.1 us)
Async XLA Ops:
  1.5 7.4 %collective-permute-start.1 = (bf16[512,128]{1,0:T(8,128)(2,1)S(1)}, bf16[512,128]{1,0:T(8,128)(2,1)S(1)}, u32[]{:S(2)}, u32[]{:S(2)}) collective-permute-start(bf16[512,128]{1,0:T(8,128)(2,1)S(1)} %bitcast.13), channel_id=1, source_target_pairs={{8,24},{24,40},{40,56},{56,72},{72,88},{88,104},{104,120},{120,136... | collective-permute-start | bytes 393224 | tf_op jit(solution)/shard_map/ppermute | solution.py:352
  2.2 10.7 %collective-permute-start = (bf16[512,128]{1,0:T(8,128)(2,1)S(1)}, bf16[512,128]{1,0:T(8,128)(2,1)S(1)}, u32[]{:S(2)}, u32[]{:S(2)}) collective-permute-start(bf16[512,128]{1,0:T(8,128)(2,1)S(1)} %bitcast.14), channel_id=1, source_target_pairs={{0,16},{16,32},{32,48},{48,64},{64,80},{80,96},{96,112},{112,128},... | collective-permute-start | bytes 393224 | tf_op jit(solution)/shard_map/ppermute | solution.py:352
  5.8 1.0 %copy-start.3 = (bf16[256,1024]{1,0:T(8,128)(2,1)S(1)}, bf16[256,1024]{1,0:T(8,128)(2,1)}, u32[]{:S(2)}) copy-start(bf16[256,1024]{1,0:T(8,128)(2,1)} %q_ref.1) | copy-start | bytes 1572868
  6.8 0.7 %copy-start.4 = (s32[64]{0:T(128)S(1)}, s32[64]{0:T(128)}, u32[]{:S(2)}) copy-start(s32[64]{0:T(128)} %order_ref.1) | copy-start | bytes 772
  14.4 3.8 %collective-permute-start.2 = (bf16[1024,256]{1,0:T(8,128)(2,1)S(1)}, bf16[1024,256]{1,0:T(8,128)(2,1)S(1)}, u32[]{:S(2)}, u32[]{:S(2)}) collective-permute-start(bf16[1024,256]{1,0:T(8,128)(2,1)S(1)} %get-tuple-element.29.out_t_ref), channel_id=1, source_target_pairs={{0,8},{8,0},{16,24},{24,16},{32,40},{40,32},{48,56},{56,48},{64,72... | collective-permute-start | bytes 1572872 | tf_op jit(solution)/shard_map/ppermute | solution.py:371
  18.2 15.6 %copy-start.2 = (bf16[256,1024]{1,0:T(8,128)(2,1)S(1)}, bf16[256,1024]{1,0:T(8,128)(2,1)}, u32[]{:S(2)}) copy-start(bf16[256,1024]{1,0:T(8,128)(2,1)} %go_ref.3) | copy-start | bytes 1572868
  19.6 29.2 %all-to-all-start = ((bf16[8,4,16,1024]{3,2,1,0:T(8,128)(2,1)}), bf16[8,4,16,1024]{3,2,1,0:T(8,128)(2,1)S(1)}, u32[]{:S(2)}, u32[]{:S(2)}) async-start(bf16[8,4,16,1024]{3,2,1,0:T(8,128)(2,1)} %gram_part.1), calls=%async_computation | async-start | bytes 2097152 | tf_op jit(solution)/shard_map/all_to_all | solution.py:384
  38.2 1.3 %copy-start = (bf16[8,2,256,256]{3,2,1,0:T(8,128)(2,1)}, bf16[8,2,256,256]{3,2,1,0:T(8,128)(2,1)S(1)}, u32[]{:S(2)}) copy-start(bf16[8,2,256,256]{3,2,1,0:T(8,128)(2,1)S(1)} %get-tuple-element.36.dscore_ref) | copy-start | bytes 6291460
  41.5 16.5 %collective-permute-start.3 = (bf16[2,256,128]{2,1,0:T(8,128)(2,1)S(1)}, bf16[2,256,128]{2,1,0:T(8,128)(2,1)S(1)}, u32[]{:S(2)}, u32[]{:S(2)}) collective-permute-start(bf16[2,256,128]{2,1,0:T(8,128)(2,1)S(1)} %get-tuple-element.42), channel_id=1, source_target_pairs={{0,496},{8,504},{16,0},{24,8},{32,16},{40,24},{48,32},{56,40},{64,... | collective-permute-start | bytes 393224 | tf_op jit(solution)/shard_map/ppermute | solution.py:352
  49.6 15.3 %all-to-all-start.1 = ((bf16[4,16,1024]{2,1,0:T(8,128)(2,1)}), bf16[4,16,1024]{2,1,0:T(8,128)(2,1)S(1)}, u32[]{:S(2)}, u32[]{:S(2)}) async-start(bf16[4,16,1024]{2,1,0:T(8,128)(2,1)} %row_sum.1.after_ref), calls=%async_computation.1 | async-start | bytes 262144 | tf_op jit(solution)/shard_map/all_to_all | solution.py:393
  52.9 1.6 %copy-start.1 = (bf16[8,2,256,256]{3,2,1,0:T(8,128)(2,1)S(1)}, bf16[8,2,256,256]{3,2,1,0:T(8,128)(2,1)}, u32[]{:S(2)}) copy-start(bf16[8,2,256,256]{3,2,1,0:T(8,128)(2,1)} %copy-done) | copy-start | bytes 6291460
